TPU v7x, 32 devices: a whole 2x2x4 slice. The times are simulated.
32 devices in a mesh: dp: 16 (over z, y, x), mp: 2 (over core).
Axes of the slice: x: 2, y: 2, z: 4, core: 2. Of those that a mesh axis runs over, the one named last changes fastest.
Arguments:
- inputs: bfloat16 [2, 16, 256, 2048], P(None, 'dp'), may hold values from -6 to 6
- segment_ids: int32 [2, 16, 256], P(None, 'dp'), may hold values from 0 to 3, never falling along the last dimension, each value on 1 to 128 neighbouring positions
- cotangent: bfloat16 [2, 16, 256, 2048], P(None, 'dp'), may hold values from -6 to 6
- mixer_gain: bfloat16 [2048], P('dp'), may hold values from 0.5 to 1.5
- mlp_gain: bfloat16 [2048], P('dp'), may hold values from 0.5 to 1.5
- w_branch: bfloat16 [2048, 2560], P('dp', 'mp'), may hold values from -0.125 to 0.125
- w_recur: bfloat16 [2048, 2560], P('dp', 'mp'), may hold values from -0.125 to 0.125
- conv_w: bfloat16 [4, 2560], P(None, ('mp', 'dp')), may hold values from -3 to 3
- w_decay: bfloat16 [16, 25600], P('mp', 'dp'), may hold values from -0.5 to 0.5
- w_input: bfloat16 [16, 25600], P('mp', 'dp'), may hold values from -0.5 to 0.5
- gate_bias: bfloat16 [2, 2560], P(None, ('mp', 'dp')), may hold values from -4 to 4
- decay_param: bfloat16 [2560], P(('mp', 'dp')), may hold values from 1.5 to 6
- w_out: bfloat16 [2560, 2048], P('mp', 'dp'), may hold values from -0.3125 to 0.3125
- w_gate: bfloat16 [2048, 6144], P('dp', 'mp'), may hold values from -0.125 to 0.125
- w_up: bfloat16 [2048, 6144], P('dp', 'mp'), may hold values from -0.125 to 0.125
- w_down: bfloat16 [6144, 2048], P('mp', 'dp'), may hold values from -0.15625 to 0.15625
Outputs:
- result: float32 [2, 16, 256, 2048], P(None, 'dp')
- input_grad: float32 [2, 16, 256, 2048], P(None, 'dp')
- grad_mixer_gain: float32 [2048], P('dp')
- grad_mlp_gain: float32 [2048], P('dp')
- grad_w_branch: float32 [2048, 2560], P('dp', 'mp')
- grad_w_recur: float32 [2048, 2560], P('dp', 'mp')
- grad_conv_w: float32 [4, 2560], P(None, ('mp', 'dp'))
- grad_w_decay: float32 [16, 25600], P('mp', 'dp')
- grad_w_input: float32 [16, 25600], P('mp', 'dp')
- grad_gate_bias: float32 [2, 2560], P(None, ('mp', 'dp'))
- grad_decay_param: float32 [2560], P(('mp', 'dp'))
- grad_w_out: float32 [2560, 2048], P('mp', 'dp')
- grad_w_gate: float32 [2048, 6144], P('dp', 'mp')
- grad_w_up: float32 [2048, 6144], P('dp', 'mp')
- grad_w_down: float32 [6144, 2048], P('mp', 'dp')
Inputs may be any that keep to these rules, and one draw needn't show every extreme that they name: `segment_ids`: along each row the ids never fall; a segment spans 1 to 128 positions.
All inputs are finite; a program needn't handle non-finite values.
Results may differ from a plain program's by a relative error of at most 0.01.
Values may be sent and summed in bfloat16 or wider, within the bound.
No kernel may reach another device: no remote copies, remote signals or barrier semaphores. Data moves between devices by JAX's collectives and lax.ppermute only.
A program may use at most 320 MiB of HBM per device.

v0:
```python
import jax
import jax.numpy as jnp
from jax import lax
from jax.sharding import PartitionSpec as P

BW = 160


def rms_scale(values, norm_gain):
    return values * lax.rsqrt(jnp.mean(values * values, axis=-1, keepdims=True) + 1e-06) * norm_gain


def same_masks(seg_row, tap_count):
    same_seg = []
    for offset in range(1, tap_count):
        matched = (seg_row[offset:] == seg_row[:-offset]).astype(jnp.float32)
        leading = jnp.zeros((offset,), jnp.float32)
        same_seg.append(jnp.concatenate([leading, matched], axis=0)[:, None])
    return same_seg


def conv_mix(signal, conv_f, same_seg):
    summed = signal * conv_f[0]
    for offset in range(1, conv_f.shape[0]):
        shifted = jnp.pad(signal, [(offset, 0), (0, 0)])[:-offset, :]
        summed = summed + conv_f[offset] * shifted * same_seg[offset - 1]
    return summed


def combine(earlier, latest):
    return (earlier[0] * latest[0], latest[0] * earlier[1] + latest[1])


def recur(branch, decay_pre, input_pre, values, biases, raw_decay, resets):
    r_gate = jax.nn.sigmoid(decay_pre + biases[0])
    i_gate = jax.nn.sigmoid(input_pre + biases[1])
    log_decay = -8.0 * r_gate * jax.nn.softplus(-raw_decay)
    carry_on = 1.0 - resets
    norm_mult = resets + carry_on * jnp.sqrt(-jnp.expm1(2.0 * log_decay))
    decay_now = jnp.exp(log_decay) * carry_on
    drive_in = norm_mult * i_gate * values
    _, hidden = lax.associative_scan(combine, (decay_now, drive_in), axis=0)
    return hidden * jax.nn.gelu(branch)


def tokens_dot(left_in, right_in):
    return lax.dot_general(
        left_in, right_in, (((0,), (0,)), ((), ())), preferred_element_type=jnp.float32
    )


def back_dot(left_in, right_in):
    return lax.dot_general(
        left_in, right_in, (((1,), (1,)), ((), ())), preferred_element_type=jnp.float32
    )


def head_mix(heads_view, weights):
    blocks = weights.reshape(weights.shape[0], BW, BW)
    return jnp.einsum("rhc,hcd->rhd", heads_view, blocks, preferred_element_type=jnp.float32)


def forward_pass(weights, x_rows, seg_row):
    (
        mixer_gain,
        mlp_gain,
        w_branch,
        w_recur,
        conv_w,
        w_decay,
        w_input,
        gate_bias,
        decay_param,
        w_out,
        w_gate,
        w_up,
        w_down,
    ) = weights
    x_float = x_rows.astype(jnp.float32)
    same_seg = same_masks(seg_row, conv_w.shape[0])
    resets = 1.0 - same_seg[0]
    normed_mix = rms_scale(x_float, mixer_gain.astype(jnp.float32)).astype(jnp.bfloat16)
    branch = jnp.dot(normed_mix, w_branch, preferred_element_type=jnp.float32)
    recur_in = jnp.dot(normed_mix, w_recur, preferred_element_type=jnp.float32)
    values_low = conv_mix(recur_in, conv_w.astype(jnp.float32), same_seg).astype(jnp.bfloat16)
    heads_view = values_low.reshape(values_low.shape[0], w_decay.shape[0], BW)
    decay_pre = head_mix(heads_view, w_decay).reshape(values_low.shape)
    input_pre = head_mix(heads_view, w_input).reshape(values_low.shape)
    mixed = recur(
        branch,
        decay_pre,
        input_pre,
        values_low.astype(jnp.float32),
        gate_bias.astype(jnp.float32),
        decay_param.astype(jnp.float32),
        resets,
    )
    mixed_low = mixed.astype(jnp.bfloat16)
    mixer_out = lax.psum(jnp.dot(mixed_low, w_out, preferred_element_type=jnp.float32), "mp")
    after_mix = x_float + mixer_out
    normed_mlp = rms_scale(after_mix, mlp_gain.astype(jnp.float32)).astype(jnp.bfloat16)
    gate_pre = jnp.dot(normed_mlp, w_gate, preferred_element_type=jnp.float32)
    up_pre = jnp.dot(normed_mlp, w_up, preferred_element_type=jnp.float32)
    hidden = (jax.nn.gelu(gate_pre) * up_pre).astype(jnp.bfloat16)
    mlp_out = lax.psum(
        jnp.dot(hidden, w_down, preferred_element_type=jnp.float32).astype(jnp.bfloat16), "mp"
    ).astype(jnp.float32)
    outcome = after_mix + mlp_out
    kept_acts = (
        x_float,
        same_seg,
        resets,
        normed_mix,
        branch,
        recur_in,
        values_low,
        decay_pre,
        input_pre,
        mixed_low,
        after_mix,
        normed_mlp,
        gate_pre,
        up_pre,
        hidden,
    )
    return (kept_acts, outcome)


def backward_pass(weights, kept_acts, cot_rows):
    (
        mixer_gain,
        mlp_gain,
        w_branch,
        w_recur,
        conv_w,
        w_decay,
        w_input,
        gate_bias,
        decay_param,
        w_out,
        w_gate,
        w_up,
        w_down,
    ) = weights
    (
        x_float,
        same_seg,
        resets,
        normed_mix,
        branch,
        recur_in,
        values_low,
        decay_pre,
        input_pre,
        mixed_low,
        after_mix,
        normed_mlp,
        gate_pre,
        up_pre,
        hidden,
    ) = kept_acts
    cot_float = cot_rows.astype(jnp.float32)
    grad_down = tokens_dot(hidden, cot_rows)
    grad_hidden = back_dot(cot_rows, w_down)
    _, pull_back = jax.vjp(lambda gate_in, up_in: jax.nn.gelu(gate_in) * up_in, gate_pre, up_pre)
    grad_gate_pre, grad_up_pre = pull_back(grad_hidden)
    gate_low = grad_gate_pre.astype(jnp.bfloat16)
    up_low = grad_up_pre.astype(jnp.bfloat16)
    grad_gate = tokens_dot(normed_mlp, gate_low)
    grad_up = tokens_dot(normed_mlp, up_low)
    grad_normed = lax.psum(back_dot(gate_low, w_gate) + back_dot(up_low, w_up), "mp")
    _, pull_back = jax.vjp(rms_scale, after_mix, mlp_gain.astype(jnp.float32))
    grad_after, grad_mlp_gain = pull_back(grad_normed)
    grad_after = cot_float + grad_after
    after_low = grad_after.astype(jnp.bfloat16)
    grad_out = tokens_dot(mixed_low, after_low)
    grad_mixed = back_dot(after_low, w_out)

    def recur_local(branch_in, decay_in, input_in, values_in, bias_in, raw_in):
        return recur(branch_in, decay_in, input_in, values_in, bias_in, raw_in, resets)

    _, pull_back = jax.vjp(
        recur_local,
        branch,
        decay_pre,
        input_pre,
        values_low.astype(jnp.float32),
        gate_bias.astype(jnp.float32),
        decay_param.astype(jnp.float32),
    )
    grad_branch, grad_decay_pre, grad_input_pre, direct, grad_bias, grad_raw = pull_back(grad_mixed)
    head_count = w_decay.shape[0]
    row_count = values_low.shape[0]
    decay_low = grad_decay_pre.astype(jnp.bfloat16).reshape(row_count, head_count, BW)
    input_low = grad_input_pre.astype(jnp.bfloat16).reshape(row_count, head_count, BW)
    heads_view = values_low.reshape(row_count, head_count, BW)
    grad_wdecay = jnp.einsum(
        "rhc,rhd->hcd", heads_view, decay_low, preferred_element_type=jnp.float32
    ).reshape(w_decay.shape)
    grad_winput = jnp.einsum(
        "rhc,rhd->hcd", heads_view, input_low, preferred_element_type=jnp.float32
    ).reshape(w_input.shape)
    decay_back = jnp.einsum(
        "rhd,hcd->rhc",
        decay_low,
        w_decay.reshape(head_count, BW, BW),
        preferred_element_type=jnp.float32,
    )
    input_back = jnp.einsum(
        "rhd,hcd->rhc",
        input_low,
        w_input.reshape(head_count, BW, BW),
        preferred_element_type=jnp.float32,
    )
    grad_values = direct + (decay_back + input_back).reshape(direct.shape)
    _, pull_back = jax.vjp(
        lambda signal, conv_f: conv_mix(signal, conv_f, same_seg),
        recur_in,
        conv_w.astype(jnp.float32),
    )
    grad_recur_in, grad_conv = pull_back(grad_values)
    recur_low = grad_recur_in.astype(jnp.bfloat16)
    branch_low = grad_branch.astype(jnp.bfloat16)
    grad_wbranch = tokens_dot(normed_mix, branch_low)
    grad_wrecur = tokens_dot(normed_mix, recur_low)
    grad_normed_mix = lax.psum(back_dot(branch_low, w_branch) + back_dot(recur_low, w_recur), "mp")
    _, pull_back = jax.vjp(rms_scale, x_float, mixer_gain.astype(jnp.float32))
    grad_x, grad_mix_gain = pull_back(grad_normed_mix)
    x_grad = grad_after + grad_x
    return (
        x_grad,
        (
            grad_mix_gain,
            grad_mlp_gain,
            grad_wbranch,
            grad_wrecur,
            grad_conv,
            grad_wdecay,
            grad_winput,
            grad_bias,
            grad_raw,
            grad_out,
            grad_gate,
            grad_up,
            grad_down,
        ),
    )


def body(
    inputs,
    segment_ids,
    cotangent,
    mixer_gain,
    mlp_gain,
    w_branch,
    w_recur,
    conv_w,
    w_decay,
    w_input,
    gate_bias,
    decay_param,
    w_out,
    w_gate,
    w_up,
    w_down,
):
    shards = (
        mixer_gain,
        mlp_gain,
        w_branch,
        w_recur,
        conv_w,
        w_decay,
        w_input,
        gate_bias,
        decay_param,
        w_out,
        w_gate,
        w_up,
        w_down,
    )
    grad_sums = tuple((jnp.zeros(piece.shape, jnp.float32) for piece in shards))
    results = []
    input_grads = []
    for micro_idx in range(inputs.shape[0]):
        weights = (
            lax.all_gather(mixer_gain, "dp", axis=0, tiled=True),
            lax.all_gather(mlp_gain, "dp", axis=0, tiled=True),
            lax.all_gather(w_branch, "dp", axis=0, tiled=True),
            lax.all_gather(w_recur, "dp", axis=0, tiled=True),
            lax.all_gather(conv_w, "dp", axis=1, tiled=True),
            lax.all_gather(w_decay, "dp", axis=1, tiled=True),
            lax.all_gather(w_input, "dp", axis=1, tiled=True),
            lax.all_gather(gate_bias, "dp", axis=1, tiled=True),
            lax.all_gather(decay_param, "dp", axis=0, tiled=True),
            lax.all_gather(w_out, "dp", axis=1, tiled=True),
            lax.all_gather(w_gate, "dp", axis=0, tiled=True),
            lax.all_gather(w_up, "dp", axis=0, tiled=True),
            lax.all_gather(w_down, "dp", axis=1, tiled=True),
        )
        kept_acts, outcome = forward_pass(weights, inputs[micro_idx, 0], segment_ids[micro_idx, 0])
        weights = (
            lax.all_gather(mixer_gain, "dp", axis=0, tiled=True),
            lax.all_gather(mlp_gain, "dp", axis=0, tiled=True),
            lax.all_gather(w_branch, "dp", axis=0, tiled=True),
            lax.all_gather(w_recur, "dp", axis=0, tiled=True),
            lax.all_gather(conv_w, "dp", axis=1, tiled=True),
            lax.all_gather(w_decay, "dp", axis=1, tiled=True),
            lax.all_gather(w_input, "dp", axis=1, tiled=True),
            lax.all_gather(gate_bias, "dp", axis=1, tiled=True),
            lax.all_gather(decay_param, "dp", axis=0, tiled=True),
            lax.all_gather(w_out, "dp", axis=1, tiled=True),
            lax.all_gather(w_gate, "dp", axis=0, tiled=True),
            lax.all_gather(w_up, "dp", axis=0, tiled=True),
            lax.all_gather(w_down, "dp", axis=1, tiled=True),
        )
        x_grad, grads = backward_pass(weights, kept_acts, cotangent[micro_idx, 0])
        results.append(outcome)
        input_grads.append(x_grad)
        pieces = (
            lax.psum_scatter(grads[0], "dp", scatter_dimension=0, tiled=True),
            lax.psum_scatter(grads[1], "dp", scatter_dimension=0, tiled=True),
            lax.psum_scatter(grads[2], "dp", scatter_dimension=0, tiled=True),
            lax.psum_scatter(grads[3], "dp", scatter_dimension=0, tiled=True),
            lax.psum_scatter(grads[4], "dp", scatter_dimension=1, tiled=True),
            lax.psum_scatter(grads[5], "dp", scatter_dimension=1, tiled=True),
            lax.psum_scatter(grads[6], "dp", scatter_dimension=1, tiled=True),
            lax.psum_scatter(grads[7], "dp", scatter_dimension=1, tiled=True),
            lax.psum_scatter(grads[8], "dp", scatter_dimension=0, tiled=True),
            lax.psum_scatter(grads[9], "dp", scatter_dimension=1, tiled=True),
            lax.psum_scatter(grads[10], "dp", scatter_dimension=0, tiled=True),
            lax.psum_scatter(grads[11], "dp", scatter_dimension=0, tiled=True),
            lax.psum_scatter(grads[12], "dp", scatter_dimension=1, tiled=True),
        )
        grad_sums = tuple((left_in + right_in for left_in, right_in in zip(grad_sums, pieces)))
    result = jnp.stack(results)[:, None]
    input_grad = jnp.stack(input_grads)[:, None]
    return (
        result,
        input_grad,
        grad_sums[0],
        grad_sums[1],
        grad_sums[2],
        grad_sums[3],
        grad_sums[4],
        grad_sums[5],
        grad_sums[6],
        grad_sums[7],
        grad_sums[8],
        grad_sums[9],
        grad_sums[10],
        grad_sums[11],
        grad_sums[12],
    )


def solution(mesh):
    in_specs = (
        P(None, "dp", None, None),
        P(None, "dp", None),
        P(None, "dp", None, None),
        P("dp"),
        P("dp"),
        P("dp", "mp"),
        P("dp", "mp"),
        P(None, ("mp", "dp")),
        P("mp", "dp"),
        P("mp", "dp"),
        P(None, ("mp", "dp")),
        P(("mp", "dp")),
        P("mp", "dp"),
        P("dp", "mp"),
        P("dp", "mp"),
        P("mp", "dp"),
    )
    out_specs = (
        P(None, "dp", None, None),
        P(None, "dp", None, None),
        P("dp"),
        P("dp"),
        P("dp", "mp"),
        P("dp", "mp"),
        P(None, ("mp", "dp")),
        P("mp", "dp"),
        P("mp", "dp"),
        P(None, ("mp", "dp")),
        P(("mp", "dp")),
        P("mp", "dp"),
        P("dp", "mp"),
        P("dp", "mp"),
        P("mp", "dp"),
    )
    return jax.shard_map(body, mesh=mesh, in_specs=in_specs, out_specs=out_specs, check_vma=False)
```

profile of v0, /device:TPU:1, one launch (start us, length us, event | category | flops | bytes accessed | tf_op | source)
XLA Modules:
  0.0 3962.0 jit_solution(9954375427308035596)
XLA Ops:
  15.1 36.2 all-reduce.210
  51.9 29.1 all-gather
  83.1 30.5 all-gather.1
  113.8 33.4 all-gather.2
  149.3 29.8 all-gather.3
  179.3 33.6 all-gather.4
  502.3 29.0 all-gather.5
  531.3 39.2 all-reduce.228.cloned.1.call-done
  575.8 150.2 %all-gather.19.cloned.1.call-done = bf16[2048,3072]{1,0:T(8,128)(2,1)} async-done(((bf16[128,3072]{1,0:T(8,128)(2,1)}), bf16[2048,3072]{1,0:T(8,128)(2,1)}) %all-gather.19.cloned.1.call-update) | async-done | bytes 12582928 | tf_op jit(solution)/shard_map/all_gather | solution.py:298
  735.6 143.6 %all-gather.21.cloned.1.call-done = bf16[2048,3072]{1,0:T(8,128)(2,1)} async-done(((bf16[128,3072]{1,0:T(8,128)(2,1)}), bf16[2048,3072]{1,0:T(8,128)(2,1)}) %all-gather.21.cloned.1.call-update) | async-done | bytes 12582928 | tf_op jit(solution)/shard_map/all_gather | solution.py:299
  899.4 177.1 %all-gather.23.cloned.1.call-done = bf16[3072,2048]{1,0:T(8,128)(2,1)} async-done(((bf16[3072,128]{1,0:T(8,128)(2,1)}), bf16[3072,2048]{1,0:T(8,128)(2,1)}) %all-gather.23.cloned.1.call-update) | async-done | bytes 12582928 | tf_op jit(solution)/shard_map/all_gather | solution.py:300
  1166.4 19.2 all-reduce.230.cloned.1.call-done
  1547.8 17.0 convolution_add_fusion
  1578.5 20.9 convolution_add_fusion.2
  1608.5 245.6 %reduce-scatter.33.cloned.1.call-done = f32[1600,8]{1,0:T(8,128)} async-done(((f32[25600,8]{1,0:T(8,128)}), f32[1600,8]{1,0:T(8,128)}) %reduce-scatter.33.cloned.1.call-update) | async-done | bytes 51216
  1856.1 277.9 %reduce-scatter.35.cloned.1.call-done = f32[1600,8]{1,0:T(8,128)} async-done(((f32[25600,8]{1,0:T(8,128)}), f32[1600,8]{1,0:T(8,128)}) %reduce-scatter.35.cloned.1.call-update) | async-done | bytes 51216
  2136.0 34.4 all-reduce.224.cloned.1.call-done
  2173.9 73.0 %all-reduce.214 = (f32[2048]{0:T(1024)S(1)}, f32[2048]{0:T(1024)S(1)}, f32[1280]{0:T(1024)S(1)}) all-reduce(f32[2048]{0:T(1024)S(1)} %add.1207, f32[2048]{0:T(1024)S(1)} %add.1208, f32[1280]{0:T(1024)S(1)} %negate_add_fusion), channel_id=15, replica_groups=mesh['dp'=16,'mp'=2] {'dp'}, use_global_device_ids=true, to_apply=%region_17.19.clone | all-reduce | flops 5376 | bytes 43008
  2255.7 140.2 %reduce-scatter.19.cloned.1.call-done = f32[128,1280]{1,0:T(8,128)} async-done(((f32[2048,1280]{1,0:T(8,128)}), f32[128,1280]{1,0:T(8,128)}) %reduce-scatter.19.cloned.1.call-update) | async-done | bytes 655376 | tf_op jit(solution)/shard_map/reduce_scatter | solution.py:324
  2395.9 227.2 %reduce-scatter.21.cloned.1.call-done = f32[128,1280]{1,0:T(8,128)} async-done(((f32[2048,1280]{1,0:T(8,128)}), f32[128,1280]{1,0:T(8,128)}) %reduce-scatter.21.cloned.1.call-update) | async-done | bytes 655376 | tf_op jit(solution)/shard_map/reduce_scatter | solution.py:325
  2623.1 226.1 %reduce-scatter.23.cloned.1.call-done = f32[1280,128]{1,0:T(8,128)} async-done(((f32[1280,2048]{1,0:T(8,128)}), f32[1280,128]{1,0:T(8,128)}) %reduce-scatter.23.cloned.1.call-update) | async-done | bytes 655376 | tf_op jit(solution)/shard_map/reduce_scatter | solution.py:331
  2849.2 371.6 %reduce-scatter.25.cloned.1.call-done = f32[128,3072]{1,0:T(8,128)} async-done(((f32[2048,3072]{1,0:T(8,128)}), f32[128,3072]{1,0:T(8,128)}) %reduce-scatter.25.cloned.1.call-update) | async-done | bytes 1572880 | tf_op jit(solution)/shard_map/reduce_scatter | solution.py:332
  3220.8 367.0 %reduce-scatter.27.cloned.1.call-done = f32[128,3072]{1,0:T(8,128)} async-done(((f32[2048,3072]{1,0:T(8,128)}), f32[128,3072]{1,0:T(8,128)}) %reduce-scatter.27.cloned.1.call-update) | async-done | bytes 1572880 | tf_op jit(solution)/shard_map/reduce_scatter | solution.py:333
  3587.8 367.2 %reduce-scatter.29.cloned.1.call-done = f32[3072,128]{1,0:T(8,128)} async-done(((f32[3072,2048]{1,0:T(8,128)}), f32[3072,128]{1,0:T(8,128)}) %reduce-scatter.29.cloned.1.call-update) | async-done | bytes 1572880 | tf_op jit(solution)/shard_map/reduce_scatter | solution.py:334
  (1240 shorter events, 822.1 us)
Async XLA Ops:
  7.2 208.6 %all-gather.13.cloned.1.call-start = ((), (), s32[]{:S(2)}) async-start(), calls=%async_computation.10 | async-start | bytes 5570560 | tf_op jit(solution)/shard_map/all_gather | solution.py:291
  7.9 472.2 %all-gather.15.cloned.1.call-start = ((), (), s32[]{:S(2)}) async-start(), calls=%async_computation.11 | async-start | bytes 5570560 | tf_op jit(solution)/shard_map/all_gather | solution.py:290
  8.7 478.1 %all-gather.17.cloned.1.call-start = ((), (), s32[]{:S(2)}) async-start(), calls=%async_computation.12 | async-start | bytes 5570560 | tf_op jit(solution)/shard_map/all_gather | solution.py:297
  9.4 561.1 %all-reduce.228.cloned.1.call-start = ((), (), s32[]{:S(2)}) async-start(), calls=%async_computation.28 | async-start | bytes 8388608 | tf_op jit(solution)/shard_map/psum | solution.py:99
  81.0 411.5 %copy-start.125 = (f32[16,1,128]{2,1,0:T(1,128)}, f32[16,1,128]{2,1,0:T(1,128)S(1)}, u32[]{:S(2)}) copy-start(f32[16,1,128]{2,1,0:T(1,128)S(1)} %convert_element_type.235) | copy-start | bytes 24580
  420.5 797.3 %copy-start.218 = (f32[2,1280]{1,0:T(2,128)}, f32[2,1280]{1,0:T(2,128)S(1)}, u32[]{:S(2)}) copy-start(f32[2,1280]{1,0:T(2,128)S(1)} %slice.1044) | copy-start | bytes 30724
  500.3 225.6 %all-gather.19.cloned.1.call-start = ((), (), s32[]{:S(2)}) async-start(), calls=%async_computation.13 | async-start | bytes 13369344 | tf_op jit(solution)/shard_map/all_gather | solution.py:298
  500.9 378.3 %all-gather.21.cloned.1.call-start = ((), (), s32[]{:S(2)}) async-start(), calls=%async_computation.14 | async-start | bytes 13369344 | tf_op jit(solution)/shard_map/all_gather | solution.py:299
  501.5 575.0 %all-gather.23.cloned.1.call-start = ((), (), s32[]{:S(2)}) async-start(), calls=%async_computation.15 | async-start | bytes 13369344 | tf_op jit(solution)/shard_map/all_gather | solution.py:300
  502.3 658.4 %all-reduce.226.cloned.1.call-start = ((), (), s32[]{:S(2)}) async-start(), calls=%async_computation.27 | async-start | bytes 8388608 | tf_op jit(solution)/shard_map/psum | solution.py:171
  575.8 303.5 %copy-start.15 = (bf16[256,2048]{1,0:T(8,128)(2,1)}, bf16[256,2048]{1,0:T(8,128)(2,1)S(1)}, u32[]{:S(2)}) copy-start(bf16[256,2048]{1,0:T(8,128)(2,1)S(1)} %get-tuple-element.352) | copy-start | bytes 3145732
  575.8 318.5 %copy-start.32 = (bf16[256,2048]{1,0:T(8,128)(2,1)}, bf16[256,2048]{1,0:T(8,128)(2,1)S(1)}, u32[]{:S(2)}) copy-start(bf16[256,2048]{1,0:T(8,128)(2,1)S(1)} %get-tuple-element.351) | copy-start | bytes 3145732
  1133.0 52.6 %all-reduce.230.cloned.1.call-start = ((), (), s32[]{:S(2)}) async-start(), calls=%async_computation.29 | async-start | bytes 4194304 | tf_op jit(solution)/shard_map/psum | solution.py:105
  1149.1 456.5 %reduce-scatter.37.cloned.1.call-start = ((), (), s32[]{:S(2)}) async-start(), calls=%async_computation.25 | async-start | bytes 696320
  1429.5 177.6 %reduce-scatter.31.cloned.1.call-start = ((), (), s32[]{:S(2)}) async-start(), calls=%async_computation.22 | async-start | bytes 696320
  1430.7 423.3 %reduce-scatter.33.cloned.1.call-start = ((), (), s32[]{:S(2)}) async-start(), calls=%async_computation.23 | async-start | bytes 13926400
  1439.5 694.5 %reduce-scatter.35.cloned.1.call-start = ((), (), s32[]{:S(2)}) async-start(), calls=%async_computation.24 | async-start | bytes 13926400
  1454.6 715.8 %all-reduce.224.cloned.1.call-start = ((), (), s32[]{:S(2)}) async-start(), calls=%async_computation.26 | async-start | bytes 8388608 | tf_op jit(solution)/shard_map/psum | solution.py:226
  1473.8 922.1 %reduce-scatter.19.cloned.1.call-start = ((), (), s32[]{:S(2)}) async-start(), calls=%async_computation.16 | async-start | bytes 11141120 | tf_op jit(solution)/shard_map/reduce_scatter | solution.py:324
  1484.8 1138.3 %reduce-scatter.21.cloned.1.call-start = ((), (), s32[]{:S(2)}) async-start(), calls=%async_computation.17 | async-start | bytes 11141120 | tf_op jit(solution)/shard_map/reduce_scatter | solution.py:325
  1494.3 1354.9 %reduce-scatter.23.cloned.1.call-start = ((), (), s32[]{:S(2)}) async-start(), calls=%async_computation.18 | async-start | bytes 11141120 | tf_op jit(solution)/shard_map/reduce_scatter | solution.py:331
  1503.4 1717.3 %reduce-scatter.25.cloned.1.call-start = ((), (), s32[]{:S(2)}) async-start(), calls=%async_computation.19 | async-start | bytes 26738688 | tf_op jit(solution)/shard_map/reduce_scatter | solution.py:332
  1534.0 2053.8 %reduce-scatter.27.cloned.1.call-start = ((), (), s32[]{:S(2)}) async-start(), calls=%async_computation.20 | async-start | bytes 26738688 | tf_op jit(solution)/shard_map/reduce_scatter | solution.py:333
  1564.9 2390.1 %reduce-scatter.29.cloned.1.call-start = ((), (), s32[]{:S(2)}) async-start(), calls=%async_computation.21 | async-start | bytes 26738688 | tf_op jit(solution)/shard_map/reduce_scatter | solution.py:334
  (345 other events, 4405.0 us)
Sparse Core Ops, SparseCore 0:
  10.8 86.8 all-gather.12
  100.4 88.2 all-gather.14
  191.4 103.1 all-gather.16
  500.5 70.0 all-reduce.227
  573.6 152.3 all-gather.18
  729.0 150.2 all-gather.20
  882.3 194.1 all-gather.22
  1133.2 27.4 all-reduce.225
  1163.1 22.4 all-reduce.229
  1429.6 66.7 reduce-scatter.36
  1498.6 73.0 reduce-scatter.30
  1573.9 280.0 reduce-scatter.32
  1856.5 277.4 reduce-scatter.34
  2136.5 33.7 all-reduce.223
  2173.1 222.7 reduce-scatter.18
  2398.6 224.3 reduce-scatter.20
  2625.8 223.3 reduce-scatter.22
  2855.4 365.3 reduce-scatter.24
  3227.1 360.6 reduce-scatter.26
  3593.9 360.9 reduce-scatter.28
where the time goes:
time: 3980 us; the launch traced here: 3960 us
  waiting for transfers between devices  2800 us (70%)
  local copies, waits for them, and re-layouts  372 us (9%)
  matrix products  302 us (8%)
  blocking collectives  295 us (7%)
  other arithmetic  169 us (4%)
    unnamed x24, waiting for transfers between devices  528 us
    reduce_scatter x1, waiting for transfers between devices, body(): lax.psum_scatter(grads[10], 'dp', scatter_dimension=0, tiled=True)  372 us
    reduce_scatter x1, waiting for transfers between devices, body(): lax.psum_scatter(grads[12], 'dp', scatter_dimension=1, tiled=True)  367 us
    reduce_scatter x1, waiting for transfers between devices, body(): lax.psum_scatter(grads[11], 'dp', scatter_dimension=0, tiled=True)  367 us
    reduce_scatter x1, waiting for transfers between devices, body(): lax.psum_scatter(grads[3], 'dp', scatter_dimension=0, tiled=True)  227 us
    reduce_scatter x1, waiting for transfers between devices, body(): lax.psum_scatter(grads[9], 'dp', scatter_dimension=1, tiled=True)  226 us
    all_gather x1, waiting for transfers between devices, body(): lax.all_gather(w_down, 'dp', axis=1, tiled=True)  177 us
    slice x120, local copies, waits for them, and re-layouts, recur(): _, hidden = lax.associative_scan(combine, (decay_now, drive_in), axis=0)  164 us
  transfers between devices with their start and end apart: 20, of which 15 were waited for; matrix products, arithmetic and copies ran while one was open for 13% of the time, Pallas kernels for 0%

commit v1 on v0

v1 whole, which is shorter than its diff:
```python
import functools

import jax
import jax.numpy as jnp
from jax import lax
from jax.experimental import pallas as pl
from jax.experimental.pallas import tpu as pltpu
from jax.sharding import PartitionSpec as P

BW = 160
G = 4
BF = jnp.bfloat16
F32 = jnp.float32
ROWS = 8
PAD = 8
C0 = 0.7978845608028654
C1 = 0.044715


def sigmoid(v):
    return 0.5 * jnp.tanh(0.5 * v) + 0.5


def gates(dec, inp, sp8, keep):
    r = sigmoid(dec)
    i = sigmoid(inp)
    log_decay = r * sp8
    a = jnp.exp(log_decay)
    gap = -jnp.tanh(log_decay) * (1.0 + a * a)
    return r, i, a, gap


def forward_kernel(cp, row, unroll, mix_hbm, mask_ref, par_ref, wg_ref, mixed_ref, values_ref, pre_ref, h_ref, vals, mixf, mix, sems):
    lanes = cp // 128
    order = list(range(lanes, 2 * lanes)) + list(range(lanes))
    copies = {
        j: [pltpu.make_async_copy(mix_hbm.at[pl.ds(r * row, row), pl.ds(128 * j, 128)], mix.at[j, pl.ds(r * (row + PAD), row)], sems.at[j, r]) for r in range(ROWS)] for j in order
    }
    for j in order:
        for c in copies[j]:
            c.start()

    def at(ref, t, off=0):
        return [ref[off + j, pl.ds(t, ROWS, stride=row + PAD), :] for j in range(lanes)]

    def put(ref, t, tiles):
        for j in range(lanes):
            ref[j, pl.ds(t, ROWS, stride=row + PAD), :] = tiles[j]

    def flat(ref, rows):
        return jnp.concatenate([ref[j, rows, :] for j in range(lanes)], axis=1)

    def mask(k, t):
        return mask_ref[k, pl.ds(pl.multiple_of(t * ROWS, ROWS), ROWS), :]

    par = [[par_ref[p, :, pl.ds(128 * j, 128)] for j in range(lanes)] for p in range(7)]
    zero = [jnp.zeros((ROWS, 128), F32)] * lanes
    for j in order[:lanes]:
        for c in copies[j]:
            c.wait()

    def conv_step(blk, carry):
        prev = [list(carry[0:lanes]), list(carry[lanes:2 * lanes]), list(carry[2 * lanes:])]
        for u in range(unroll):
            t = blk * unroll + u
            now = at(mix, t, lanes)
            same = [mask(k, t) for k in range(3)]
            out = []
            for j in range(lanes):
                s = now[j] * par[0][j]
                for k in range(3):
                    s = s + par[k + 1][j] * prev[k][j] * same[k]
                out.append(s)
            put(vals, t, out)
            prev = [now, prev[0], prev[1]]
        return tuple(prev[0] + prev[1] + prev[2])

    lax.fori_loop(0, row // unroll, conv_step, tuple(zero * 3))

    for r in range(ROWS):
        rows = pl.ds(r * row, row)
        prow = pl.ds(r * (row + PAD), row)
        low = flat(vals, prow).astype(BF)
        values_ref[rows, :] = low
        pre = jnp.dot(low, wg_ref[...], preferred_element_type=F32)
        for j in range(2 * lanes):
            pre_ref[j, prow, :] = pre[:, 128 * j : 128 * (j + 1)]
    for j in order[lanes:]:
        for c in copies[j]:
            c.wait()

    def step(blk, carry):
        h = list(carry)
        for u in range(unroll):
            t = blk * unroll + u
            dec, inp, val, br = at(pre_ref, t), at(pre_ref, t, lanes), at(vals, t), at(mix, t)
            keep = mask(0, t)
            out = []
            for j in range(lanes):
                r, i, a, gap = gates(dec[j] + par[4][j], inp[j] + par[5][j], par[6][j], keep)
                m = (1.0 - keep) + keep * jnp.sqrt(jnp.maximum(gap, 0.0))
                v = val[j].astype(BF).astype(F32)
                h[j] = a * keep * h[j] + m * i * v
                b = br[j]
                tt = jnp.tanh(C0 * (b + C1 * b * b * b))
                out.append(h[j] * (0.5 * b * (1.0 + tt)))
            put(h_ref, t, h)
            put(mixf, t, out)
        return tuple(h)

    lax.fori_loop(0, row // unroll, step, tuple(zero))
    for r in range(ROWS):
        rows = pl.ds(r * row, row)
        mixed_ref[rows, :] = flat(mixf, pl.ds(r * (row + PAD), row)).astype(BF)


def forward_call(mix, mask, par, wg, unroll=8):
    tokens, cp = mix.shape[0], mix.shape[1] // 2
    row = tokens // ROWS
    lanes = cp // 128
    vm = pl.BlockSpec(memory_space=pltpu.VMEM)
    return pl.pallas_call(
        functools.partial(forward_kernel, cp, row, unroll),
        in_specs=[pl.BlockSpec(memory_space=pl.ANY), vm, vm, vm],
        out_specs=(vm, vm, vm, vm),
        out_shape=(
            jax.ShapeDtypeStruct((tokens, cp), BF),
            jax.ShapeDtypeStruct((tokens, cp), BF),
            jax.ShapeDtypeStruct((2 * lanes, tokens + ROWS * PAD, 128), F32),
            jax.ShapeDtypeStruct((lanes, tokens + ROWS * PAD, 128), F32),
        ),
        scratch_shapes=[
            pltpu.VMEM((lanes, tokens + ROWS * PAD, 128), F32),
            pltpu.VMEM((lanes, tokens + ROWS * PAD, 128), F32),
            pltpu.VMEM((2 * lanes, tokens + ROWS * PAD, 128), F32),
            pltpu.SemaphoreType.DMA((2 * lanes, ROWS)),
        ],
        compiler_params=pltpu.CompilerParams(vmem_limit_bytes=60 * 1024 * 1024),
        name="recur_forward",
    )(mix, mask, par, wg)


def backward_kernel(
    cp, row, unroll, mix_hbm, gm_hbm, mask_ref, par_ref, wg_ref, values_ref, pre_ref, h_ref,
    mixlow_ref, low_ref, acc_ref, vals, mix, gm, gdec, ginp, gval, sems,
):
    lanes = cp // 128
    pitch = row + PAD
    copies = []
    for j in range(lanes):
        for r in range(ROWS):
            src = pl.ds(r * row, row)
            dst = pl.ds(r * pitch, row)
            cols = pl.ds(128 * j, 128)
            rec = pl.ds(cp + 128 * j, 128)
            copies.append(pltpu.make_async_copy(mix_hbm.at[src, cols], mix.at[j, dst], sems.at[0, j, r]))
            copies.append(
                pltpu.make_async_copy(mix_hbm.at[src, rec], mix.at[lanes + j, dst], sems.at[1, j, r])
            )
            copies.append(pltpu.make_async_copy(gm_hbm.at[src, cols], gm.at[j, dst], sems.at[2, j, r]))
    for c in copies:
        c.start()

    def at(ref, t, off=0):
        return [ref[off + j, pl.ds(t, ROWS, stride=pitch), :] for j in range(lanes)]

    def put(ref, t, tiles):
        for j in range(lanes):
            ref[j, pl.ds(t, ROWS, stride=pitch), :] = tiles[j]

    def flat(ref, rows):
        return jnp.concatenate([ref[j, rows, :] for j in range(lanes)], axis=1)

    def mask(k, t):
        return mask_ref[k, pl.ds(pl.multiple_of(t * ROWS, ROWS), ROWS), :]

    par = [[par_ref[p, :, pl.ds(128 * j, 128)] for j in range(lanes)] for p in range(7)]
    zero = [jnp.zeros((ROWS, 128), F32)] * lanes
    for r in range(ROWS):
        low = values_ref[pl.ds(r * row, row), :].astype(F32)
        for j in range(lanes):
            vals[j, pl.ds(r * pitch, row), :] = low[:, 128 * j : 128 * (j + 1)]
    for c in copies:
        c.wait()

    def step(blk, carry):
        carry = [list(carry[lanes * p : lanes * (p + 1)]) for p in range(4)]
        ag, sum_dec, sum_inp, sum_raw = carry
        for u in range(unroll):
            t = row - 1 - (blk * unroll + u)
            dec, inp, val = at(pre_ref, t), at(pre_ref, t, lanes), at(vals, t)
            br, up, here, before = at(mix, t), at(gm, t), at(h_ref, t), at(h_ref, jnp.maximum(t - 1, 0))
            keep = mask(0, t)
            out_b, out_d, out_i, out_v = [], [], [], []
            for j in range(lanes):
                r, i, a, gap = gates(dec[j] + par[4][j], inp[j] + par[5][j], par[6][j], keep)
                gap = jnp.maximum(gap, 1e-30)
                inv = lax.rsqrt(gap)
                m = (1.0 - keep) + keep * (gap * inv)
                b = br[j]
                sq = b * b
                tt = jnp.tanh(C0 * (b + C1 * b * sq))
                half = 0.5 * (1.0 + tt)
                slope = half + 0.5 * b * (1.0 - tt * tt) * (C0 + 3.0 * C0 * C1 * sq)
                g = up[j] * (b * half) + ag[j]
                gi = g * i
                decay = a * keep
                g_log = g * before[j] * decay - gi * val[j] * keep * (a * a * inv)
                ag[j] = decay * g
                gr = g_log * r
                g_dec = gr * par[6][j] * (1.0 - r)
                g_dir = gi * m
                g_inp = g_dir * val[j] * (1.0 - i)
                sum_raw[j] = sum_raw[j] + gr
                sum_dec[j] = sum_dec[j] + g_dec
                sum_inp[j] = sum_inp[j] + g_inp
                out_b.append(up[j] * here[j] * slope)
                out_d.append(g_dec)
                out_i.append(g_inp)
                out_v.append(g_dir)
            put(gm, t, out_b)
            put(gdec, t, out_d)
            put(ginp, t, out_i)
            put(gval, t, out_v)
        return tuple(ag + sum_dec + sum_inp + sum_raw)

    sums = lax.fori_loop(0, row // unroll, step, tuple(zero * 4))
    for p in range(3):
        for j in range(lanes):
            acc_ref[4 + p, :, pl.ds(128 * j, 128)] = sums[lanes * (p + 1) + j]

    for r in range(ROWS):
        rows = pl.ds(r * row, row)
        prow = pl.ds(r * pitch, row)
        low = jnp.concatenate([flat(gdec, prow), flat(ginp, prow)], axis=1).astype(BF)
        low_ref[rows, :] = low
        back = lax.dot_general(low, wg_ref[...], (((1,), (1,)), ((), ())), preferred_element_type=F32)
        for j in range(lanes):
            gval[j, prow, :] = gval[j, prow, :] + back[:, 128 * j : 128 * (j + 1)]
        mixlow_ref[rows, pl.ds(0, cp)] = flat(gm, prow).astype(BF)

    def conv_step(blk, carry):
        carry = [list(carry[lanes * p : lanes * (p + 1)]) for p in range(10)]
        late, sums = carry[:6], carry[6:]
        for u in range(unroll):
            t = row - 1 - (blk * unroll + u)
            now, rec = at(gval, t), at(mix, t, lanes)
            same = [mask(k, t) for k in range(3)]
            taps = [now, late[0], late[1], late[3]]
            out = []
            for j in range(lanes):
                s = par[0][j] * now[j]
                for k in range(1, 4):
                    s = s + par[k][j] * taps[k][j]
                out.append(s)
                for k in range(4):
                    sums[k][j] = sums[k][j] + rec[j] * taps[k][j]
            put(gdec, t, out)
            scaled = [[now[j] * same[k] for j in range(lanes)] for k in range(3)]
            late = [scaled[0], late[2], scaled[1], late[4], late[5], scaled[2]]
        return tuple(sum(late + sums, []))

    sums = lax.fori_loop(0, row // unroll, conv_step, tuple(zero * 10))
    for k in range(4):
        for j in range(lanes):
            acc_ref[k, :, pl.ds(128 * j, 128)] = sums[lanes * (6 + k) + j]
    for r in range(ROWS):
        mixlow_ref[pl.ds(r * row, row), pl.ds(cp, cp)] = flat(gdec, pl.ds(r * pitch, row)).astype(BF)


def backward_call(mix, gm, mask, par, wg, values, pre, h, unroll=4):
    tokens, cp = gm.shape
    row = tokens // ROWS
    lanes = cp // 128
    vm = pl.BlockSpec(memory_space=pltpu.VMEM)
    hbm = pl.BlockSpec(memory_space=pl.ANY)
    slab = pltpu.VMEM((lanes, tokens + ROWS * PAD, 128), F32)
    return pl.pallas_call(
        functools.partial(backward_kernel, cp, row, unroll),
        in_specs=[hbm, hbm, vm, vm, vm, vm, vm, vm],
        out_specs=(vm, vm, vm),
        out_shape=(
            jax.ShapeDtypeStruct((tokens, 2 * cp), BF),
            jax.ShapeDtypeStruct((tokens, 2 * cp), BF),
            jax.ShapeDtypeStruct((7, ROWS, cp), F32),
        ),
        scratch_shapes=[
            slab,
            pltpu.VMEM((2 * lanes, tokens + ROWS * PAD, 128), F32),
            slab,
            slab,
            slab,
            slab,
            pltpu.SemaphoreType.DMA((3, lanes, ROWS)),
        ],
        compiler_params=pltpu.CompilerParams(vmem_limit_bytes=60 * 1024 * 1024),
        name="recur_backward",
    )(mix, gm, mask, par, wg, values, pre, h)


def rms_scale(values, norm_gain):
    return values * lax.rsqrt(jnp.mean(values * values, axis=-1, keepdims=True) + 1e-06) * norm_gain


def same_masks(seg_rows, tap_count):
    same_seg = []
    for offset in range(1, tap_count):
        matched = (seg_rows[..., offset:] == seg_rows[..., :-offset]).astype(F32)
        leading = jnp.zeros(seg_rows.shape[:-1] + (offset,), F32)
        same_seg.append(jnp.concatenate([leading, matched], axis=-1))
    return jnp.stack(same_seg)


def dot(a, b, ca, cb, out=F32):
    return lax.dot_general(a, b, (((ca,), (cb,)), ((), ())), preferred_element_type=out)


def unxor(pieces, g):
    low, high = (g & 1) == 1, (g >> 1) == 1
    p0, p1, p2, p3 = pieces
    q0, q1 = jnp.where(low, p1, p0), jnp.where(low, p0, p1)
    q2, q3 = jnp.where(low, p3, p2), jnp.where(low, p2, p3)
    return [
        jnp.where(high, q2, q0),
        jnp.where(high, q3, q1),
        jnp.where(high, q0, q2),
        jnp.where(high, q1, q3),
    ]


def make_body(n, m):
    far = n // G
    z_groups = [[c + G * k for k in range(far)] for c in range(G)]
    flips = [[(i, i ^ d) for i in range(n)] for d in range(G)]
    cores = [(0, 1), (1, 0)]

    def flip(a, d):
        return lax.ppermute(a, "dp", flips[d])

    far_flips = [[(i, i ^ (G * k)) for i in range(n)] for k in range(far)]

    def far_flip(a, k):
        return lax.ppermute(a, "dp", far_flips[k])

    def pick(a, i):
        return lax.dynamic_index_in_dim(a, i, 0, keepdims=False)

    def gather_far(a, z):
        got = jnp.stack([a] + [far_flip(a, k) for k in range(1, far)])
        return jnp.stack([pick(got, z ^ j) for j in range(far)])

    def sum_far(a, z, low=lambda v: v):
        total = pick(a, z)
        for k in range(1, far):
            total = total + far_flip(low(pick(a, z ^ k)), k).astype(F32)
        return total

    def swap_core(a):
        return lax.ppermute(a, "mp", cores)

    def gather8(own):
        mine = jnp.concatenate([own] + [flip(own, d) for d in range(1, G)], axis=0)
        return jnp.concatenate([mine, swap_core(mine)], axis=0)

    def scatter8(make, own_rows):
        other = make(1).astype(BF)
        arrived = swap_core(other)
        mine = make(0) + arrived.astype(F32)
        pieces = [mine[d * own_rows : (d + 1) * own_rows] for d in range(G)]
        total = pieces[0]
        for d in range(1, G):
            total = total + flip(pieces[d].astype(BF), d).astype(F32)
        return total

    def body(
        inputs,
        segment_ids,
        cotangent,
        mixer_gain,
        mlp_gain,
        w_branch,
        w_recur,
        conv_w,
        w_decay,
        w_input,
        gate_bias,
        decay_param,
        w_out,
        w_gate,
        w_up,
        w_down,
    ):
        dp = lax.axis_index("dp")
        mp = lax.axis_index("mp")
        g = dp % G
        z = dp // G
        micro, _, row, width = inputs.shape
        depth = width // n
        ch = w_branch.shape[1] // G
        ff = w_gate.shape[1] // G
        heads = w_decay.shape[0] // G
        taps = conv_w.shape[0]

        def own_part(a):
            return lax.dynamic_index_in_dim(a, mp, 0, keepdims=False)[0]

        x_own = own_part(inputs)
        c_own = own_part(cotangent)
        x_all = gather8(x_own)
        seg_all = gather8(own_part(segment_ids)[:, None])[:, 0].reshape(2 * G, row)

        small = jnp.concatenate(
            [a.reshape(-1) for a in (mixer_gain, mlp_gain, conv_w, gate_bias, decay_param)]
        )
        small = jnp.stack(unxor([small] + [flip(small, d) for d in range(1, G)], g))
        small = gather_far(small, z).reshape(n, -1).astype(F32)
        part = conv_w.shape[1]
        mixer_gain_f = small[:, :depth].reshape(width)
        mlp_gain_f = small[:, depth : 2 * depth].reshape(width)
        chan = small[:, 2 * depth :].reshape(n, taps + 3, part)
        chan = jnp.transpose(chan, (1, 0, 2)).reshape(taps + 3, n * part)
        chan = lax.dynamic_slice_in_dim(chan, g * ch, ch, 1)
        wide = -(-ch // 128) * 128
        sp8 = -8.0 * jax.nn.softplus(-chan[taps + 2 :])
        par = jnp.concatenate([chan[: taps + 2], sp8], axis=0)
        par = jnp.pad(par, ((0, 0), (0, wide - ch)), constant_values=((0, 0), (0, -1.0)))
        par = par * jnp.where((jnp.arange(wide) >= ch) & (jnp.arange(taps + 3) < taps + 2)[:, None], 0.0, 1.0)
        par_f = jnp.broadcast_to(par[:, None], (taps + 3, ROWS, wide))
        mask = jnp.transpose(same_masks(seg_all, taps), (0, 2, 1)).reshape(taps - 1, ROWS * row, 1)
        mask = jnp.broadcast_to(mask, (taps - 1, ROWS * row, 128))

        def fetch(weights):
            cols = [jnp.split(w, G, axis=1) for w in weights]
            blocks = [jnp.concatenate([c[j] for c in cols], axis=1) for j in range(G)]
            sends = unxor(blocks, g)
            got = [sends[0]] + [flip(sends[d], d) for d in range(1, G)]
            rows = jnp.concatenate(unxor(got, g), axis=0)
            return lax.all_gather(rows, "dp", axis=0, axis_index_groups=z_groups, tiled=True)

        w_mix = fetch((w_branch, w_recur))
        gates = jnp.stack([w_decay, w_input]).reshape(2, G, heads, -1)
        sends = unxor([gates[:, j] for j in range(G)], g)
        got = [sends[0]] + [flip(sends[d], d) for d in range(1, G)]
        gates = jnp.stack(unxor(got, g))
        gates = gather_far(gates, z).reshape(n, 2, heads, -1)
        gates = jnp.transpose(gates, (1, 2, 0, 3)).reshape(2, heads, BW, BW)
        wg = [
            sum(
                jnp.pad(gates[q, h], ((h * BW, wide - (h + 1) * BW), (h * BW, wide - (h + 1) * BW)))
                for h in range(heads)
            )
            for q in range(2)
        ]
        wg = jnp.concatenate(wg, axis=1)
        w_mix = jnp.concatenate(
            [jnp.pad(w, ((0, 0), (0, wide - ch))) for w in (w_mix[:, :ch], w_mix[:, ch:])], axis=1
        )
        w_out_t = jnp.pad(fetch((w_out.T,)), ((0, 0), (0, wide - ch)))
        w_in = fetch((w_gate, w_up))
        w_down_t = fetch((w_down.T,))
        c_all = gather8(c_own)

        half = G * row
        x_float = x_all.astype(F32)
        normed_mix = rms_scale(x_float, mixer_gain_f).astype(BF)
        mix = dot(normed_mix, w_mix, 1, 0)
        mixed, values, pre, h_all = forward_call(mix, mask, par_f, wg)
        x_own_f = x_own.astype(F32)
        after_mix = x_own_f + scatter8(
            lambda h: dot(mixed[h * half : (h + 1) * half], w_out_t, 1, 1), row
        )
        normed_own = rms_scale(after_mix, mlp_gain_f).astype(BF)
        normed_mlp = gather8(normed_own)
        gate_up = dot(normed_mlp, w_in, 1, 0)
        gate_pre, up_pre = gate_up[:, :ff], gate_up[:, ff:]
        hidden = (jax.nn.gelu(gate_pre) * up_pre).astype(BF)
        result = after_mix + scatter8(
            lambda h: dot(hidden[h * half : (h + 1) * half], w_down_t, 1, 1), row
        )

        grad_down = dot(c_all, hidden, 0, 0)
        grad_hidden = dot(c_all, w_down_t, 1, 0)
        _, pull = jax.vjp(lambda a, b: jax.nn.gelu(a) * b, gate_pre, up_pre)
        grad_gate_pre, grad_up_pre = pull(grad_hidden)
        low = jnp.concatenate([grad_gate_pre.astype(BF), grad_up_pre.astype(BF)], axis=1)
        grad_in = dot(normed_mlp, low, 0, 0)
        grad_normed = scatter8(lambda h: dot(low[h * half : (h + 1) * half], w_in, 1, 1), row)
        _, pull = jax.vjp(rms_scale, after_mix, mlp_gain_f)
        grad_after, grad_mlp_gain = pull(grad_normed)
        grad_after = c_own.astype(F32) + grad_after
        after_low = gather8(grad_after.astype(BF))
        grad_out = dot(after_low, mixed, 0, 0)[:, :ch]
        grad_mixed = dot(after_low, w_out_t, 1, 0)

        mix_low, gate_low, acc = backward_call(mix, grad_mixed, mask, par_f, wg, values, pre, h_all)
        grad_gates = dot(values, gate_low, 0, 0)
        grad_gates = jnp.stack(
            [
                grad_gates[h * BW : (h + 1) * BW, q * wide + h * BW : q * wide + (h + 1) * BW]
                for q in range(2)
                for h in range(heads)
            ]
        )
        acc = jnp.sum(acc, axis=1)[:, :ch]
        chan_grad = jnp.concatenate(
            [acc[: taps + 2], acc[taps + 2 :] * (8.0 * jax.nn.sigmoid(-chan[taps + 2 :]))], axis=0
        )
        grad_mix = dot(normed_mix, mix_low, 0, 0)
        grad_mix = jnp.concatenate([grad_mix[:, :ch], grad_mix[:, wide : wide + ch]], axis=1)
        grad_normed_mix = scatter8(
            lambda h: dot(mix_low[h * half : (h + 1) * half], w_mix, 1, 1), row
        )
        _, pull = jax.vjp(rms_scale, x_own_f, mixer_gain_f)
        grad_x, grad_mix_gain = pull(grad_normed_mix)
        input_grad_own = grad_after + grad_x

        def give(grad, sizes):
            piece = lax.psum_scatter(
                grad.astype(BF), "dp", scatter_dimension=0, axis_index_groups=z_groups, tiled=True
            )
            sends = unxor([piece[j * depth : (j + 1) * depth] for j in range(G)], g)
            got = [sends[0]] + [flip(sends[d], d) for d in range(1, G)]
            got = [a.astype(F32) for a in unxor(got, g)]
            outs, at = [], 0
            for size in sizes:
                outs.append(jnp.concatenate([a[:, at : at + size] for a in got], axis=1))
                at += size
            return outs

        (out_down,) = give(grad_down, (ff,))
        out_gate, out_up = give(grad_in, (ff, ff))
        (out_out,) = give(grad_out, (ch,))
        out_branch, out_recur = give(grad_mix, (ch, ch))
        flat = jnp.transpose(grad_gates.reshape(2, heads, n, -1), (2, 0, 1, 3))
        piece = sum_far(flat.reshape((far, G) + flat.shape[1:]), z, lambda v: v.astype(BF)).astype(BF)
        sends = unxor([piece[j] for j in range(G)], g)
        got = unxor([sends[0]] + [flip(sends[d], d) for d in range(1, G)], g)
        got = jnp.concatenate(got, axis=1).astype(F32)
        out_decay, out_input = got[0], got[1]

        placed = jnp.concatenate([jnp.where(g == j, chan_grad, 0.0) for j in range(G)], axis=1)
        placed = jnp.transpose(placed.reshape(taps + 3, n, part), (1, 0, 2)).reshape(n, -1)
        packed = jnp.concatenate(
            [grad_mix_gain.reshape(n, depth), grad_mlp_gain.reshape(n, depth), placed], axis=1
        )
        packed = sum_far(packed.reshape(far, G, -1), z)
        sends = unxor([packed[j] for j in range(G)], g)
        packed = sends[0]
        for d in range(1, G):
            packed = packed + flip(sends[d], d)
        gains = packed[: 2 * depth]
        gains = gains + swap_core(gains)
        chan_out = packed[2 * depth :].reshape(taps + 3, part)

        def both_rows(own):
            other = swap_core(own)
            first = jnp.where(mp == 0, own, other)
            second = jnp.where(mp == 0, other, own)
            return jnp.stack([first, second])[:, None]

        return (
            both_rows(result),
            both_rows(input_grad_own),
            gains[:depth],
            gains[depth:],
            out_branch,
            out_recur,
            chan_out[:taps],
            out_decay,
            out_input,
            chan_out[taps : taps + 2],
            chan_out[taps + 2],
            out_out.T,
            out_gate,
            out_up,
            out_down.T,
        )

    return body


def solution(mesh):
    in_specs = (
        P(None, "dp", None, None),
        P(None, "dp", None),
        P(None, "dp", None, None),
        P("dp"),
        P("dp"),
        P("dp", "mp"),
        P("dp", "mp"),
        P(None, ("mp", "dp")),
        P("mp", "dp"),
        P("mp", "dp"),
        P(None, ("mp", "dp")),
        P(("mp", "dp")),
        P("mp", "dp"),
        P("dp", "mp"),
        P("dp", "mp"),
        P("mp", "dp"),
    )
    out_specs = (
        P(None, "dp", None, None),
        P(None, "dp", None, None),
        P("dp"),
        P("dp"),
        P("dp", "mp"),
        P("dp", "mp"),
        P(None, ("mp", "dp")),
        P("mp", "dp"),
        P("mp", "dp"),
        P(None, ("mp", "dp")),
        P(("mp", "dp")),
        P("mp", "dp"),
        P("dp", "mp"),
        P("dp", "mp"),
        P("mp", "dp"),
    )
    body = make_body(mesh.shape["dp"], mesh.shape["mp"])
    return jax.shard_map(body, mesh=mesh, in_specs=in_specs, out_specs=out_specs, check_vma=False)
```

time: 3980 us -> 911 us (0.23)
  waiting for transfers between devices: 2800 us -> 375 us
  blocking collectives: 295 us -> 0 us
  local copies, waits for them, and re-layouts: 372 us -> 82.4 us
  starting transfers between devices: 1.45 us -> 136 us
  matrix products: 302 us -> 171 us
  other arithmetic: 169 us -> 78.8 us
  Pallas kernels: 0 us -> 45 us
    reduce_scatter x6 -> x4, waiting for transfers between devices: 1700 us -> 0.05 us  [give(): lax.psum_scatter(grad.astype(BF), 'dp', scatter_dimension=0, axis_index_g...]
    unnamed x24 -> x8, waiting for transfers between devices: 528 us -> 0.13 us
    all_gather x6 -> x4, waiting for transfers between devices: 471 us -> 35.3 us  [fetch(): lax.all_gather(rows, 'dp', axis=0, axis_index_groups=z_groups, tiled=True)]
    ppermute x0 -> x87, waiting for transfers between devices: none -> 339 us  [the longest x63 329 us: flip(): return lax.ppermute(a, 'dp', flips[d])]
    all_gather x6 -> x0, blocking collectives: 185 us -> none  [the longest x1 33.6 us: body(): lax.all_gather(w_input, 'dp', axis=1, tiled=True)]
    slice x122 -> x24, local copies, waits for them, and re-layouts: 164 us -> 13.1 us  [the longest x4 5.36 us: scatter8(): pieces = [mine[d * own_rows:(d + 1) * own_rows] for d in range(G)]]
    ppermute x0 -> x87, starting transfers between devices: none -> 136 us  [the longest x63 58.8 us: flip(): return lax.ppermute(a, 'dp', flips[d])]
    dot_general x48 -> x17, matrix products: 302 us -> 171 us  [dot(): lax.dot_general(a, b, (((ca,), (cb,)), ((), ())), preferred_element_type=...]
  transfers between devices with their start and end apart: 20 -> 95, of which waited for: 15 -> 36; matrix products, arithmetic and copies ran while one was open for 13% -> 32% of each run, Pallas kernels for 0% -> 5%
where the time goes in v1:
time: 911 us; the launch traced here: 905 us
  waiting for transfers between devices  375 us (41%)
  matrix products  171 us (19%)
  starting transfers between devices  136 us (15%)
  local copies, waits for them, and re-layouts  82.4 us (9%)
  other arithmetic  78.8 us (9%)
  Pallas kernels  45 us (5%)
  between operations  15.6 us (2%)
    ppermute x63, waiting for transfers between devices, flip(): return lax.ppermute(a, 'dp', flips[d])  329 us
    dot_general x17, matrix products, dot(): lax.dot_general(a, b, (((ca,), (cb,)), ((), ())), preferred_element_type=...  171 us
    ppermute x63, starting transfers between devices, flip(): return lax.ppermute(a, 'dp', flips[d])  58.8 us
    ppermute x12, starting transfers between devices, swap_core(): return lax.ppermute(a, 'mp', cores)  51.7 us
    all_gather x4, waiting for transfers between devices, fetch(): lax.all_gather(rows, 'dp', axis=0, axis_index_groups=z_groups, tiled=True)  35.3 us
    unnamed x148, local copies, waits for them, and re-layouts  32.8 us
    pallas_call x1, Pallas kernels, backward_call(): pl.pallas_call(functools.partial(backward_kernel, cp, row, unroll), in_sp...  27 us
    ppermute x12, starting transfers between devices, far_flip(): return lax.ppermute(a, 'dp', far_flips[k])  25.1 us
  transfers between devices with their start and end apart: 95, of which 36 were waited for; matrix products, arithmetic and copies ran while one was open for 32% of the time, Pallas kernels for 5%

profile of v1, /device:TPU:1, one launch (start us, length us, event | category | flops | bytes accessed | tf_op | source)
XLA Modules:
  0.0 904.6 jit_solution(16713427553293234462)
XLA Ops:
  39.5 44.5 %collective-permute-done.11 = bf16[128,640]{0,1:T(8,128)(2,1)} collective-permute-done((bf16[128,640]{0,1:T(8,128)(2,1)}, bf16[128,640]{0,1:T(8,128)(2,1)}, u32[]{:S(2)}, u32[]{:S(2)}) %collective-permute-start.11) | collective-permute-done | bytes 163872 | tf_op jit(solution)/shard_map/ppermute | solution.py:338
  137.0 11.4 %all-gather.5.cloned.1.call-done = bf16[2048,640]{0,1:T(8,128)(2,1)} async-done(((bf16[512,640]{0,1:T(8,128)(2,1)}), bf16[2048,640]{0,1:T(8,128)(2,1)}) %all-gather.5.cloned.1.call-update) | async-done | bytes 2621456 | tf_op jit(solution)/shard_map/all_gather | solution.py:438
  173.9 17.9 %recur_forward.1 = (bf16[2048,384]{1,0:T(8,128)(2,1)}, bf16[2048,384]{1,0:T(8,128)(2,1)}, f32[6,2112,128]{2,1,0:T(8,128)}, f32[3,2112,128]{2,1,0:T(8,128)}) custom-call(f32[2048,768]{1,0:T(8,128)} %fusion.20.mix_hbm, f32[3,2048,128]{2,1,0:T(8,128)} %broadcast_in_dim.57.mask_ref, f32[7,8,384]{2,1,0:T(8,128)} %broadcast_in_dim.60.par_ref, ...), custom_call_target="tpu_custom_call" | custom-call | tf_op jit(solution)/shard_map/recur_forward/pallas_call | solution.py:122
  232.6 17.3 %collective-permute-done.27 = bf16[256,2048]{1,0:T(8,128)(2,1)S(1)} collective-permute-done((bf16[256,2048]{1,0:T(8,128)(2,1)S(1)}, bf16[256,2048]{1,0:T(8,128)(2,1)S(1)}, u32[]{:S(2)}, u32[]{:S(2)}) %collective-permute-start.27) | collective-permute-done | bytes 1048608 | tf_op jit(solution)/shard_map/ppermute | solution.py:338
  251.1 22.2 %collective-permute-done.29 = bf16[256,2048]{1,0:T(8,128)(2,1)S(1)} collective-permute-done((bf16[256,2048]{1,0:T(8,128)(2,1)S(1)}, bf16[256,2048]{1,0:T(8,128)(2,1)S(1)}, u32[]{:S(2)}, u32[]{:S(2)}) %collective-permute-start.29) | collective-permute-done | bytes 1048608 | tf_op jit(solution)/shard_map/ppermute | solution.py:338
  277.9 17.9 %collective-permute-done.47 = bf16[256,2048]{1,0:T(8,128)(2,1)S(1)} collective-permute-done((bf16[256,2048]{1,0:T(8,128)(2,1)S(1)}, bf16[256,2048]{1,0:T(8,128)(2,1)S(1)}, u32[]{:S(2)}, u32[]{:S(2)}) %collective-permute-start.47) | collective-permute-done | bytes 1048608 | tf_op jit(solution)/shard_map/ppermute | solution.py:338
  297.0 23.0 %collective-permute-done.46 = bf16[256,2048]{1,0:T(8,128)(2,1)S(1)} collective-permute-done((bf16[256,2048]{1,0:T(8,128)(2,1)S(1)}, bf16[256,2048]{1,0:T(8,128)(2,1)S(1)}, u32[]{:S(2)}, u32[]{:S(2)}) %collective-permute-start.46) | collective-permute-done | bytes 1048608 | tf_op jit(solution)/shard_map/ppermute | solution.py:338
  322.7 26.3 %collective-permute-start.48 = (bf16[1024,2048]{1,0:T(8,128)(2,1)}, bf16[1024,2048]{1,0:T(8,128)(2,1)}, u32[]{:S(2)}, u32[]{:S(2)}) collective-permute-start(bf16[1024,2048]{1,0:T(8,128)(2,1)} %pad_maximum_fusion.4), channel_id=1, source_target_pairs={{0,1},{1,0},{2,3},{3,2},{4,5},{5,4},{6,7},{7,6},{8,9},{9,8},{10,11... | collective-permute-start | bytes 12582920 | tf_op jit(solution)/shard_map/ppermute | solution.py:359
  349.0 15.0 %collective-permute-done.31 = bf16[256,2048]{1,0:T(8,128)(2,1)S(1)} collective-permute-done((bf16[256,2048]{1,0:T(8,128)(2,1)S(1)}, bf16[256,2048]{1,0:T(8,128)(2,1)S(1)}, u32[]{:S(2)}, u32[]{:S(2)}) %collective-permute-start.31) | collective-permute-done | bytes 1048608 | tf_op jit(solution)/shard_map/ppermute | solution.py:338
  402.5 19.0 %fusion.122 = f32[2048,1536]{0,1:T(8,128)} fusion(bf16[2048,2048]{1,0:T(8,128)(2,1)} %constant_dynamic-update-slice_fusion.12, bf16[2048,1536]{1,0:T(8,128)(2,1)} %all-gather.9.cloned.1.call-done), kind=kOutput, calls=%fused_computation.449 | convolution fusion | flops 12884901888 | bytes 27262976 | tf_op jit(solution)/shard_map/dot_general | solution.py:315
  421.6 23.8 %all-gather.11.cloned.1.call-done = bf16[2048,768]{1,0:T(8,128)(2,1)} async-done(((bf16[512,768]{1,0:T(8,128)(2,1)}), bf16[2048,768]{1,0:T(8,128)(2,1)}) %all-gather.11.cloned.1.call-update) | async-done | bytes 3145744 | tf_op jit(solution)/shard_map/all_gather | solution.py:438
  445.4 19.9 %multiply_convert_fusion = (bf16[2048,768]{0,1:T(8,128)(2,1)}, bf16[2048,768]{0,1:T(8,128)(2,1)}, bf16[2048,768]{0,1:T(8,128)(2,1)}) fusion(f32[2048,1536]{0,1:T(8,128)} %fusion.122, bf16[2048,2048]{1,0:T(8,128)(2,1)} %constant_dynamic-update-slice_fusion.17, bf16[2048,768]{1,0:T(8,128)(2,1)} %all-gather.11.cloned.1.call-done), kind=kOutput, calls=%fused_computation.25 | convolution fusion | flops 6483345408 | bytes 33554432 | tf_op jit(solution)/shard_map/dot_general | solution.py:315
  465.3 11.4 %convolution_convert_fusion.1 = bf16[1024,2048]{1,0:T(8,128)(2,1)} fusion(bf16[2048,1536]{1,0:T(8,128)(2,1)} %all-gather.9.cloned.1.call-done, bf16[2048,768]{0,1:T(8,128)(2,1)} %get-tuple-element.127, bf16[2048,768]{0,1:T(8,128)(2,1)} %get-tuple-element.126), kind=kOutput, calls=%fused_computation.40 | convolution fusion | flops 6450839552 | bytes 16777216 | tf_op jit(solution)/shard_map/dot_general | solution.py:315
  495.9 12.9 %fusion.119 = (bf16[1024,2048]{1,0:T(8,128)(2,1)S(1)}, f32[1024,2048]{1,0:T(8,128)}) fusion(bf16[1024,2048]{1,0:T(8,128)(2,1)} %collective-permute-done.49, bf16[2048,1536]{1,0:T(8,128)(2,1)} %all-gather.9.cloned.1.call-done, bf16[2048,768]{0,1:T(8,128)(2,1)} %get-tuple-element.127, bf16[2048,768]{0,1:T(8,128)(2,1)} %get-tuple-element.126), kind=kOutput, calls=%fused_computation.446 | convolution fusion | flops 6455033856 | bytes 29360128 | tf_op jit(solution)/shard_map/dot_general | solution.py:315
  513.0 17.2 %convolution_convert_fusion = bf16[2048,1536]{1,0:T(8,128)(2,1)} fusion(bf16[2048,2048]{1,0:T(8,128)(2,1)S(1)} %bitcast.190, bf16[2048,768]{0,1:T(8,128)(2,1)} %get-tuple-element.126, bf16[2048,768]{0,1:T(8,128)(2,1)} %get-tuple-element.127), kind=kOutput, calls=%fused_computation.16 | convolution fusion | flops 12900630528 | bytes 20971520 | tf_op jit(solution)/shard_map/dot_general | solution.py:315
  534.7 23.4 %collective-permute-done.52 = bf16[256,2048]{1,0:T(8,128)(2,1)} collective-permute-done((bf16[256,2048]{1,0:T(8,128)(2,1)}, bf16[256,2048]{1,0:T(8,128)(2,1)}, u32[]{:S(2)}, u32[]{:S(2)}) %collective-permute-start.52) | collective-permute-done | bytes 1048608 | tf_op jit(solution)/shard_map/ppermute | solution.py:338
  566.1 20.3 %collective-permute-done.55 = bf16[256,2048]{1,0:T(8,128)(2,1)S(1)} collective-permute-done((bf16[256,2048]{1,0:T(8,128)(2,1)S(1)}, bf16[256,2048]{1,0:T(8,128)(2,1)S(1)}, u32[]{:S(2)}, u32[]{:S(2)}) %collective-permute-start.55) | collective-permute-done | bytes 1048608 | tf_op jit(solution)/shard_map/ppermute | solution.py:338
  586.5 25.6 %collective-permute-done.54 = bf16[256,2048]{1,0:T(8,128)(2,1)S(1)} collective-permute-done((bf16[256,2048]{1,0:T(8,128)(2,1)S(1)}, bf16[256,2048]{1,0:T(8,128)(2,1)S(1)}, u32[]{:S(2)}, u32[]{:S(2)}) %collective-permute-start.54) | collective-permute-done | bytes 1048608 | tf_op jit(solution)/shard_map/ppermute | solution.py:338
  636.5 20.0 %collective-permute-done.86 = bf16[128,768]{1,0:T(8,128)(2,1)S(1)} collective-permute-done((bf16[128,768]{1,0:T(8,128)(2,1)S(1)}, bf16[128,768]{1,0:T(8,128)(2,1)S(1)}, u32[]{:S(2)}, u32[]{:S(2)}) %collective-permute-start.86) | collective-permute-done | bytes 196640 | tf_op jit(solution)/shard_map/ppermute | solution.py:338
  686.8 27.0 %recur_backward.1 = (bf16[2048,768]{1,0:T(8,128)(2,1)}, bf16[2048,768]{1,0:T(8,128)(2,1)}, f32[7,8,384]{2,1,0:T(8,128)}) custom-call(f32[2048,768]{1,0:T(8,128)} %fusion.20.mix_hbm, f32[2048,384]{1,0:T(8,128)} %fusion.47.gm_hbm, f32[3,2048,128]{2,1,0:T(8,128)} %broadcast_in_dim.57.mask_ref, f32[7,8,384]{2,1,0:T(8,128)} %broadcast_in_dim.60.par_ref, ...), custom_call_target="tpu_custom_call" | custom-call | tf_op jit(solution)/shard_map/recur_backward/pallas_call | solution.py:278
  789.1 18.6 %collective-permute-done.58 = bf16[256,2048]{1,0:T(8,128)(2,1)} collective-permute-done((bf16[256,2048]{1,0:T(8,128)(2,1)}, bf16[256,2048]{1,0:T(8,128)(2,1)}, u32[]{:S(2)}, u32[]{:S(2)}) %collective-permute-start.58) | collective-permute-done | bytes 1048608 | tf_op jit(solution)/shard_map/ppermute | solution.py:338
  808.4 17.0 %collective-permute-done.60 = bf16[256,2048]{1,0:T(8,128)(2,1)} collective-permute-done((bf16[256,2048]{1,0:T(8,128)(2,1)}, bf16[256,2048]{1,0:T(8,128)(2,1)}, u32[]{:S(2)}, u32[]{:S(2)}) %collective-permute-start.60) | collective-permute-done | bytes 1048608 | tf_op jit(solution)/shard_map/ppermute | solution.py:338
  831.9 13.8 %collective-permute-start.64 = (f32[4,816]{1,0:T(4,128)S(1)}, f32[4,816]{1,0:T(4,128)S(1)}, u32[]{:S(2)}, u32[]{:S(2)}) collective-permute-start(f32[4,816]{1,0:T(4,128)S(1)} %get-tuple-element.265), channel_id=1, source_target_pairs={{0,24},{2,26},{4,28},{6,30},{8,16},{10,18},{12,20},{14,22},{16,8},... | collective-permute-start | bytes 39176 | tf_op jit(solution)/shard_map/ppermute | solution.py:343
  862.3 13.6 %collective-permute-start.68 = (f32[256]{0:T(256)S(1)}, f32[256]{0:T(256)S(1)}, u32[]{:S(2)}, u32[]{:S(2)}) collective-permute-start(f32[256]{0:T(256)S(1)} %slice.402), channel_id=1, source_target_pairs={{0,1},{1,0},{2,3},{3,2},{4,5},{5,4},{6,7},{7,6},{8,9},{9,8},{10,11... | collective-permute-start | bytes 3080 | tf_op jit(solution)/shard_map/ppermute | solution.py:359
  (502 shorter events, 409.8 us)
Async XLA Ops:
  7.2 141.2 %all-gather.5.cloned.1.call-start = ((), (), s32[]{:S(2)}) async-start(), calls=%async_computation.4 | async-start | bytes 3276800 | tf_op jit(solution)/shard_map/all_gather | solution.py:438
  28.4 69.0 %collective-permute-start.2 = (bf16[256,2048]{1,0:T(8,128)(2,1)S(1)}, bf16[256,2048]{1,0:T(8,128)(2,1)S(1)}, u32[]{:S(2)}, u32[]{:S(2)}) collective-permute-start(bf16[256,2048]{1,0:T(8,128)(2,1)S(1)} %get-tuple-element.99), channel_id=1, source_target_pairs={{0,6},{2,4},{4,2},{6,0},{8,14},{10,12},{12,10},{14,8},{16,22},{18,... | collective-permute-start | bytes 3145736 | tf_op jit(solution)/shard_map/ppermute | solution.py:338
  30.7 67.8 %collective-permute-start.1 = (bf16[256,2048]{1,0:T(8,128)(2,1)S(1)}, bf16[256,2048]{1,0:T(8,128)(2,1)S(1)}, u32[]{:S(2)}, u32[]{:S(2)}) collective-permute-start(bf16[256,2048]{1,0:T(8,128)(2,1)S(1)} %get-tuple-element.99), channel_id=1, source_target_pairs={{0,4},{2,6},{4,0},{6,2},{8,12},{10,14},{12,8},{14,10},{16,20},{18,... | collective-permute-start | bytes 3145736 | tf_op jit(solution)/shard_map/ppermute | solution.py:338
  31.0 53.1 %collective-permute-start.11 = (bf16[128,640]{0,1:T(8,128)(2,1)}, bf16[128,640]{0,1:T(8,128)(2,1)}, u32[]{:S(2)}, u32[]{:S(2)}) collective-permute-start(bf16[128,640]{0,1:T(8,128)(2,1)} %get-tuple-element.120), channel_id=1, source_target_pairs={{0,4},{2,6},{4,0},{6,2},{8,12},{10,14},{12,8},{14,10},{16,20},{18,... | collective-permute-start | bytes 491528 | tf_op jit(solution)/shard_map/ppermute | solution.py:338
  32.3 53.2 %collective-permute-start.12 = (bf16[128,640]{0,1:T(8,128)(2,1)}, bf16[128,640]{0,1:T(8,128)(2,1)}, u32[]{:S(2)}, u32[]{:S(2)}) collective-permute-start(bf16[128,640]{0,1:T(8,128)(2,1)} %get-tuple-element.211), channel_id=1, source_target_pairs={{0,2},{2,0},{4,6},{6,4},{8,10},{10,8},{12,14},{14,12},{16,18},{18,... | collective-permute-start | bytes 491528 | tf_op jit(solution)/shard_map/ppermute | solution.py:338
  36.8 50.9 %collective-permute-start.10 = (bf16[128,640]{0,1:T(8,128)(2,1)}, bf16[128,640]{0,1:T(8,128)(2,1)}, u32[]{:S(2)}, u32[]{:S(2)}) collective-permute-start(bf16[128,640]{0,1:T(8,128)(2,1)} %broadcast_select_fusion.87), channel_id=1, source_target_pairs={{0,6},{2,4},{4,2},{6,0},{8,14},{10,12},{12,10},{14,8},{16,22},{18,... | collective-permute-start | bytes 491528 | tf_op jit(solution)/shard_map/ppermute | solution.py:338
  91.1 100.7 %all-gather.7.cloned.1.call-start = ((), (), s32[]{:S(2)}) async-start(), calls=%async_computation.5 | async-start | bytes 1638400 | tf_op jit(solution)/shard_map/all_gather | solution.py:438
  132.3 270.2 %all-gather.9.cloned.1.call-start = ((), (), s32[]{:S(2)}) async-start(), calls=%async_computation.6 | async-start | bytes 7864320 | tf_op jit(solution)/shard_map/all_gather | solution.py:438
  220.4 224.9 %all-gather.11.cloned.1.call-start = ((), (), s32[]{:S(2)}) async-start(), calls=%async_computation.7 | async-start | bytes 3932160 | tf_op jit(solution)/shard_map/all_gather | solution.py:438
  230.2 65.7 %collective-permute-start.47 = (bf16[256,2048]{1,0:T(8,128)(2,1)S(1)}, bf16[256,2048]{1,0:T(8,128)(2,1)S(1)}, u32[]{:S(2)}, u32[]{:S(2)}) collective-permute-start(bf16[256,2048]{1,0:T(8,128)(2,1)S(1)} %get-tuple-element.104), channel_id=1, source_target_pairs={{0,6},{2,4},{4,2},{6,0},{8,14},{10,12},{12,10},{14,8},{16,22},{18,... | collective-permute-start | bytes 3145736 | tf_op jit(solution)/shard_map/ppermute | solution.py:338
  232.3 87.7 %collective-permute-start.46 = (bf16[256,2048]{1,0:T(8,128)(2,1)S(1)}, bf16[256,2048]{1,0:T(8,128)(2,1)S(1)}, u32[]{:S(2)}, u32[]{:S(2)}) collective-permute-start(bf16[256,2048]{1,0:T(8,128)(2,1)S(1)} %get-tuple-element.104), channel_id=1, source_target_pairs={{0,4},{2,6},{4,0},{6,2},{8,12},{10,14},{12,8},{14,10},{16,20},{18,... | collective-permute-start | bytes 3145736 | tf_op jit(solution)/shard_map/ppermute | solution.py:338
  249.9 70.1 %collective-permute-start.45 = (bf16[256,2048]{1,0:T(8,128)(2,1)S(1)}, bf16[256,2048]{1,0:T(8,128)(2,1)S(1)}, u32[]{:S(2)}, u32[]{:S(2)}) collective-permute-start(bf16[256,2048]{1,0:T(8,128)(2,1)S(1)} %get-tuple-element.104), channel_id=1, source_target_pairs={{0,2},{2,0},{4,6},{6,4},{8,10},{10,8},{12,14},{14,12},{16,18},{18,... | collective-permute-start | bytes 3145736 | tf_op jit(solution)/shard_map/ppermute | solution.py:338
  275.6 73.4 %collective-permute-start.32 = (bf16[256,2048]{1,0:T(8,128)(2,1)S(1)}, bf16[256,2048]{1,0:T(8,128)(2,1)S(1)}, u32[]{:S(2)}, u32[]{:S(2)}) collective-permute-start(bf16[256,2048]{1,0:T(8,128)(2,1)S(1)} %get-tuple-element.109), channel_id=1, source_target_pairs={{0,6},{2,4},{4,2},{6,0},{8,14},{10,12},{12,10},{14,8},{16,22},{18,... | collective-permute-start | bytes 3145736 | tf_op jit(solution)/shard_map/ppermute | solution.py:338
  276.7 87.3 %collective-permute-start.31 = (bf16[256,2048]{1,0:T(8,128)(2,1)S(1)}, bf16[256,2048]{1,0:T(8,128)(2,1)S(1)}, u32[]{:S(2)}, u32[]{:S(2)}) collective-permute-start(bf16[256,2048]{1,0:T(8,128)(2,1)S(1)} %get-tuple-element.109), channel_id=1, source_target_pairs={{0,4},{2,6},{4,0},{6,2},{8,12},{10,14},{12,8},{14,10},{16,20},{18,... | collective-permute-start | bytes 3145736 | tf_op jit(solution)/shard_map/ppermute | solution.py:338
  295.8 68.2 %collective-permute-start.30 = (bf16[256,2048]{1,0:T(8,128)(2,1)S(1)}, bf16[256,2048]{1,0:T(8,128)(2,1)S(1)}, u32[]{:S(2)}, u32[]{:S(2)}) collective-permute-start(bf16[256,2048]{1,0:T(8,128)(2,1)S(1)} %get-tuple-element.109), channel_id=1, source_target_pairs={{0,2},{2,0},{4,6},{6,4},{8,10},{10,8},{12,14},{14,12},{16,18},{18,... | collective-permute-start | bytes 3145736 | tf_op jit(solution)/shard_map/ppermute | solution.py:338
  322.7 66.6 %collective-permute-start.48 = (bf16[1024,2048]{1,0:T(8,128)(2,1)}, bf16[1024,2048]{1,0:T(8,128)(2,1)}, u32[]{:S(2)}, u32[]{:S(2)}) collective-permute-start(bf16[1024,2048]{1,0:T(8,128)(2,1)} %pad_maximum_fusion.4), channel_id=1, source_target_pairs={{0,1},{1,0},{2,3},{3,2},{4,5},{5,4},{6,7},{7,6},{8,9},{9,8},{10,11... | collective-permute-start | bytes 12582920 | tf_op jit(solution)/shard_map/ppermute | solution.py:359
  383.5 244.4 %reduce-scatter.11.cloned.1.call-start = ((), (), s32[]{:S(2)}) async-start(), calls=%async_computation.11 | async-start | bytes 3932160 | tf_op jit(solution)/shard_map/reduce_scatter | solution.py:518
  487.9 264.9 %reduce-scatter.9.cloned.1.call-start = ((), (), s32[]{:S(2)}) async-start(), calls=%async_computation.10 | async-start | bytes 7864320 | tf_op jit(solution)/shard_map/reduce_scatter | solution.py:518
  495.9 119.2 %collective-permute-start.40 = (bf16[1024,2048]{1,0:T(8,128)(2,1)}, bf16[1024,2048]{1,0:T(8,128)(2,1)}, u32[]{:S(2)}, u32[]{:S(2)}) collective-permute-start(bf16[1024,2048]{1,0:T(8,128)(2,1)} %convolution_convert_fusion.4), channel_id=1, source_target_pairs={{0,1},{1,0},{2,3},{3,2},{4,5},{5,4},{6,7},{7,6},{8,9},{9,8},{10,11... | collective-permute-start | bytes 12582920 | tf_op jit(solution)/shard_map/ppermute | solution.py:359
  530.2 257.9 %reduce-scatter.7.cloned.1.call-start = ((), (), s32[]{:S(2)}) async-start(), calls=%async_computation.9 | async-start | bytes 1638400 | tf_op jit(solution)/shard_map/reduce_scatter | solution.py:518
  614.7 50.4 %collective-permute-start.56 = (bf16[1024,2048]{1,0:T(8,128)(2,1)}, bf16[1024,2048]{1,0:T(8,128)(2,1)}, u32[]{:S(2)}, u32[]{:S(2)}) collective-permute-start(bf16[1024,2048]{1,0:T(8,128)(2,1)} %pad_maximum_fusion.5), channel_id=1, source_target_pairs={{0,1},{1,0},{2,3},{3,2},{4,5},{5,4},{6,7},{7,6},{8,9},{9,8},{10,11... | collective-permute-start | bytes 12582920 | tf_op jit(solution)/shard_map/ppermute | solution.py:359
  627.3 234.3 %collective-permute-start.41 = (bf16[256,2048]{1,0:T(8,128)(2,1)}, bf16[256,2048]{1,0:T(8,128)(2,1)}, u32[]{:S(2)}, u32[]{:S(2)}) collective-permute-start(bf16[256,2048]{1,0:T(8,128)(2,1)} %get-tuple-element.139), channel_id=1, source_target_pairs={{0,2},{2,0},{4,6},{6,4},{8,10},{10,8},{12,14},{14,12},{16,18},{18,... | collective-permute-start | bytes 3145736 | tf_op jit(solution)/shard_map/ppermute | solution.py:338
  735.5 114.2 %reduce-scatter.5.cloned.1.call-start = ((), (), s32[]{:S(2)}) async-start(), calls=%async_computation.8 | async-start | bytes 3276800 | tf_op jit(solution)/shard_map/reduce_scatter | solution.py:518
  761.4 100.9 %collective-permute-start.43 = (bf16[256,2048]{1,0:T(8,128)(2,1)}, bf16[256,2048]{1,0:T(8,128)(2,1)}, u32[]{:S(2)}, u32[]{:S(2)}) collective-permute-start(bf16[256,2048]{1,0:T(8,128)(2,1)} %get-tuple-element.140), channel_id=1, source_target_pairs={{0,6},{2,4},{4,2},{6,0},{8,14},{10,12},{12,10},{14,8},{16,22},{18,... | collective-permute-start | bytes 3145736 | tf_op jit(solution)/shard_map/ppermute | solution.py:338
  (129 other events, 2215.7 us)
Sparse Core Ops, SparseCore 0:
  91.2 57.1 all-gather.4
  150.6 30.6 all-gather.6
  220.6 114.8 all-gather.8
  383.6 61.7 all-gather.10
  488.0 58.1 reduce-scatter.10
  548.4 110.9 reduce-scatter.8
  735.6 30.6 reduce-scatter.6
  768.6 51.0 reduce-scatter.4

commit v2 on v1

--- a/solution.py
+++ b/solution.py
@@ -12,6 +12,7 @@
 BF = jnp.bfloat16
 F32 = jnp.float32
 ROWS = 8
+HALF = ROWS // 2
 PAD = 8
 C0 = 0.7978845608028654
 C1 = 0.044715
@@ -30,11 +31,12 @@
     return r, i, a, gap
 
 
-def forward_kernel(cp, row, unroll, mix_hbm, mask_ref, par_ref, wg_ref, mixed_ref, values_ref, pre_ref, h_ref, vals, mixf, mix, sems):
+def forward_kernel(cp, row, unroll, extra, near_hbm, far_hbm, mask_ref, par_ref, wg_ref, *refs):
+    mixed_ref, values_ref, pre_ref, h_ref, vals, mixf, mix, sems = refs[extra:]
     lanes = cp // 128
     order = list(range(lanes, 2 * lanes)) + list(range(lanes))
     copies = {
-        j: [pltpu.make_async_copy(mix_hbm.at[pl.ds(r * row, row), pl.ds(128 * j, 128)], mix.at[j, pl.ds(r * (row + PAD), row)], sems.at[j, r]) for r in range(ROWS)] for j in order
+        j: [pltpu.make_async_copy((near_hbm, far_hbm)[r // HALF].at[pl.ds(r % HALF * row, row), pl.ds(128 * j, 128)], mix.at[j, pl.ds(r * (row + PAD), row)], sems.at[j, r]) for r in range(ROWS)] for j in order
     }
     for j in order:
         for c in copies[j]:
@@ -114,14 +116,15 @@
         mixed_ref[rows, :] = flat(mixf, pl.ds(r * (row + PAD), row)).astype(BF)
 
 
-def forward_call(mix, mask, par, wg, unroll=8):
-    tokens, cp = mix.shape[0], mix.shape[1] // 2
+def forward_call(near, far, mask, par, wg, *earlier, unroll=8):
+    tokens, cp = 2 * near.shape[0], near.shape[1] // 2
     row = tokens // ROWS
     lanes = cp // 128
     vm = pl.BlockSpec(memory_space=pltpu.VMEM)
+    hbm = pl.BlockSpec(memory_space=pl.ANY)
     return pl.pallas_call(
-        functools.partial(forward_kernel, cp, row, unroll),
-        in_specs=[pl.BlockSpec(memory_space=pl.ANY), vm, vm, vm],
+        functools.partial(forward_kernel, cp, row, unroll, len(earlier)),
+        in_specs=[hbm] * 2 + [vm] * 3 + [hbm] * len(earlier),
         out_specs=(vm, vm, vm, vm),
         out_shape=(
             jax.ShapeDtypeStruct((tokens, cp), BF),
@@ -136,20 +139,23 @@
             pltpu.SemaphoreType.DMA((2 * lanes, ROWS)),
         ],
         compiler_params=pltpu.CompilerParams(vmem_limit_bytes=60 * 1024 * 1024),
+        cost_estimate=pl.CostEstimate(flops=150 * tokens * cp, bytes_accessed=84 * tokens * cp, transcendentals=6 * tokens * cp),
         name="recur_forward",
-    )(mix, mask, par, wg)
+    )(near, far, mask, par, wg, *earlier)
 
 
 def backward_kernel(
-    cp, row, unroll, mix_hbm, gm_hbm, mask_ref, par_ref, wg_ref, values_ref, pre_ref, h_ref,
-    mixlow_ref, low_ref, acc_ref, vals, mix, gm, gdec, ginp, gval, sems,
+    cp, row, unroll, extra, mix_near, mix_far, gm_near, gm_far, mask_ref, par_ref, wg_ref, values_ref, pre_ref, h_ref,
+    *refs,
 ):
+    mixlow_ref, low_ref, acc_ref, vals, mix, gm, gdec, ginp, gval, sems = refs[extra:]
     lanes = cp // 128
     pitch = row + PAD
     copies = []
     for j in range(lanes):
         for r in range(ROWS):
-            src = pl.ds(r * row, row)
+            src = pl.ds(r % HALF * row, row)
+            mix_hbm, gm_hbm = ((mix_near, gm_near), (mix_far, gm_far))[r // HALF]
             dst = pl.ds(r * pitch, row)
             cols = pl.ds(128 * j, 128)
             rec = pl.ds(cp + 128 * j, 128)
@@ -268,16 +274,16 @@
         mixlow_ref[pl.ds(r * row, row), pl.ds(cp, cp)] = flat(gdec, pl.ds(r * pitch, row)).astype(BF)
 
 
-def backward_call(mix, gm, mask, par, wg, values, pre, h, unroll=4):
-    tokens, cp = gm.shape
+def backward_call(mix, gm, mask, par, wg, values, pre, h, *earlier, unroll=4):
+    tokens, cp = 2 * gm[0].shape[0], gm[0].shape[1]
     row = tokens // ROWS
     lanes = cp // 128
     vm = pl.BlockSpec(memory_space=pltpu.VMEM)
     hbm = pl.BlockSpec(memory_space=pl.ANY)
     slab = pltpu.VMEM((lanes, tokens + ROWS * PAD, 128), F32)
     return pl.pallas_call(
-        functools.partial(backward_kernel, cp, row, unroll),
-        in_specs=[hbm, hbm, vm, vm, vm, vm, vm, vm],
+        functools.partial(backward_kernel, cp, row, unroll, len(earlier)),
+        in_specs=[hbm] * 4 + [vm] * 6 + [hbm] * len(earlier),
         out_specs=(vm, vm, vm),
         out_shape=(
             jax.ShapeDtypeStruct((tokens, 2 * cp), BF),
@@ -294,8 +300,9 @@
             pltpu.SemaphoreType.DMA((3, lanes, ROWS)),
         ],
         compiler_params=pltpu.CompilerParams(vmem_limit_bytes=60 * 1024 * 1024),
+        cost_estimate=pl.CostEstimate(flops=200 * tokens * cp, bytes_accessed=128 * tokens * cp, transcendentals=6 * tokens * cp),
         name="recur_backward",
-    )(mix, gm, mask, par, wg, values, pre, h)
+    )(*mix, *gm, mask, par, wg, values, pre, h, *earlier)
 
 
 def rms_scale(values, norm_gain):
@@ -315,62 +322,33 @@
     return lax.dot_general(a, b, (((ca,), (cb,)), ((), ())), preferred_element_type=out)
 
 
-def unxor(pieces, g):
-    low, high = (g & 1) == 1, (g >> 1) == 1
-    p0, p1, p2, p3 = pieces
-    q0, q1 = jnp.where(low, p1, p0), jnp.where(low, p0, p1)
-    q2, q3 = jnp.where(low, p3, p2), jnp.where(low, p2, p3)
-    return [
-        jnp.where(high, q2, q0),
-        jnp.where(high, q3, q1),
-        jnp.where(high, q0, q2),
-        jnp.where(high, q1, q3),
-    ]
-
-
 def make_body(n, m):
     far = n // G
-    z_groups = [[c + G * k for k in range(far)] for c in range(G)]
-    flips = [[(i, i ^ d) for i in range(n)] for d in range(G)]
+    planes = [[G * k + c for c in range(G)] for k in range(far)]
+    lines = [[c + G * k for k in range(far)] for c in range(G)]
     cores = [(0, 1), (1, 0)]
 
-    def flip(a, d):
-        return lax.ppermute(a, "dp", flips[d])
-
-    far_flips = [[(i, i ^ (G * k)) for i in range(n)] for k in range(far)]
-
-    def far_flip(a, k):
-        return lax.ppermute(a, "dp", far_flips[k])
+    def trade(a, groups=planes):
+        return lax.all_to_all(a, "dp", 0, 0, axis_index_groups=groups, tiled=True)
+
+    def spread(a, groups=planes):
+        return trade(jnp.broadcast_to(a, (len(groups[0]),) + a.shape), groups)
+
+    def swap_core(a):
+        return lax.ppermute(a, "mp", cores)
 
     def pick(a, i):
         return lax.dynamic_index_in_dim(a, i, 0, keepdims=False)
 
-    def gather_far(a, z):
-        got = jnp.stack([a] + [far_flip(a, k) for k in range(1, far)])
-        return jnp.stack([pick(got, z ^ j) for j in range(far)])
-
-    def sum_far(a, z, low=lambda v: v):
-        total = pick(a, z)
-        for k in range(1, far):
-            total = total + far_flip(low(pick(a, z ^ k)), k).astype(F32)
+    def index_zero(*earlier):
+        total = jnp.int32(0)
+        for a in earlier:
+            e = a[(0,) * a.ndim]
+            total = total + (e != e).astype(jnp.int32)
         return total
 
-    def swap_core(a):
-        return lax.ppermute(a, "mp", cores)
-
-    def gather8(own):
-        mine = jnp.concatenate([own] + [flip(own, d) for d in range(1, G)], axis=0)
-        return jnp.concatenate([mine, swap_core(mine)], axis=0)
-
-    def scatter8(make, own_rows):
-        other = make(1).astype(BF)
-        arrived = swap_core(other)
-        mine = make(0) + arrived.astype(F32)
-        pieces = [mine[d * own_rows : (d + 1) * own_rows] for d in range(G)]
-        total = pieces[0]
-        for d in range(1, G):
-            total = total + flip(pieces[d].astype(BF), d).astype(F32)
-        return total
+    def zero(*earlier):
+        return index_zero(*earlier).astype(F32)
 
     def body(
         inputs,
@@ -393,56 +371,70 @@
         dp = lax.axis_index("dp")
         mp = lax.axis_index("mp")
         g = dp % G
-        z = dp // G
         micro, _, row, width = inputs.shape
         depth = width // n
         ch = w_branch.shape[1] // G
         ff = w_gate.shape[1] // G
         heads = w_decay.shape[0] // G
         taps = conv_w.shape[0]
-
-        def own_part(a):
-            return lax.dynamic_index_in_dim(a, mp, 0, keepdims=False)[0]
-
-        x_own = own_part(inputs)
-        c_own = own_part(cotangent)
-        x_all = gather8(x_own)
-        seg_all = gather8(own_part(segment_ids)[:, None])[:, 0].reshape(2 * G, row)
-
-        small = jnp.concatenate(
-            [a.reshape(-1) for a in (mixer_gain, mlp_gain, conv_w, gate_bias, decay_param)]
-        )
-        small = jnp.stack(unxor([small] + [flip(small, d) for d in range(1, G)], g))
-        small = gather_far(small, z).reshape(n, -1).astype(F32)
         part = conv_w.shape[1]
+        wide = -(-ch // 128) * 128
+        half = G * row
+
+        def own_part(a, *earlier):
+            return lax.dynamic_index_in_dim(a, mp + index_zero(*earlier), 0, keepdims=False)[0]
+
+        def gather4(own):
+            return spread(own).reshape(half, -1)
+
+        def scatter4(sums):
+            return jnp.sum(trade(sums.reshape(G, row, -1)).astype(F32), axis=0)
+
+        def halves(a):
+            return a[:half], a[half:]
+
+        def token_sum(left, right):
+            return dot(left[0], right[0], 0, 0) + dot(left[1], right[1], 0, 0)
+
+        def scatter_z(grad):
+            return lax.psum_scatter(grad, "dp", scatter_dimension=0, axis_index_groups=lines, tiled=True)
+
+        def gather_z(rows):
+            return lax.all_gather(rows, "dp", axis=0, axis_index_groups=lines, tiled=True)
+
+        def by_column(weights):
+            split = [jnp.swapaxes(w.reshape(depth, G, -1), 0, 1) for w in weights]
+            return jnp.concatenate(split, axis=2)
+
+        small = [a.reshape(-1) for a in (mixer_gain, mlp_gain, conv_w, gate_bias, decay_param)]
+        small = jnp.concatenate(small + [segment_ids.astype(BF).reshape(-1)])
+        small_size = small.shape[0] - micro * row
+        gate_width = w_decay.shape[1]
+        gate_rows = 2 * heads
+        small_rows = -(-small.shape[0] // gate_width)
+        small = jnp.pad(small, (0, small_rows * gate_width - small.shape[0]))
+        pack = [w.reshape(G, heads * gate_width) for w in (w_decay, w_input)]
+        pack = jnp.concatenate(pack + [jnp.broadcast_to(small, (G,) + small.shape)], axis=1)
+        pack_size = pack.shape[1]
+        first = by_column((w_branch, w_recur, w_out.T, w_down.T))
+        columns = first.shape[2]
+        pack_rows = -(-pack_size // columns)
+        pack = jnp.pad(pack, ((0, 0), (0, pack_rows * columns - pack_size)))
+        first = trade(jnp.concatenate([first, pack.reshape(G, pack_rows, columns)], axis=1))
+        mix_rows = first[:, :depth, : 3 * ch].reshape(G * depth, -1)
+        w_down_rows = first[:, :depth, 3 * ch :].reshape(G * depth, -1)
+        pack = first[:, depth:].reshape(G, -1)[:, :pack_size].reshape(G, gate_rows + small_rows, gate_width)
+        seg_rows = pack[:, gate_rows:].reshape(G, -1)[:, small_size : small_size + micro * row]
+        seg_rows = jnp.swapaxes(seg_rows.reshape(G, micro, row), 0, 1)
+        seg_all = jnp.concatenate([pick(seg_rows, mp), pick(seg_rows, 1 - mp)], axis=0)
+        packs = spread(pack, lines).reshape(n, gate_rows + small_rows, gate_width)
+        small = packs[:, gate_rows:].reshape(n, -1)[:, :small_size].astype(F32)
         mixer_gain_f = small[:, :depth].reshape(width)
         mlp_gain_f = small[:, depth : 2 * depth].reshape(width)
         chan = small[:, 2 * depth :].reshape(n, taps + 3, part)
         chan = jnp.transpose(chan, (1, 0, 2)).reshape(taps + 3, n * part)
         chan = lax.dynamic_slice_in_dim(chan, g * ch, ch, 1)
-        wide = -(-ch // 128) * 128
-        sp8 = -8.0 * jax.nn.softplus(-chan[taps + 2 :])
-        par = jnp.concatenate([chan[: taps + 2], sp8], axis=0)
-        par = jnp.pad(par, ((0, 0), (0, wide - ch)), constant_values=((0, 0), (0, -1.0)))
-        par = par * jnp.where((jnp.arange(wide) >= ch) & (jnp.arange(taps + 3) < taps + 2)[:, None], 0.0, 1.0)
-        par_f = jnp.broadcast_to(par[:, None], (taps + 3, ROWS, wide))
-        mask = jnp.transpose(same_masks(seg_all, taps), (0, 2, 1)).reshape(taps - 1, ROWS * row, 1)
-        mask = jnp.broadcast_to(mask, (taps - 1, ROWS * row, 128))
-
-        def fetch(weights):
-            cols = [jnp.split(w, G, axis=1) for w in weights]
-            blocks = [jnp.concatenate([c[j] for c in cols], axis=1) for j in range(G)]
-            sends = unxor(blocks, g)
-            got = [sends[0]] + [flip(sends[d], d) for d in range(1, G)]
-            rows = jnp.concatenate(unxor(got, g), axis=0)
-            return lax.all_gather(rows, "dp", axis=0, axis_index_groups=z_groups, tiled=True)
-
-        w_mix = fetch((w_branch, w_recur))
-        gates = jnp.stack([w_decay, w_input]).reshape(2, G, heads, -1)
-        sends = unxor([gates[:, j] for j in range(G)], g)
-        got = [sends[0]] + [flip(sends[d], d) for d in range(1, G)]
-        gates = jnp.stack(unxor(got, g))
-        gates = gather_far(gates, z).reshape(n, 2, heads, -1)
+        gates = packs[:, :gate_rows].reshape(n, 2, heads, -1)
         gates = jnp.transpose(gates, (1, 2, 0, 3)).reshape(2, heads, BW, BW)
         wg = [
             sum(
@@ -452,47 +444,89 @@
             for q in range(2)
         ]
         wg = jnp.concatenate(wg, axis=1)
+        sp8 = -8.0 * jax.nn.softplus(-chan[taps + 2 :])
+        par = jnp.concatenate(
+            [
+                jnp.pad(chan[: taps + 2], ((0, 0), (0, wide - ch))),
+                jnp.pad(sp8, ((0, 0), (0, wide - ch)), constant_values=-1.0),
+            ],
+            axis=0,
+        )
+        par_f = jnp.broadcast_to(par[:, None], (taps + 3, ROWS, wide))
+        mask = jnp.transpose(same_masks(seg_all, taps), (0, 2, 1)).reshape(taps - 1, ROWS * row, 1)
+        mask = jnp.broadcast_to(mask, (taps - 1, ROWS * row, 128))
+
+        rows = gather_z(mix_rows)
+        w_down_t = gather_z(w_down_rows)
+        x_own_f = own_part(inputs).astype(F32)
+        normed_own = rms_scale(x_own_f, mixer_gain_f)
+        normed_near = gather4(normed_own.astype(BF))
+        normed_mix = [normed_near, swap_core(normed_near)]
+        c_near = gather4(own_part(cotangent, normed_near))
+        c_half = [c_near, swap_core(c_near)]
+        w_in_rows = trade(by_column((w_gate, w_up))).reshape(G * depth, -1)
+        w_in = gather_z(w_in_rows)
         w_mix = jnp.concatenate(
-            [jnp.pad(w, ((0, 0), (0, wide - ch))) for w in (w_mix[:, :ch], w_mix[:, ch:])], axis=1
-        )
-        w_out_t = jnp.pad(fetch((w_out.T,)), ((0, 0), (0, wide - ch)))
-        w_in = fetch((w_gate, w_up))
-        w_down_t = fetch((w_down.T,))
-        c_all = gather8(c_own)
-
-        half = G * row
-        x_float = x_all.astype(F32)
-        normed_mix = rms_scale(x_float, mixer_gain_f).astype(BF)
-        mix = dot(normed_mix, w_mix, 1, 0)
-        mixed, values, pre, h_all = forward_call(mix, mask, par_f, wg)
-        x_own_f = x_own.astype(F32)
-        after_mix = x_own_f + scatter8(
-            lambda h: dot(mixed[h * half : (h + 1) * half], w_out_t, 1, 1), row
-        )
-        normed_own = rms_scale(after_mix, mlp_gain_f).astype(BF)
-        normed_mlp = gather8(normed_own)
-        gate_up = dot(normed_mlp, w_in, 1, 0)
-        gate_pre, up_pre = gate_up[:, :ff], gate_up[:, ff:]
-        hidden = (jax.nn.gelu(gate_pre) * up_pre).astype(BF)
-        result = after_mix + scatter8(
-            lambda h: dot(hidden[h * half : (h + 1) * half], w_down_t, 1, 1), row
-        )
-
-        grad_down = dot(c_all, hidden, 0, 0)
-        grad_hidden = dot(c_all, w_down_t, 1, 0)
-        _, pull = jax.vjp(lambda a, b: jax.nn.gelu(a) * b, gate_pre, up_pre)
-        grad_gate_pre, grad_up_pre = pull(grad_hidden)
-        low = jnp.concatenate([grad_gate_pre.astype(BF), grad_up_pre.astype(BF)], axis=1)
-        grad_in = dot(normed_mlp, low, 0, 0)
-        grad_normed = scatter8(lambda h: dot(low[h * half : (h + 1) * half], w_in, 1, 1), row)
+            [jnp.pad(w, ((0, 0), (0, wide - ch))) for w in (rows[:, :ch], rows[:, ch : 2 * ch])], axis=1
+        ) + zero(w_in_rows).astype(BF)
+        w_out_t = jnp.pad(rows[:, 2 * ch :], ((0, 0), (0, wide - ch)))
+
+        mix = [dot(a, w_mix, 1, 0) for a in normed_mix]
+        mixed, values, pre, h_all = forward_call(*mix, mask, par_f, wg)
+        mixed_near, mixed_far = halves(mixed)
+        c_part = c_near[:, :wide]
+        mixed_far = mixed_far + (c_part != c_part).astype(BF)
+        arrived = swap_core(dot(mixed_far, w_out_t, 1, 1, BF))
+        sums = dot(mixed_near, w_out_t, 1, 1) + arrived.astype(F32)
+        after_mix = x_own_f + scatter4(sums.astype(BF))
+        normed_own = (rms_scale(after_mix, mlp_gain_f) + zero(w_in)).astype(BF)
+        normed_near = gather4(normed_own)
+        normed = [normed_near, swap_core(normed_near + zero(w_down_t).astype(BF))]
+        hidden, gate_up = [], []
+        for a in normed:
+            pre_act = dot(a, w_in, 1, 0)
+            gate_up.append(pre_act)
+            hidden.append((jax.nn.gelu(pre_act[:, :ff]) * pre_act[:, ff:]).astype(BF))
+
+        grad_down = token_sum(c_half, hidden).astype(BF)
+        down_piece = scatter_z(grad_down)
+        low = []
+        for c_part, pre_act in zip(c_half, gate_up):
+            grad_hidden = dot(c_part, w_down_t, 1, 0)
+            _, pull = jax.vjp(lambda a, b: jax.nn.gelu(a) * b, pre_act[:, :ff], pre_act[:, ff:])
+            low.append(jnp.concatenate([(a + zero(grad_down)).astype(BF) for a in pull(grad_hidden)], axis=1))
+        arrived = swap_core(dot(low[1], w_in, 1, 1, BF))
+        sums = (dot(low[0], w_in, 1, 1) + arrived.astype(F32)).astype(BF)
+        low_all = jnp.concatenate([a + zero(sums).astype(BF) for a in low], axis=0)
+        grad_in = dot(jnp.concatenate(normed, axis=0), low_all, 0, 0).astype(BF)
+        in_piece = scatter_z(grad_in)
+        hidden = [a + zero(sums).astype(BF) for a in hidden]
+        arrived = swap_core(dot(hidden[1], w_down_t, 1, 1, BF))
+        result_sums = (dot(hidden[0], w_down_t, 1, 1) + arrived.astype(F32)).astype(BF)
+        grad_normed = scatter4(sums) + zero(grad_in, down_piece, result_sums)
         _, pull = jax.vjp(rms_scale, after_mix, mlp_gain_f)
         grad_after, grad_mlp_gain = pull(grad_normed)
-        grad_after = c_own.astype(F32) + grad_after
-        after_low = gather8(grad_after.astype(BF))
-        grad_out = dot(after_low, mixed, 0, 0)[:, :ch]
-        grad_mixed = dot(after_low, w_out_t, 1, 0)
-
-        mix_low, gate_low, acc = backward_call(mix, grad_mixed, mask, par_f, wg, values, pre, h_all)
+        grad_after = own_part(cotangent).astype(F32) + grad_after
+        after_own = grad_after.astype(BF)
+        after_near = gather4(after_own)
+        after_low = [after_near, swap_core(after_near)]
+        grad_mixed = [dot(a, w_out_t, 1, 0) for a in after_low]
+        grad_out = token_sum(after_low, (mixed_near, mixed_far))
+        grad_out = grad_out[:, :ch].astype(BF)
+
+        out_piece = scatter_z(grad_out)
+        mix_low, gate_low, acc = backward_call(
+            mix, grad_mixed, mask, par_f, wg, values, pre, h_all, grad_out, result_sums
+        )
+        result = after_mix + scatter4(result_sums) + zero(mix_low)
+        low_near, low_far = halves(mix_low)
+        arrived = swap_core(dot(low_far, w_mix, 1, 1, BF))
+        sums = (dot(low_near, w_mix, 1, 1) + arrived.astype(F32) + zero(result)).astype(BF)
+        behind = zero(sums).astype(BF)
+        grad_mix = token_sum(normed_mix, halves(mix_low + behind))
+        gate_low = gate_low + behind
+        grad_mix = jnp.concatenate([grad_mix[:, :ch], grad_mix[:, wide : wide + ch]], axis=1).astype(BF)
+
         grad_gates = dot(values, gate_low, 0, 0)
         grad_gates = jnp.stack(
             [
@@ -501,56 +535,54 @@
                 for h in range(heads)
             ]
         )
+        grad_gates = jnp.swapaxes(grad_gates.reshape(gate_rows, n, gate_width), 0, 1).reshape(n, -1)
         acc = jnp.sum(acc, axis=1)[:, :ch]
         chan_grad = jnp.concatenate(
             [acc[: taps + 2], acc[taps + 2 :] * (8.0 * jax.nn.sigmoid(-chan[taps + 2 :]))], axis=0
         )
-        grad_mix = dot(normed_mix, mix_low, 0, 0)
-        grad_mix = jnp.concatenate([grad_mix[:, :ch], grad_mix[:, wide : wide + ch]], axis=1)
-        grad_normed_mix = scatter8(
-            lambda h: dot(mix_low[h * half : (h + 1) * half], w_mix, 1, 1), row
+        chan_grad = jnp.concatenate([jnp.where(g == j, chan_grad, 0.0) for j in range(G)], axis=1)
+        chan_grad = jnp.transpose(chan_grad.reshape(taps + 3, n, part), (1, 0, 2)).reshape(n, -1)
+        extra = jnp.concatenate([grad_gates, chan_grad, grad_mlp_gain.reshape(n, depth)], axis=1)
+        more = -(-extra.shape[1] // (2 * ch))
+        extra = jnp.pad(extra, ((0, 0), (0, more * 2 * ch - extra.shape[1]))).astype(BF)
+        grad_mix = jnp.concatenate(
+            [grad_mix.reshape(n, depth, -1), extra.reshape(n, more, 2 * ch)], axis=1
         )
+        mix_piece = scatter_z(grad_mix)
+        sums = trade(sums.reshape(G, row, -1))
+        grad_normed_mix = jnp.sum(sums.astype(F32), axis=0) + zero(grad_mix, in_piece, out_piece)
         _, pull = jax.vjp(rms_scale, x_own_f, mixer_gain_f)
         grad_x, grad_mix_gain = pull(grad_normed_mix)
         input_grad_own = grad_after + grad_x
 
-        def give(grad, sizes):
-            piece = lax.psum_scatter(
-                grad.astype(BF), "dp", scatter_dimension=0, axis_index_groups=z_groups, tiled=True
-            )
-            sends = unxor([piece[j * depth : (j + 1) * depth] for j in range(G)], g)
-            got = [sends[0]] + [flip(sends[d], d) for d in range(1, G)]
-            got = [a.astype(F32) for a in unxor(got, g)]
-            outs, at = [], 0
-            for size in sizes:
-                outs.append(jnp.concatenate([a[:, at : at + size] for a in got], axis=1))
-                at += size
-            return outs
-
-        (out_down,) = give(grad_down, (ff,))
-        out_gate, out_up = give(grad_in, (ff, ff))
-        (out_out,) = give(grad_out, (ch,))
-        out_branch, out_recur = give(grad_mix, (ch, ch))
-        flat = jnp.transpose(grad_gates.reshape(2, heads, n, -1), (2, 0, 1, 3))
-        piece = sum_far(flat.reshape((far, G) + flat.shape[1:]), z, lambda v: v.astype(BF)).astype(BF)
-        sends = unxor([piece[j] for j in range(G)], g)
-        got = unxor([sends[0]] + [flip(sends[d], d) for d in range(1, G)], g)
-        got = jnp.concatenate(got, axis=1).astype(F32)
-        out_decay, out_input = got[0], got[1]
-
-        placed = jnp.concatenate([jnp.where(g == j, chan_grad, 0.0) for j in range(G)], axis=1)
-        placed = jnp.transpose(placed.reshape(taps + 3, n, part), (1, 0, 2)).reshape(n, -1)
-        packed = jnp.concatenate(
-            [grad_mix_gain.reshape(n, depth), grad_mlp_gain.reshape(n, depth), placed], axis=1
-        )
-        packed = sum_far(packed.reshape(far, G, -1), z)
-        sends = unxor([packed[j] for j in range(G)], g)
-        packed = sends[0]
-        for d in range(1, G):
-            packed = packed + flip(sends[d], d)
-        gains = packed[: 2 * depth]
-        gains = gains + swap_core(gains)
-        chan_out = packed[2 * depth :].reshape(taps + 3, part)
+        pieces = [p.reshape(G, depth, -1) for p in (down_piece, in_piece, out_piece)]
+        got = trade(jnp.concatenate(pieces, axis=2) + zero(sums).astype(BF))
+        outs = []
+        for at, size in ((0, ff), (ff, ff), (2 * ff, ff), (3 * ff, ch)):
+            outs.append(jnp.swapaxes(got[:, :, at : at + size], 0, 1).reshape(depth, -1).astype(F32))
+        out_down, out_gate, out_up, out_out = outs
+        got = trade(mix_piece)
+        out_branch, out_recur = [
+            jnp.swapaxes(got[:, :depth, at : at + ch], 0, 1).reshape(depth, -1).astype(F32) for at in (0, ch)
+        ]
+        got = got[:, depth:].reshape(G, -1)
+        gate_size = gate_rows * gate_width
+        flat = jnp.swapaxes(got[:, :gate_size].reshape(G, 2, heads, -1), 0, 1)
+        flat = flat.reshape(2, G * heads, -1).astype(F32)
+        got = jnp.sum(got[:, gate_size : gate_size + (taps + 3) * part + depth].astype(F32), axis=0)
+        chan_out = got[: (taps + 3) * part].reshape(taps + 3, part)
+        mlp_gain_out = got[(taps + 3) * part :]
+        mlp_gain_out = mlp_gain_out + swap_core(mlp_gain_out)
+        def sum_flips(a, at, count, step):
+            total = pick(a, at)
+            for k in range(1, count):
+                pairs = [(i, i ^ (k * step)) for i in range(n)]
+                total = total + lax.ppermute(pick(a, at ^ k), "dp", pairs)
+            return total
+
+        mix_gain_out = sum_flips(grad_mix_gain.reshape(far, G, depth), dp // G, far, G)
+        mix_gain_out = sum_flips(mix_gain_out, g, G, 1)
+        mix_gain_out = mix_gain_out + swap_core(mix_gain_out)
 
         def both_rows(own):
             other = swap_core(own)
@@ -561,13 +593,13 @@
         return (
             both_rows(result),
             both_rows(input_grad_own),
-            gains[:depth],
-            gains[depth:],
+            mix_gain_out,
+            mlp_gain_out,
             out_branch,
             out_recur,
             chan_out[:taps],
-            out_decay,
-            out_input,
+            flat[0],
+            flat[1],
             chan_out[taps : taps + 2],
             chan_out[taps + 2],
             out_out.T,

time: 911 us -> 774 us (0.85)
  waiting for transfers between devices: 375 us -> 250 us
  starting transfers between devices: 136 us -> 76.9 us
  blocking collectives: 0 us -> 27 us
  between operations: 15.6 us -> 38.5 us
  other arithmetic: 78.8 us -> 65 us
    ppermute x75 -> x6, waiting for transfers between devices: 339 us -> 12.8 us  [sum_flips(): total = total + lax.ppermute(pick(a, at ^ k), 'dp', pairs)]
    all_to_all x0 -> x12, waiting for transfers between devices: none -> 153 us  [trade(): return lax.all_to_all(a, 'dp', 0, 0, axis_index_groups=groups, tiled=True)]
    ppermute x75 -> x6, starting transfers between devices: 83.9 us -> 7.53 us  [sum_flips(): total = total + lax.ppermute(pick(a, at ^ k), 'dp', pairs)]
    all_to_all x0 -> x12, starting transfers between devices: none -> 56.7 us  [trade(): return lax.all_to_all(a, 'dp', 0, 0, axis_index_groups=groups, tiled=True)]
    ppermute x12, starting transfers between devices: 51.7 us -> 12 us  [swap_core(): return lax.ppermute(a, 'mp', cores)]
    all_gather x4 -> x3, waiting for transfers between devices: 35.3 us -> 74.5 us  [gather_z(): lax.all_gather(rows, 'dp', axis=0, axis_index_groups=lines, tiled=True)]
    all_to_all x0 -> x1, blocking collectives: none -> 27 us  [trade(): return lax.all_to_all(a, 'dp', 0, 0, axis_index_groups=groups, tiled=True)]
    add x3 -> x10, other arithmetic: 0.02 us -> 14.5 us  [the longest x1 3.91 us: body(): grad_mix = token_sum(normed_mix, halves(mix_low + behind))]
  transfers between devices with their start and end apart: 95 -> 37, of which waited for: 36 -> 18; matrix products, arithmetic and copies ran while one was open for 32% -> 33% of each run, Pallas kernels for 5% -> 6%
where the time goes in v2:
time: 774 us; the launch traced here: 766 us
  waiting for transfers between devices  250 us (32%)
  matrix products  174 us (22%)
  local copies, waits for them, and re-layouts  89.1 us (12%)
  starting transfers between devices  76.9 us (10%)
  other arithmetic  65 us (8%)
  Pallas kernels  45.4 us (6%)
  between operations  38.5 us (5%)
  blocking collectives  27 us (3%)
    dot_general x24, matrix products, dot(): lax.dot_general(a, b, (((ca,), (cb,)), ((), ())), preferred_element_type=...  174 us
    all_to_all x12, waiting for transfers between devices, trade(): return lax.all_to_all(a, 'dp', 0, 0, axis_index_groups=groups, tiled=True)  153 us
    all_gather x3, waiting for transfers between devices, gather_z(): lax.all_gather(rows, 'dp', axis=0, axis_index_groups=lines, tiled=True)  74.5 us
    all_to_all x12, starting transfers between devices, trade(): return lax.all_to_all(a, 'dp', 0, 0, axis_index_groups=groups, tiled=True)  56.7 us
    pallas_call x1, Pallas kernels, backward_call(): pl.pallas_call(functools.partial(backward_kernel, cp, row, unroll, len(ea...  27.5 us
    all_to_all x1, blocking collectives, trade(): return lax.all_to_all(a, 'dp', 0, 0, axis_index_groups=groups, tiled=True)  27 us
    unnamed x130, local copies, waits for them, and re-layouts  24.2 us
    pallas_call x1, Pallas kernels, forward_call(): pl.pallas_call(functools.partial(forward_kernel, cp, row, unroll, len(ear...  17.9 us
  transfers between devices with their start and end apart: 37, of which 18 were waited for; matrix products, arithmetic and copies ran while one was open for 33% of the time, Pallas kernels for 6%

profile of v2, /device:TPU:1, one launch (start us, length us, event | category | flops | bytes accessed | tf_op | source)
XLA Modules:
  0.0 765.8 jit_solution(4117610733217714349)
XLA Ops:
  22.8 27.0 %all_to_all.65 = bf16[4,133,1728]{2,1,0:T(8,128)(2,1)S(1)} all-to-all(bf16[4,133,1728]{2,1,0:T(8,128)(2,1)} %copy.145), channel_id=1, replica_groups={{0,2,4,6},{8,10,12,14},{16,18,20,22},{24,26,28,30},{1,3,5,7},{9,11,13,1..., dimensions={0} | all-to-all | bytes 3677184 | tf_op jit(solution)/shard_map/all_to_all | solution.py:332
  73.2 44.8 %all-to-all-done.2 = bf16[4,256,2048]{2,1,0:T(8,128)(2,1)} async-done(((bf16[4,256,2048]{2,1,0:T(8,128)(2,1)}), bf16[4,256,2048]{2,1,0:T(8,128)(2,1)}, u32[]{:S(2)}, u32[]{:S(2)}) %all-to-all-start.2) | async-done | bytes 4194336 | tf_op jit(solution)/shard_map/all_to_all | solution.py:332
  123.2 17.0 %all-to-all-done.3 = bf16[4,128,1536]{1,2,0:T(8,128)(2,1)S(1)} async-done(((bf16[4,128,1536]{1,2,0:T(8,128)(2,1)}), bf16[4,128,1536]{1,2,0:T(8,128)(2,1)S(1)}, u32[]{:S(2)}, u32[]{:S(2)}) %all-to-all-start.3) | async-done | bytes 1572896 | tf_op jit(solution)/shard_map/all_to_all | solution.py:332
  160.5 8.4 %fusion.123.near_hbm.mix_near = f32[1024,768]{1,0:T(8,128)} fusion(bf16[1024,2048]{1,0:T(8,128)(2,1)} %bitcast.14, bf16[2048,320]{0,1:T(8,128)(2,1)S(1)} %get-tuple-element.103, bf16[2048,384]{0,1:T(8,128)(2,1)S(1)} %slice_select_fusion, bf16[]{:T(256)} %bitcast.21), kind=kOutput, calls=%fused_computation.227 | convolution fusion | flops 3233808384 | bytes 10223618 | tf_op jit(solution)/shard_map/dot_general | solution.py:322
  168.9 7.4 fusion.121.far_hbm.mix_far
  179.1 17.9 %recur_forward.1 = (bf16[2048,384]{1,0:T(8,128)(2,1)}, bf16[2048,384]{1,0:T(8,128)(2,1)}, f32[6,2112,128]{2,1,0:T(8,128)}, f32[3,2112,128]{2,1,0:T(8,128)}) custom-call(f32[1024,768]{1,0:T(8,128)} %fusion.123.near_hbm.mix_near, f32[1024,768]{1,0:T(8,128)} %fusion.121.far_hbm.mix_far, f32[3,2048,128]{2,1,0:T(8,128)} %broadcast_in_dim.62.mask_ref, ...), custom_call_target="tpu_custom_call" | custom-call | flops 117964800 | bytes 66060288 | tf_op jit(solution)/shard_map/recur_forward/pallas_call | solution.py:125
  207.6 6.8 collective-permute-done.1
  226.3 33.8 %all-gather.6.cloned.1.call-done = bf16[2048,1536]{1,0:T(8,128)(2,1)} async-done(((bf16[512,1536]{1,0:T(8,128)(2,1)}), bf16[2048,1536]{1,0:T(8,128)(2,1)}) %all-gather.6.cloned.1.call-update) | async-done | bytes 6291472 | tf_op jit(solution)/shard_map/all_gather | solution.py:403
  262.5 8.3 %all-to-all-done.5 = bf16[4,256,2048]{2,1,0:T(8,128)(2,1)} async-done(((bf16[4,256,2048]{2,1,0:T(8,128)(2,1)}), bf16[4,256,2048]{2,1,0:T(8,128)(2,1)}, u32[]{:S(2)}, u32[]{:S(2)}) %all-to-all-start.5) | async-done | bytes 4194336 | tf_op jit(solution)/shard_map/all_to_all | solution.py:332
  282.4 40.7 %all-gather.8.cloned.1.call-done = bf16[2048,768]{1,0:T(8,128)(2,1)} async-done(((bf16[512,768]{1,0:T(8,128)(2,1)}), bf16[2048,768]{1,0:T(8,128)(2,1)}) %all-gather.8.cloned.1.call-update) | async-done | bytes 3145744 | tf_op jit(solution)/shard_map/all_gather | solution.py:403
  333.3 10.2 %fusion.130 = f32[1024,1536]{1,0:T(8,128)S(1)} fusion(bf16[1024,2048]{1,0:T(8,128)(2,1)} %bitcast.43, bf16[2048,1536]{1,0:T(8,128)(2,1)} %all-gather.6.cloned.1.call-done), kind=kOutput, calls=%fused_computation.233 | convolution fusion | flops 6442450944 | bytes 16777216 | tf_op jit(solution)/shard_map/dot_general | solution.py:322
  346.7 6.4 fusion.131
  353.1 6.6 fusion.132
  373.5 10.4 %fusion.26 = (bf16[1024,768]{1,0:T(8,128)(2,1)S(1)}, bf16[1024,768]{1,0:T(8,128)(2,1)S(1)}) fusion(f32[1024,1536]{1,0:T(8,128)} %copy-done.11, f32[]{:T(128)} %bitcast.46, bf16[1024,2048]{1,0:T(8,128)(2,1)} %copy-done.49, bf16[2048,768]{1,0:T(8,128)(2,1)} %all-gather.8.cloned.1.call-done), kind=kOutput, calls=%fused_computation.47 | convolution fusion | flops 3241672704 | bytes 16777220 | tf_op jit(solution)/shard_map/dot_general | solution.py:322
  383.9 12.6 %fusion.41 = bf16[1024,2048]{1,0:T(8,128)(2,1)} fusion(bf16[2048,1536]{1,0:T(8,128)(2,1)} %all-gather.6.cloned.1.call-done, bf16[1024,768]{1,0:T(8,128)(2,1)S(1)} %get-tuple-element.98, bf16[1024,768]{1,0:T(8,128)(2,1)S(1)} %get-tuple-element.97), kind=kOutput, calls=%fused_computation.85 | convolution fusion | flops 6448742400 | bytes 13631488 | tf_op jit(solution)/shard_map/dot_general | solution.py:322
  397.0 10.4 %fusion.18 = (bf16[1024,768]{1,0:T(8,128)(2,1)S(1)}, bf16[1024,768]{1,0:T(8,128)(2,1)S(1)}) fusion(f32[1024,1536]{1,0:T(8,128)} %copy-done.10, f32[]{:T(128)} %bitcast.46, bf16[1024,2048]{1,0:T(8,128)(2,1)} %bitcast.39, bf16[2048,768]{1,0:T(8,128)(2,1)} %all-gather.8.cloned.1.call-done), kind=kOutput, calls=%fused_computation.39 | convolution fusion | flops 3241672704 | bytes 16777220 | tf_op jit(solution)/shard_map/dot_general | solution.py:322
  407.4 11.6 %add_convert_fusion.2 = bf16[1024,2048]{1,0:T(8,128)(2,1)S(1)} fusion(bf16[1024,2048]{1,0:T(8,128)(2,1)} %collective-permute-done.4, bf16[2048,1536]{1,0:T(8,128)(2,1)} %all-gather.6.cloned.1.call-done, bf16[1024,768]{1,0:T(8,128)(2,1)S(1)} %get-tuple-element.96, bf16[1024,768]{1,0:T(8,128)(2,1)S(1)} %get-tuple-element.95), kind=kOutput, calls=%fused_computation.9 | convolution fusion | flops 6455033856 | bytes 17825792 | tf_op jit(solution)/shard_map/dot_general | solution.py:322
  436.1 16.4 %fusion.4 = bf16[2048,1536]{1,0:T(8,128)(2,1)} fusion(bf16[1024,2048]{1,0:T(8,128)(2,1)S(1)} %copy-done.48, bf16[1024,2048]{1,0:T(8,128)(2,1)} %bitcast.43, bf16[1024,1536]{1,0:T(8,128)(2,1)S(1)} %fusion.40, bf16[1024,1536]{1,0:T(8,128)(2,1)S(1)} %fusion.42), kind=kOutput, calls=%fused_computation.12 | convolution fusion | flops 12917407744 | bytes 20971520 | tf_op jit(solution)/shard_map/dot_general | solution.py:322
  459.8 18.2 %all-to-all-done.8 = bf16[4,256,2048]{2,1,0:T(8,128)(2,1)} async-done(((bf16[4,256,2048]{2,1,0:T(8,128)(2,1)}), bf16[4,256,2048]{2,1,0:T(8,128)(2,1)}, u32[]{:S(2)}, u32[]{:S(2)}) %all-to-all-start.8) | async-done | bytes 4194336 | tf_op jit(solution)/shard_map/all_to_all | solution.py:332
  500.3 46.3 %all-to-all-done.9 = bf16[4,256,2048]{2,1,0:T(8,128)(2,1)} async-done(((bf16[4,256,2048]{2,1,0:T(8,128)(2,1)}), bf16[4,256,2048]{2,1,0:T(8,128)(2,1)}, u32[]{:S(2)}, u32[]{:S(2)}) %all-to-all-start.9) | async-done | bytes 4194336 | tf_op jit(solution)/shard_map/all_to_all | solution.py:332
  575.8 27.5 %recur_backward.1 = (bf16[2048,768]{1,0:T(8,128)(2,1)}, bf16[2048,768]{1,0:T(8,128)(2,1)}, f32[7,8,384]{2,1,0:T(8,128)}) custom-call(f32[1024,768]{1,0:T(8,128)} %fusion.123.near_hbm.mix_near, f32[1024,768]{1,0:T(8,128)} %fusion.121.far_hbm.mix_far, f32[1024,384]{1,0:T(8,128)} %fusion.62.gm_near, f32[1024,384]{1,0:T(8,128)} %fusion.60.gm_far, ...), custom_call_target="tpu_custom_call" | custom-call | flops 157286400 | bytes 100663296 | tf_op jit(solution)/shard_map/recur_backward/pallas_call | solution.py:284
  603.3 7.3 fusion.48
  621.3 6.6 add_convert_fusion
  711.0 11.8 %collective-permute-done.13 = f32[128]{0:T(128)S(1)} collective-permute-done((f32[128]{0:T(128)S(1)}, f32[128]{0:T(128)S(1)}, u32[]{:S(2)}, u32[]{:S(2)}) %collective-permute-start.13) | collective-permute-done | bytes 544 | tf_op jit(solution)/shard_map/ppermute | solution.py:580
  (372 shorter events, 313.0 us)
Async XLA Ops:
  57.0 99.4 %all-gather.4.cloned.1.call-start = ((), (), s32[]{:S(2)}) async-start(), calls=%async_computation.17 | async-start | bytes 4915200 | tf_op jit(solution)/shard_map/all_gather | solution.py:403
  66.1 51.9 %all-to-all-start.2 = ((bf16[4,256,2048]{2,1,0:T(8,128)(2,1)}), bf16[4,256,2048]{2,1,0:T(8,128)(2,1)}, u32[]{:S(2)}, u32[]{:S(2)}) async-start(bf16[4,256,2048]{2,1,0:T(8,128)(2,1)} %broadcast_in_dim.59), calls=%async_computation.2 | async-start | bytes 8388608 | tf_op jit(solution)/shard_map/all_to_all | solution.py:332
  118.0 22.2 %all-to-all-start.3 = ((bf16[4,128,1536]{1,2,0:T(8,128)(2,1)}), bf16[4,128,1536]{1,2,0:T(8,128)(2,1)S(1)}, u32[]{:S(2)}, u32[]{:S(2)}) async-start(bf16[4,128,1536]{1,2,0:T(8,128)(2,1)} %pad_maximum_fusion.8), calls=%async_computation.3 | async-start | bytes 3145728 | tf_op jit(solution)/shard_map/all_to_all | solution.py:332
  121.6 138.4 %all-gather.6.cloned.1.call-start = ((), (), s32[]{:S(2)}) async-start(), calls=%async_computation.18 | async-start | bytes 7864320 | tf_op jit(solution)/shard_map/all_gather | solution.py:403
  121.6 47.2 %collective-permute-start = (bf16[1024,2048]{1,0:T(8,128)(2,1)}, bf16[1024,2048]{1,0:T(8,128)(2,1)}, u32[]{:S(2)}, u32[]{:S(2)}) collective-permute-start(bf16[1024,2048]{1,0:T(8,128)(2,1)} %bitcast.14), channel_id=1, source_target_pairs={{0,1},{1,0},{2,3},{3,2},{4,5},{5,4},{6,7},{7,6},{8,9},{9,8},{10,11... | collective-permute-start | bytes 12582920 | tf_op jit(solution)/shard_map/ppermute | solution.py:338
  149.7 52.5 %all-to-all-start.4 = ((bf16[4,256,2048]{2,1,0:T(8,128)(2,1)}), bf16[4,256,2048]{2,1,0:T(8,128)(2,1)}, u32[]{:S(2)}, u32[]{:S(2)}) async-start(bf16[4,256,2048]{2,1,0:T(8,128)(2,1)} %broadcast_in_dim.64), calls=%async_computation.4 | async-start | bytes 8388608 | tf_op jit(solution)/shard_map/all_to_all | solution.py:332
  218.8 52.0 %all-to-all-start.5 = ((bf16[4,256,2048]{2,1,0:T(8,128)(2,1)}), bf16[4,256,2048]{2,1,0:T(8,128)(2,1)}, u32[]{:S(2)}, u32[]{:S(2)}) async-start(bf16[4,256,2048]{2,1,0:T(8,128)(2,1)} %bitcast.229), calls=%async_computation.5 | async-start | bytes 8388608 | tf_op jit(solution)/shard_map/all_to_all | solution.py:332
  223.6 99.5 %all-gather.8.cloned.1.call-start = ((), (), s32[]{:S(2)}) async-start(), calls=%async_computation.19 | async-start | bytes 3932160 | tf_op jit(solution)/shard_map/all_gather | solution.py:403
  277.4 51.7 %all-to-all-start.6 = ((bf16[4,256,2048]{2,1,0:T(8,128)(2,1)}), bf16[4,256,2048]{2,1,0:T(8,128)(2,1)}, u32[]{:S(2)}, u32[]{:S(2)}) async-start(bf16[4,256,2048]{2,1,0:T(8,128)(2,1)} %broadcast_in_dim.65), calls=%async_computation.6 | async-start | bytes 8388608 | tf_op jit(solution)/shard_map/all_to_all | solution.py:332
  282.3 175.0 %reduce-scatter.5.cloned.1.call-start = ((), (), s32[]{:S(2)}) async-start(), calls=%async_computation.20 | async-start | bytes 3932160 | tf_op jit(solution)/shard_map/reduce_scatter | solution.py:400
  331.6 21.5 %collective-permute-start.3 = (bf16[1024,2048]{1,0:T(8,128)(2,1)S(1)}, bf16[1024,2048]{1,0:T(8,128)(2,1)S(1)}, u32[]{:S(2)}, u32[]{:S(2)}) collective-permute-start(bf16[1024,2048]{1,0:T(8,128)(2,1)S(1)} %broadcast_add_fusion), channel_id=1, source_target_pairs={{0,1},{1,0},{2,3},{3,2},{4,5},{5,4},{6,7},{7,6},{8,9},{9,8},{10,11... | collective-permute-start | bytes 12582920 | tf_op jit(solution)/shard_map/ppermute | solution.py:338
  333.2 29.2 %collective-permute-start.2 = (bf16[1024,2048]{1,0:T(8,128)(2,1)}, bf16[1024,2048]{1,0:T(8,128)(2,1)S(1)}, u32[]{:S(2)}, u32[]{:S(2)}) collective-permute-start(bf16[1024,2048]{1,0:T(8,128)(2,1)} %bitcast.39), channel_id=1, source_target_pairs={{0,1},{1,0},{2,3},{3,2},{4,5},{5,4},{6,7},{7,6},{8,9},{9,8},{10,11... | collective-permute-start | bytes 12582920 | tf_op jit(solution)/shard_map/ppermute | solution.py:338
  426.0 55.4 %collective-permute-start.5 = (bf16[1024,2048]{1,0:T(8,128)(2,1)}, bf16[1024,2048]{1,0:T(8,128)(2,1)}, u32[]{:S(2)}, u32[]{:S(2)}) collective-permute-start(bf16[1024,2048]{1,0:T(8,128)(2,1)} %fusion.54), channel_id=1, source_target_pairs={{0,1},{1,0},{2,3},{3,2},{4,5},{5,4},{6,7},{7,6},{8,9},{9,8},{10,11... | collective-permute-start | bytes 12582920 | tf_op jit(solution)/shard_map/ppermute | solution.py:338
  426.0 52.0 %all-to-all-start.8 = ((bf16[4,256,2048]{2,1,0:T(8,128)(2,1)}), bf16[4,256,2048]{2,1,0:T(8,128)(2,1)}, u32[]{:S(2)}, u32[]{:S(2)}) async-start(bf16[4,256,2048]{2,1,0:T(8,128)(2,1)} %bitcast.228), calls=%async_computation.8 | async-start | bytes 8388608 | tf_op jit(solution)/shard_map/all_to_all | solution.py:332
  494.8 51.7 %all-to-all-start.9 = ((bf16[4,256,2048]{2,1,0:T(8,128)(2,1)}), bf16[4,256,2048]{2,1,0:T(8,128)(2,1)}, u32[]{:S(2)}, u32[]{:S(2)}) async-start(bf16[4,256,2048]{2,1,0:T(8,128)(2,1)} %broadcast_in_dim.67), calls=%async_computation.10 | async-start | bytes 8388608 | tf_op jit(solution)/shard_map/all_to_all | solution.py:332
  499.7 169.4 %reduce-scatter.7.cloned.1.call-start = ((), (), s32[]{:S(2)}) async-start(), calls=%async_computation.21 | async-start | bytes 7864320 | tf_op jit(solution)/shard_map/reduce_scatter | solution.py:400
  546.5 17.3 %collective-permute-start.6 = (bf16[1024,2048]{1,0:T(8,128)(2,1)}, bf16[1024,2048]{1,0:T(8,128)(2,1)}, u32[]{:S(2)}, u32[]{:S(2)}) collective-permute-start(bf16[1024,2048]{1,0:T(8,128)(2,1)} %bitcast.52), channel_id=1, source_target_pairs={{0,1},{1,0},{2,3},{3,2},{4,5},{5,4},{6,7},{7,6},{8,9},{9,8},{10,11... | collective-permute-start | bytes 12582920 | tf_op jit(solution)/shard_map/ppermute | solution.py:338
  548.0 62.6 %all-to-all-start.7 = ((bf16[4,256,2048]{2,1,0:T(8,128)(2,1)}), bf16[4,256,2048]{2,1,0:T(8,128)(2,1)}, u32[]{:S(2)}, u32[]{:S(2)}) async-start(bf16[4,256,2048]{2,1,0:T(8,128)(2,1)} %bitcast.219), calls=%async_computation.7 | async-start | bytes 8388608 | tf_op jit(solution)/shard_map/all_to_all | solution.py:332
  553.1 121.1 %reduce-scatter.9.cloned.1.call-start = ((), (), s32[]{:S(2)}) async-start(), calls=%async_computation.22 | async-start | bytes 1966080 | tf_op jit(solution)/shard_map/reduce_scatter | solution.py:400
  629.9 52.0 %all-to-all-start.10 = ((bf16[4,256,2048]{2,1,0:T(8,128)(2,1)}), bf16[4,256,2048]{2,1,0:T(8,128)(2,1)}, u32[]{:S(2)}, u32[]{:S(2)}) async-start(bf16[4,256,2048]{2,1,0:T(8,128)(2,1)} %bitcast.227), calls=%async_computation.11 | async-start | bytes 8388608 | tf_op jit(solution)/shard_map/all_to_all | solution.py:332
  634.8 102.0 %reduce-scatter.11.cloned.1.call-start = ((), (), s32[]{:S(2)}) async-start(), calls=%async_computation.23 | async-start | bytes 3686400 | tf_op jit(solution)/shard_map/reduce_scatter | solution.py:400
  668.5 40.6 %collective-permute-start.7 = (f32[256,2048]{1,0:T(8,128)}, f32[256,2048]{1,0:T(8,128)}, u32[]{:S(2)}, u32[]{:S(2)}) collective-permute-start(f32[256,2048]{1,0:T(8,128)} %copy-done.6), channel_id=1, source_target_pairs={{0,1},{1,0},{2,3},{3,2},{4,5},{5,4},{6,7},{7,6},{8,9},{9,8},{10,11... | collective-permute-start | bytes 6291464 | tf_op jit(solution)/shard_map/ppermute | solution.py:338
  687.9 40.7 %all-to-all-start.12 = ((bf16[4,128,2624]{1,2,0:T(8,128)(2,1)}), bf16[4,128,2624]{1,2,0:T(8,128)(2,1)}, u32[]{:S(2)}, u32[]{:S(2)}) async-start(bf16[4,128,2624]{1,2,0:T(8,128)(2,1)} %maximum_add_fusion), calls=%async_computation.16 | async-start | bytes 5373952 | tf_op jit(solution)/shard_map/all_to_all | solution.py:332
  704.2 36.1 %collective-permute-start.9 = (f32[256,2048]{1,0:T(8,128)}, f32[256,2048]{1,0:T(8,128)}, u32[]{:S(2)}, u32[]{:S(2)}) collective-permute-start(f32[256,2048]{1,0:T(8,128)} %fusion.37), channel_id=1, source_target_pairs={{0,1},{1,0},{2,3},{3,2},{4,5},{5,4},{6,7},{7,6},{8,9},{9,8},{10,11... | collective-permute-start | bytes 6291464 | tf_op jit(solution)/shard_map/ppermute | solution.py:338
  (71 other events, 561.8 us)
Sparse Core Ops, SparseCore 0:
  60.0 78.0 all-gather.3
  143.0 117.0 all-gather.5
  261.6 61.4 all-gather.7
  397.1 60.1 reduce-scatter.4
  502.5 113.5 reduce-scatter.6
  620.1 36.8 reduce-scatter.8
  667.0 59.2 reduce-scatter.10

commit v3 on v2

--- a/solution.py
+++ b/solution.py
@@ -138,7 +138,7 @@
             pltpu.VMEM((2 * lanes, tokens + ROWS * PAD, 128), F32),
             pltpu.SemaphoreType.DMA((2 * lanes, ROWS)),
         ],
-        compiler_params=pltpu.CompilerParams(vmem_limit_bytes=60 * 1024 * 1024),
+        compiler_params=pltpu.CompilerParams(vmem_limit_bytes=36 * 1024 * 1024),
         cost_estimate=pl.CostEstimate(flops=150 * tokens * cp, bytes_accessed=84 * tokens * cp, transcendentals=6 * tokens * cp),
         name="recur_forward",
     )(near, far, mask, par, wg, *earlier)
@@ -299,7 +299,7 @@
             slab,
             pltpu.SemaphoreType.DMA((3, lanes, ROWS)),
         ],
-        compiler_params=pltpu.CompilerParams(vmem_limit_bytes=60 * 1024 * 1024),
+        compiler_params=pltpu.CompilerParams(vmem_limit_bytes=48 * 1024 * 1024),
         cost_estimate=pl.CostEstimate(flops=200 * tokens * cp, bytes_accessed=128 * tokens * cp, transcendentals=6 * tokens * cp),
         name="recur_backward",
     )(*mix, *gm, mask, par, wg, values, pre, h, *earlier)
@@ -416,13 +416,12 @@
         pack = [w.reshape(G, heads * gate_width) for w in (w_decay, w_input)]
         pack = jnp.concatenate(pack + [jnp.broadcast_to(small, (G,) + small.shape)], axis=1)
         pack_size = pack.shape[1]
-        first = by_column((w_branch, w_recur, w_out.T, w_down.T))
+        first = by_column((w_branch, w_recur, w_out.T))
         columns = first.shape[2]
         pack_rows = -(-pack_size // columns)
         pack = jnp.pad(pack, ((0, 0), (0, pack_rows * columns - pack_size)))
         first = trade(jnp.concatenate([first, pack.reshape(G, pack_rows, columns)], axis=1))
-        mix_rows = first[:, :depth, : 3 * ch].reshape(G * depth, -1)
-        w_down_rows = first[:, :depth, 3 * ch :].reshape(G * depth, -1)
+        mix_rows = first[:, :depth].reshape(G * depth, -1)
         pack = first[:, depth:].reshape(G, -1)[:, :pack_size].reshape(G, gate_rows + small_rows, gate_width)
         seg_rows = pack[:, gate_rows:].reshape(G, -1)[:, small_size : small_size + micro * row]
         seg_rows = jnp.swapaxes(seg_rows.reshape(G, micro, row), 0, 1)
@@ -457,14 +456,15 @@
         mask = jnp.broadcast_to(mask, (taps - 1, ROWS * row, 128))
 
         rows = gather_z(mix_rows)
-        w_down_t = gather_z(w_down_rows)
         x_own_f = own_part(inputs).astype(F32)
         normed_own = rms_scale(x_own_f, mixer_gain_f)
         normed_near = gather4(normed_own.astype(BF))
         normed_mix = [normed_near, swap_core(normed_near)]
-        c_near = gather4(own_part(cotangent, normed_near))
+        w_in_rows = trade(by_column((w_gate, w_up))).reshape(G * depth, -1)
+        w_down_rows = trade(by_column((w_down.T,))).reshape(G * depth, -1)
+        w_down_t = gather_z(w_down_rows)
+        c_near = gather4(own_part(cotangent, normed_near, w_down_rows))
         c_half = [c_near, swap_core(c_near)]
-        w_in_rows = trade(by_column((w_gate, w_up))).reshape(G * depth, -1)
         w_in = gather_z(w_in_rows)
         w_mix = jnp.concatenate(
             [jnp.pad(w, ((0, 0), (0, wide - ch))) for w in (rows[:, :ch], rows[:, ch : 2 * ch])], axis=1
@@ -523,7 +523,9 @@
         arrived = swap_core(dot(low_far, w_mix, 1, 1, BF))
         sums = (dot(low_near, w_mix, 1, 1) + arrived.astype(F32) + zero(result)).astype(BF)
         behind = zero(sums).astype(BF)
-        grad_mix = token_sum(normed_mix, halves(mix_low + behind))
+        first_sums = sums[:, : 2 * wide]
+        nothing = (first_sums != first_sums).astype(BF)
+        grad_mix = token_sum(normed_mix, (low_near + nothing, low_far + nothing))
         gate_low = gate_low + behind
         grad_mix = jnp.concatenate([grad_mix[:, :ch], grad_mix[:, wide : wide + ch]], axis=1).astype(BF)
 

time: 774 us -> 775 us (level)
  blocking collectives: 27 us -> 65.7 us
  waiting for transfers between devices: 250 us -> 225 us
  other arithmetic: 65 us -> 56.5 us
  Pallas kernels: 45.4 us -> 37.6 us
    all_to_all x12, waiting for transfers between devices: 153 us -> 101 us  [trade(): return lax.all_to_all(a, 'dp', 0, 0, axis_index_groups=groups, tiled=True)]
    all_to_all x1 -> x2, blocking collectives: 27 us -> 65.7 us  [trade(): return lax.all_to_all(a, 'dp', 0, 0, axis_index_groups=groups, tiled=True)]
    all_gather x3, waiting for transfers between devices: 74.5 us -> 104 us  [gather_z(): lax.all_gather(rows, 'dp', axis=0, axis_index_groups=lines, tiled=True)]
    unnamed x130 -> x162, local copies, waits for them, and re-layouts: 24.2 us -> 35.9 us
    slice x16 -> x17, local copies, waits for them, and re-layouts: 15.6 us -> 17.4 us  [index_zero(): e = a[(0,) * a.ndim]]
  transfers between devices with their start and end apart: 37 -> 37, of which waited for: 18 -> 15; matrix products, arithmetic and copies ran while one was open for 33% -> 31% of each run, Pallas kernels for 6% -> 5%
where the time goes in v3:
time: 775 us; the launch traced here: 767 us
  waiting for transfers between devices  225 us (29%)
  matrix products  171 us (22%)
  local copies, waits for them, and re-layouts  94.1 us (12%)
  starting transfers between devices  76.5 us (10%)
  blocking collectives  65.7 us (8%)
  other arithmetic  56.5 us (7%)
  between operations  40.2 us (5%)
  Pallas kernels  37.6 us (5%)
    dot_general x24, matrix products, dot(): lax.dot_general(a, b, (((ca,), (cb,)), ((), ())), preferred_element_type=...  171 us
    all_gather x3, waiting for transfers between devices, gather_z(): lax.all_gather(rows, 'dp', axis=0, axis_index_groups=lines, tiled=True)  104 us
    all_to_all x12, waiting for transfers between devices, trade(): return lax.all_to_all(a, 'dp', 0, 0, axis_index_groups=groups, tiled=True)  101 us
    all_to_all x2, blocking collectives, trade(): return lax.all_to_all(a, 'dp', 0, 0, axis_index_groups=groups, tiled=True)  65.7 us
    all_to_all x12, starting transfers between devices, trade(): return lax.all_to_all(a, 'dp', 0, 0, axis_index_groups=groups, tiled=True)  54.1 us
    unnamed x162, local copies, waits for them, and re-layouts  35.9 us
    pallas_call x1, Pallas kernels, backward_call(): pl.pallas_call(functools.partial(backward_kernel, cp, row, unroll, len(ea...  25.3 us
    slice x17, local copies, waits for them, and re-layouts, index_zero(): e = a[(0,) * a.ndim]  17.4 us
  transfers between devices with their start and end apart: 37, of which 15 were waited for; matrix products, arithmetic and copies ran while one was open for 31% of the time, Pallas kernels for 5%

profile of v3, /device:TPU:1, one launch (start us, length us, event | category | flops | bytes accessed | tf_op | source)
XLA Modules:
  0.0 767.3 jit_solution(9920792163213772104)
XLA Ops:
  19.9 18.3 %all_to_all.70 = bf16[4,137,960]{2,1,0:T(8,128)(2,1)S(1)} all-to-all(bf16[4,137,960]{2,1,0:T(8,128)(2,1)S(1)} %copy.146), channel_id=1, replica_groups={{0,2,4,6},{8,10,12,14},{16,18,20,22},{24,26,28,30},{1,3,5,7},{9,11,13,1..., dimensions={0} | all-to-all | bytes 2104320 | tf_op jit(solution)/shard_map/all_to_all | solution.py:332
  51.9 47.3 %all_to_all.71 = bf16[4,256,2048]{2,1,0:T(8,128)(2,1)} all-to-all(bf16[4,256,2048]{2,1,0:T(8,128)(2,1)S(1)} %broadcast_in_dim.59), channel_id=1, replica_groups={{0,2,4,6},{8,10,12,14},{16,18,20,22},{24,26,28,30},{1,3,5,7},{9,11,13,1..., dimensions={0} | all-to-all | bytes 8388608 | tf_op jit(solution)/shard_map/all_to_all | solution.py:332
  122.8 9.1 %all-to-all-done.3 = bf16[4,128,1536]{1,2,0:T(8,128)(2,1)S(1)} async-done(((bf16[4,128,1536]{1,2,0:T(8,128)(2,1)}), bf16[4,128,1536]{1,2,0:T(8,128)(2,1)S(1)}, u32[]{:S(2)}, u32[]{:S(2)}) %all-to-all-start.3) | async-done | bytes 1572896 | tf_op jit(solution)/shard_map/all_to_all | solution.py:332
  152.9 7.1 fusion.123.far_hbm.mix_far
  161.7 12.3 %recur_forward.1 = (bf16[2048,384]{1,0:T(8,128)(2,1)S(1)}, bf16[2048,384]{1,0:T(8,128)(2,1)S(1)}, f32[6,2112,128]{2,1,0:T(8,128)}, f32[3,2112,128]{2,1,0:T(8,128)S(1)}) custom-call(f32[1024,768]{1,0:T(8,128)S(1)} %fusion.125.near_hbm.mix_near, f32[1024,768]{1,0:T(8,128)S(1)} %fusion.123.far_hbm.mix_far, f32[3,2048,128]{2,1,0:T(8,128)S(1)} %broadcast_in_dim.62.mask_ref, ...), custom_call_target="tpu_custom_call" | custom-call | flops 117964800 | bytes 66060288 | tf_op jit(solution)/shard_map/recur_forward/pallas_call | solution.py:125
  179.1 7.2 all-to-all-done.5
  191.7 6.8 collective-permute-done.1
  208.5 55.5 %all-gather.6.cloned.1.call-done = bf16[2048,1536]{1,0:T(8,128)(2,1)} async-done(((bf16[512,1536]{1,0:T(8,128)(2,1)}), bf16[2048,1536]{1,0:T(8,128)(2,1)}) %all-gather.6.cloned.1.call-update) | async-done | bytes 6291472 | tf_op jit(solution)/shard_map/all_gather | solution.py:403
  279.3 48.3 %all-gather.8.cloned.1.call-done = bf16[2048,768]{1,0:T(8,128)(2,1)} async-done(((bf16[512,768]{1,0:T(8,128)(2,1)}), bf16[2048,768]{1,0:T(8,128)(2,1)}) %all-gather.8.cloned.1.call-update) | async-done | bytes 3145744 | tf_op jit(solution)/shard_map/all_gather | solution.py:403
  333.4 10.5 %fusion.132 = f32[1024,1536]{1,0:T(8,128)S(1)} fusion(bf16[1024,2048]{1,0:T(8,128)(2,1)} %bitcast.44, bf16[2048,1536]{1,0:T(8,128)(2,1)} %all-gather.6.cloned.1.call-done), kind=kOutput, calls=%fused_computation.235 | convolution fusion | flops 6442450944 | bytes 16777216 | tf_op jit(solution)/shard_map/dot_general | solution.py:322
  353.5 6.6 fusion.134
  373.8 10.4 %fusion.26 = (bf16[1024,768]{1,0:T(8,128)(2,1)S(1)}, bf16[1024,768]{1,0:T(8,128)(2,1)S(1)}) fusion(f32[1024,1536]{1,0:T(8,128)} %copy-done.22, f32[]{:T(128)} %bitcast.46, bf16[1024,2048]{1,0:T(8,128)(2,1)} %copy-done.67, bf16[2048,768]{1,0:T(8,128)(2,1)} %all-gather.8.cloned.1.call-done), kind=kOutput, calls=%fused_computation.46 | convolution fusion | flops 3241672704 | bytes 16777220 | tf_op jit(solution)/shard_map/dot_general | solution.py:322
  384.2 12.3 %fusion.41 = bf16[1024,2048]{1,0:T(8,128)(2,1)} fusion(bf16[2048,1536]{1,0:T(8,128)(2,1)} %all-gather.6.cloned.1.call-done, bf16[1024,768]{1,0:T(8,128)(2,1)S(1)} %get-tuple-element.98, bf16[1024,768]{1,0:T(8,128)(2,1)S(1)} %get-tuple-element.97), kind=kOutput, calls=%fused_computation.85 | convolution fusion | flops 6448742400 | bytes 13631488 | tf_op jit(solution)/shard_map/dot_general | solution.py:322
  397.1 10.5 %fusion.18 = (bf16[1024,768]{1,0:T(8,128)(2,1)S(1)}, bf16[1024,768]{1,0:T(8,128)(2,1)S(1)}) fusion(f32[1024,1536]{1,0:T(8,128)} %copy-done.21, f32[]{:T(128)} %bitcast.46, bf16[1024,2048]{1,0:T(8,128)(2,1)} %bitcast.40, bf16[2048,768]{1,0:T(8,128)(2,1)} %all-gather.8.cloned.1.call-done), kind=kOutput, calls=%fused_computation.38 | convolution fusion | flops 3241672704 | bytes 16777220 | tf_op jit(solution)/shard_map/dot_general | solution.py:322
  407.7 11.5 %add_convert_fusion.2 = bf16[1024,2048]{1,0:T(8,128)(2,1)S(1)} fusion(bf16[1024,2048]{1,0:T(8,128)(2,1)} %collective-permute-done.4, bf16[2048,1536]{1,0:T(8,128)(2,1)} %all-gather.6.cloned.1.call-done, bf16[1024,768]{1,0:T(8,128)(2,1)S(1)} %get-tuple-element.96, bf16[1024,768]{1,0:T(8,128)(2,1)S(1)} %get-tuple-element.95), kind=kOutput, calls=%fused_computation.9 | convolution fusion | flops 6455033856 | bytes 17825792 | tf_op jit(solution)/shard_map/dot_general | solution.py:322
  436.4 16.4 %fusion.4 = bf16[2048,1536]{1,0:T(8,128)(2,1)} fusion(bf16[1024,2048]{1,0:T(8,128)(2,1)S(1)} %copy-done.66, bf16[1024,2048]{1,0:T(8,128)(2,1)} %bitcast.44, bf16[1024,1536]{1,0:T(8,128)(2,1)S(1)} %fusion.40, bf16[1024,1536]{1,0:T(8,128)(2,1)S(1)} %fusion.42), kind=kOutput, calls=%fused_computation.12 | convolution fusion | flops 12917407744 | bytes 20971520 | tf_op jit(solution)/shard_map/dot_general | solution.py:322
  457.8 20.4 %all-to-all-done.9 = bf16[4,256,2048]{2,1,0:T(8,128)(2,1)} async-done(((bf16[4,256,2048]{2,1,0:T(8,128)(2,1)}), bf16[4,256,2048]{2,1,0:T(8,128)(2,1)}, u32[]{:S(2)}, u32[]{:S(2)}) %all-to-all-start.9) | async-done | bytes 4194336 | tf_op jit(solution)/shard_map/all_to_all | solution.py:332
  501.0 46.3 %all-to-all-done.10 = bf16[4,256,2048]{2,1,0:T(8,128)(2,1)} async-done(((bf16[4,256,2048]{2,1,0:T(8,128)(2,1)}), bf16[4,256,2048]{2,1,0:T(8,128)(2,1)}, u32[]{:S(2)}, u32[]{:S(2)}) %all-to-all-start.10) | async-done | bytes 4194336 | tf_op jit(solution)/shard_map/all_to_all | solution.py:332
  579.6 25.3 %recur_backward.1 = (bf16[2048,768]{1,0:T(8,128)(2,1)}, bf16[2048,768]{1,0:T(8,128)(2,1)}, f32[7,8,384]{2,1,0:T(8,128)S(1)}) custom-call(f32[1024,768]{1,0:T(8,128)} %copy-done.1, f32[1024,768]{1,0:T(8,128)} %copy-done.2, f32[1024,384]{1,0:T(8,128)S(1)} %copy-done.4, f32[1024,384]{1,0:T(8,128)S(1)} %copy-done.5, f32[3,2048,128]{2,1,0:T(8,128)} %copy-done, ...), custom_call_target="tpu_custom_call" | custom-call | flops 157286400 | bytes 100663296 | tf_op jit(solution)/shard_map/recur_backward/pallas_call | solution.py:284
  622.8 7.0 add_convert_fusion
  643.2 6.9 fusion.46
  650.2 6.6 add_convert_fusion.4
  676.6 7.9 %all-to-all-done.11 = bf16[4,256,2048]{2,1,0:T(8,128)(2,1)} async-done(((bf16[4,256,2048]{2,1,0:T(8,128)(2,1)}), bf16[4,256,2048]{2,1,0:T(8,128)(2,1)}, u32[]{:S(2)}, u32[]{:S(2)}) %all-to-all-start.11) | async-done | bytes 4194336 | tf_op jit(solution)/shard_map/all_to_all | solution.py:332
  711.1 12.2 %collective-permute-done.13 = f32[128]{0:T(128)S(1)} collective-permute-done((f32[128]{0:T(128)S(1)}, f32[128]{0:T(128)S(1)}, u32[]{:S(2)}, u32[]{:S(2)}) %collective-permute-start.13) | collective-permute-done | bytes 544 | tf_op jit(solution)/shard_map/ppermute | solution.py:582
  (407 shorter events, 304.4 us)
Async XLA Ops:
  45.0 99.0 %all-gather.4.cloned.1.call-start = ((), (), s32[]{:S(2)}) async-start(), calls=%async_computation.18 | async-start | bytes 4915200 | tf_op jit(solution)/shard_map/all_gather | solution.py:403
  102.9 50.0 %collective-permute-start = (bf16[1024,2048]{1,0:T(8,128)(2,1)}, bf16[1024,2048]{1,0:T(8,128)(2,1)}, u32[]{:S(2)}, u32[]{:S(2)}) collective-permute-start(bf16[1024,2048]{1,0:T(8,128)(2,1)} %bitcast.228), channel_id=1, source_target_pairs={{0,1},{1,0},{2,3},{3,2},{4,5},{5,4},{6,7},{7,6},{8,9},{9,8},{10,11... | collective-permute-start | bytes 12582920 | tf_op jit(solution)/shard_map/ppermute | solution.py:338
  110.1 21.7 %all-to-all-start.3 = ((bf16[4,128,1536]{1,2,0:T(8,128)(2,1)}), bf16[4,128,1536]{1,2,0:T(8,128)(2,1)S(1)}, u32[]{:S(2)}, u32[]{:S(2)}) async-start(bf16[4,128,1536]{1,2,0:T(8,128)(2,1)} %pad_maximum_fusion.8), calls=%async_computation.3 | async-start | bytes 3145728 | tf_op jit(solution)/shard_map/all_to_all | solution.py:332
  134.4 51.8 %all-to-all-start.5 = ((bf16[4,256,2048]{2,1,0:T(8,128)(2,1)}), bf16[4,256,2048]{2,1,0:T(8,128)(2,1)}, u32[]{:S(2)}, u32[]{:S(2)}) async-start(bf16[4,256,2048]{2,1,0:T(8,128)(2,1)} %broadcast_in_dim.64), calls=%async_computation.5 | async-start | bytes 8388608 | tf_op jit(solution)/shard_map/all_to_all | solution.py:332
  139.4 124.5 %all-gather.6.cloned.1.call-start = ((), (), s32[]{:S(2)}) async-start(), calls=%async_computation.19 | async-start | bytes 7864320 | tf_op jit(solution)/shard_map/all_gather | solution.py:403
  202.9 63.5 %all-to-all-start.6 = ((bf16[4,256,2048]{2,1,0:T(8,128)(2,1)}), bf16[4,256,2048]{2,1,0:T(8,128)(2,1)}, u32[]{:S(2)}, u32[]{:S(2)}) async-start(bf16[4,256,2048]{2,1,0:T(8,128)(2,1)} %bitcast.234), calls=%async_computation.6 | async-start | bytes 8388608 | tf_op jit(solution)/shard_map/all_to_all | solution.py:332
  207.7 119.8 %all-gather.8.cloned.1.call-start = ((), (), s32[]{:S(2)}) async-start(), calls=%async_computation.20 | async-start | bytes 3932160 | tf_op jit(solution)/shard_map/all_gather | solution.py:403
  274.4 55.7 %all-to-all-start.7 = ((bf16[4,256,2048]{2,1,0:T(8,128)(2,1)}), bf16[4,256,2048]{2,1,0:T(8,128)(2,1)}, u32[]{:S(2)}, u32[]{:S(2)}) async-start(bf16[4,256,2048]{2,1,0:T(8,128)(2,1)} %broadcast_in_dim.65), calls=%async_computation.7 | async-start | bytes 8388608 | tf_op jit(solution)/shard_map/all_to_all | solution.py:332
  279.2 176.2 %reduce-scatter.5.cloned.1.call-start = ((), (), s32[]{:S(2)}) async-start(), calls=%async_computation.21 | async-start | bytes 3932160 | tf_op jit(solution)/shard_map/reduce_scatter | solution.py:400
  332.5 20.9 %collective-permute-start.3 = (bf16[1024,2048]{1,0:T(8,128)(2,1)S(1)}, bf16[1024,2048]{1,0:T(8,128)(2,1)S(1)}, u32[]{:S(2)}, u32[]{:S(2)}) collective-permute-start(bf16[1024,2048]{1,0:T(8,128)(2,1)S(1)} %broadcast_add_fusion), channel_id=1, source_target_pairs={{0,1},{1,0},{2,3},{3,2},{4,5},{5,4},{6,7},{7,6},{8,9},{9,8},{10,11... | collective-permute-start | bytes 12582920 | tf_op jit(solution)/shard_map/ppermute | solution.py:338
  333.3 29.5 %collective-permute-start.2 = (bf16[1024,2048]{1,0:T(8,128)(2,1)}, bf16[1024,2048]{1,0:T(8,128)(2,1)S(1)}, u32[]{:S(2)}, u32[]{:S(2)}) collective-permute-start(bf16[1024,2048]{1,0:T(8,128)(2,1)} %bitcast.40), channel_id=1, source_target_pairs={{0,1},{1,0},{2,3},{3,2},{4,5},{5,4},{6,7},{7,6},{8,9},{9,8},{10,11... | collective-permute-start | bytes 12582920 | tf_op jit(solution)/shard_map/ppermute | solution.py:338
  426.2 55.5 %collective-permute-start.5 = (bf16[1024,2048]{1,0:T(8,128)(2,1)}, bf16[1024,2048]{1,0:T(8,128)(2,1)}, u32[]{:S(2)}, u32[]{:S(2)}) collective-permute-start(bf16[1024,2048]{1,0:T(8,128)(2,1)} %fusion.48), channel_id=1, source_target_pairs={{0,1},{1,0},{2,3},{3,2},{4,5},{5,4},{6,7},{7,6},{8,9},{9,8},{10,11... | collective-permute-start | bytes 12582920 | tf_op jit(solution)/shard_map/ppermute | solution.py:338
  426.2 52.1 %all-to-all-start.9 = ((bf16[4,256,2048]{2,1,0:T(8,128)(2,1)}), bf16[4,256,2048]{2,1,0:T(8,128)(2,1)}, u32[]{:S(2)}, u32[]{:S(2)}) async-start(bf16[4,256,2048]{2,1,0:T(8,128)(2,1)} %bitcast.233), calls=%async_computation.9 | async-start | bytes 8388608 | tf_op jit(solution)/shard_map/all_to_all | solution.py:332
  495.5 51.7 %all-to-all-start.10 = ((bf16[4,256,2048]{2,1,0:T(8,128)(2,1)}), bf16[4,256,2048]{2,1,0:T(8,128)(2,1)}, u32[]{:S(2)}, u32[]{:S(2)}) async-start(bf16[4,256,2048]{2,1,0:T(8,128)(2,1)} %broadcast_in_dim.67), calls=%async_computation.11 | async-start | bytes 8388608 | tf_op jit(solution)/shard_map/all_to_all | solution.py:332
  500.4 165.5 %reduce-scatter.7.cloned.1.call-start = ((), (), s32[]{:S(2)}) async-start(), calls=%async_computation.22 | async-start | bytes 7864320 | tf_op jit(solution)/shard_map/reduce_scatter | solution.py:400
  547.2 17.5 %collective-permute-start.6 = (bf16[1024,2048]{1,0:T(8,128)(2,1)}, bf16[1024,2048]{1,0:T(8,128)(2,1)}, u32[]{:S(2)}, u32[]{:S(2)}) collective-permute-start(bf16[1024,2048]{1,0:T(8,128)(2,1)} %bitcast.52), channel_id=1, source_target_pairs={{0,1},{1,0},{2,3},{3,2},{4,5},{5,4},{6,7},{7,6},{8,9},{9,8},{10,11... | collective-permute-start | bytes 12582920 | tf_op jit(solution)/shard_map/ppermute | solution.py:338
  548.8 62.6 %all-to-all-start.8 = ((bf16[4,256,2048]{2,1,0:T(8,128)(2,1)}), bf16[4,256,2048]{2,1,0:T(8,128)(2,1)}, u32[]{:S(2)}, u32[]{:S(2)}) async-start(bf16[4,256,2048]{2,1,0:T(8,128)(2,1)} %bitcast.219), calls=%async_computation.8 | async-start | bytes 8388608 | tf_op jit(solution)/shard_map/all_to_all | solution.py:332
  553.7 116.6 %reduce-scatter.9.cloned.1.call-start = ((), (), s32[]{:S(2)}) async-start(), calls=%async_computation.23 | async-start | bytes 1966080 | tf_op jit(solution)/shard_map/reduce_scatter | solution.py:400
  631.9 52.6 %all-to-all-start.11 = ((bf16[4,256,2048]{2,1,0:T(8,128)(2,1)}), bf16[4,256,2048]{2,1,0:T(8,128)(2,1)}, u32[]{:S(2)}, u32[]{:S(2)}) async-start(bf16[4,256,2048]{2,1,0:T(8,128)(2,1)} %bitcast.232), calls=%async_computation.12 | async-start | bytes 8388608 | tf_op jit(solution)/shard_map/all_to_all | solution.py:332
  636.8 101.3 %reduce-scatter.11.cloned.1.call-start = ((), (), s32[]{:S(2)}) async-start(), calls=%async_computation.24 | async-start | bytes 3686400 | tf_op jit(solution)/shard_map/reduce_scatter | solution.py:400
  665.4 43.1 %collective-permute-start.7 = (f32[256,2048]{1,0:T(8,128)}, f32[256,2048]{1,0:T(8,128)}, u32[]{:S(2)}, u32[]{:S(2)}) collective-permute-start(f32[256,2048]{1,0:T(8,128)} %add_add_fusion.2), channel_id=1, source_target_pairs={{0,1},{1,0},{2,3},{3,2},{4,5},{5,4},{6,7},{7,6},{8,9},{9,8},{10,11... | collective-permute-start | bytes 6291464 | tf_op jit(solution)/shard_map/ppermute | solution.py:338
  689.0 39.9 %all-to-all-start.13 = ((bf16[4,128,2624]{1,2,0:T(8,128)(2,1)}), bf16[4,128,2624]{1,2,0:T(8,128)(2,1)S(1)}, u32[]{:S(2)}, u32[]{:S(2)}) async-start(bf16[4,128,2624]{1,2,0:T(8,128)(2,1)} %maximum_add_fusion), calls=%async_computation.17 | async-start | bytes 5373952 | tf_op jit(solution)/shard_map/all_to_all | solution.py:332
  703.7 37.9 %collective-permute-start.9 = (f32[256,2048]{1,0:T(8,128)}, f32[256,2048]{1,0:T(8,128)}, u32[]{:S(2)}, u32[]{:S(2)}) collective-permute-start(f32[256,2048]{1,0:T(8,128)} %fusion.37), channel_id=1, source_target_pairs={{0,1},{1,0},{2,3},{3,2},{4,5},{5,4},{6,7},{7,6},{8,9},{9,8},{10,11... | collective-permute-start | bytes 6291464 | tf_op jit(solution)/shard_map/ppermute | solution.py:338
  705.5 17.8 %collective-permute-start.13 = (f32[128]{0:T(128)S(1)}, f32[128]{0:T(128)S(1)}, u32[]{:S(2)}, u32[]{:S(2)}) collective-permute-start(f32[128]{0:T(128)S(1)} %get-tuple-element.133), channel_id=1, source_target_pairs={{0,2},{2,0},{4,6},{6,4},{8,10},{10,8},{12,14},{14,12},{16,18},{18,... | collective-permute-start | bytes 1544 | tf_op jit(solution)/shard_map/ppermute | solution.py:582
  (89 other events, 708.7 us)
Sparse Core Ops, SparseCore 0:
  48.0 78.2 all-gather.3
  144.1 119.7 all-gather.5
  266.1 61.4 all-gather.7
  397.2 58.1 reduce-scatter.4
  503.2 110.5 reduce-scatter.6
  621.7 33.8 reduce-scatter.8
  664.1 56.0 reduce-scatter.10

commit v4 on v3

--- a/solution.py
+++ b/solution.py
@@ -274,7 +274,7 @@
         mixlow_ref[pl.ds(r * row, row), pl.ds(cp, cp)] = flat(gdec, pl.ds(r * pitch, row)).astype(BF)
 
 
-def backward_call(mix, gm, mask, par, wg, values, pre, h, *earlier, unroll=4):
+def backward_call(mix, gm, mask, par, wg, values, pre, h, *earlier, unroll=8):
     tokens, cp = 2 * gm[0].shape[0], gm[0].shape[1]
     row = tokens // ROWS
     lanes = cp // 128
@@ -479,14 +479,15 @@
         arrived = swap_core(dot(mixed_far, w_out_t, 1, 1, BF))
         sums = dot(mixed_near, w_out_t, 1, 1) + arrived.astype(F32)
         after_mix = x_own_f + scatter4(sums.astype(BF))
-        normed_own = (rms_scale(after_mix, mlp_gain_f) + zero(w_in)).astype(BF)
+        normed_own = rms_scale(after_mix, mlp_gain_f).astype(BF)
         normed_near = gather4(normed_own)
-        normed = [normed_near, swap_core(normed_near + zero(w_down_t).astype(BF))]
+        normed = [normed_near, swap_core(normed_near + zero(w_in).astype(BF))]
         hidden, gate_up = [], []
         for a in normed:
             pre_act = dot(a, w_in, 1, 0)
             gate_up.append(pre_act)
-            hidden.append((jax.nn.gelu(pre_act[:, :ff]) * pre_act[:, ff:]).astype(BF))
+            act = jax.nn.gelu(pre_act[:, :ff]) * pre_act[:, ff:]
+            hidden.append((act + zero(w_down_t) if hidden else act).astype(BF))
 
         grad_down = token_sum(c_half, hidden).astype(BF)
         down_piece = scatter_z(grad_down)

time: 775 us -> 774 us (level)
    all_gather x3, waiting for transfers between devices: 104 us -> 7.11 us  [gather_z(): lax.all_gather(rows, 'dp', axis=0, axis_index_groups=lines, tiled=True)]
    all_to_all x12, waiting for transfers between devices: 101 us -> 192 us  [trade(): return lax.all_to_all(a, 'dp', 0, 0, axis_index_groups=groups, tiled=True)]
    unnamed x162 -> x158, local copies, waits for them, and re-layouts: 35.9 us -> 34.2 us
  transfers between devices with their start and end apart: 37 -> 37, of which waited for: 15 -> 16; matrix products, arithmetic and copies ran while one was open for 31% -> 32% of each run, Pallas kernels for 5% -> 5%
where the time goes in v4:
time: 774 us; the launch traced here: 766 us
  waiting for transfers between devices  220 us (28%)
  matrix products  173 us (22%)
  local copies, waits for them, and re-layouts  92.7 us (12%)
  starting transfers between devices  78 us (10%)
  blocking collectives  65.7 us (8%)
  other arithmetic  58.5 us (8%)
  between operations  40.2 us (5%)
  Pallas kernels  37 us (5%)
    all_to_all x12, waiting for transfers between devices, trade(): return lax.all_to_all(a, 'dp', 0, 0, axis_index_groups=groups, tiled=True)  192 us
    dot_general x24, matrix products, dot(): lax.dot_general(a, b, (((ca,), (cb,)), ((), ())), preferred_element_type=...  173 us
    all_to_all x2, blocking collectives, trade(): return lax.all_to_all(a, 'dp', 0, 0, axis_index_groups=groups, tiled=True)  65.7 us
    all_to_all x12, starting transfers between devices, trade(): return lax.all_to_all(a, 'dp', 0, 0, axis_index_groups=groups, tiled=True)  54.5 us
    unnamed x158, local copies, waits for them, and re-layouts  34.2 us
    pallas_call x1, Pallas kernels, backward_call(): pl.pallas_call(functools.partial(backward_kernel, cp, row, unroll, len(ea...  24.7 us
    slice x17, local copies, waits for them, and re-layouts, index_zero(): e = a[(0,) * a.ndim]  17.6 us
    ppermute x12, starting transfers between devices, swap_core(): return lax.ppermute(a, 'mp', cores)  16.4 us
  transfers between devices with their start and end apart: 37, of which 16 were waited for; matrix products, arithmetic and copies ran while one was open for 32% of the time, Pallas kernels for 5%

profile of v4, /device:TPU:1, one launch (start us, length us, event | category | flops | bytes accessed | tf_op | source)
XLA Modules:
  0.0 765.7 jit_solution(9849672174180736566)
XLA Ops:
  19.9 18.3 %all_to_all.70 = bf16[4,137,960]{2,1,0:T(8,128)(2,1)S(1)} all-to-all(bf16[4,137,960]{2,1,0:T(8,128)(2,1)S(1)} %copy.146), channel_id=1, replica_groups={{0,2,4,6},{8,10,12,14},{16,18,20,22},{24,26,28,30},{1,3,5,7},{9,11,13,1..., dimensions={0} | all-to-all | bytes 2104320 | tf_op jit(solution)/shard_map/all_to_all | solution.py:332
  51.9 47.3 %all_to_all.71 = bf16[4,256,2048]{2,1,0:T(8,128)(2,1)} all-to-all(bf16[4,256,2048]{2,1,0:T(8,128)(2,1)S(1)} %broadcast_in_dim.59), channel_id=1, replica_groups={{0,2,4,6},{8,10,12,14},{16,18,20,22},{24,26,28,30},{1,3,5,7},{9,11,13,1..., dimensions={0} | all-to-all | bytes 8388608 | tf_op jit(solution)/shard_map/all_to_all | solution.py:332
  122.9 9.0 %all-to-all-done.3 = bf16[4,128,1536]{1,2,0:T(8,128)(2,1)S(1)} async-done(((bf16[4,128,1536]{1,2,0:T(8,128)(2,1)}), bf16[4,128,1536]{1,2,0:T(8,128)(2,1)S(1)}, u32[]{:S(2)}, u32[]{:S(2)}) %all-to-all-start.3) | async-done | bytes 1572896 | tf_op jit(solution)/shard_map/all_to_all | solution.py:332
  152.9 7.1 fusion.123.far_hbm.mix_far
  161.7 12.3 %recur_forward.1 = (bf16[2048,384]{1,0:T(8,128)(2,1)S(1)}, bf16[2048,384]{1,0:T(8,128)(2,1)S(1)}, f32[6,2112,128]{2,1,0:T(8,128)}, f32[3,2112,128]{2,1,0:T(8,128)S(1)}) custom-call(f32[1024,768]{1,0:T(8,128)S(1)} %fusion.125.near_hbm.mix_near, f32[1024,768]{1,0:T(8,128)S(1)} %fusion.123.far_hbm.mix_far, f32[3,2048,128]{2,1,0:T(8,128)S(1)} %broadcast_in_dim.62.mask_ref, ...), custom_call_target="tpu_custom_call" | custom-call | flops 117964800 | bytes 66060288 | tf_op jit(solution)/shard_map/recur_forward/pallas_call | solution.py:125
  179.1 7.2 all-to-all-done.5
  191.7 6.8 collective-permute-done.1
  208.4 46.4 %all-to-all-done.6 = bf16[4,256,2048]{2,1,0:T(8,128)(2,1)} async-done(((bf16[4,256,2048]{2,1,0:T(8,128)(2,1)}), bf16[4,256,2048]{2,1,0:T(8,128)(2,1)}, u32[]{:S(2)}, u32[]{:S(2)}) %all-to-all-start.6) | async-done | bytes 4194336 | tf_op jit(solution)/shard_map/all_to_all | solution.py:332
  270.2 44.3 %all-to-all-done.7 = bf16[4,256,2048]{2,1,0:T(8,128)(2,1)} async-done(((bf16[4,256,2048]{2,1,0:T(8,128)(2,1)}), bf16[4,256,2048]{2,1,0:T(8,128)(2,1)}, u32[]{:S(2)}, u32[]{:S(2)}) %all-to-all-start.7) | async-done | bytes 4194336 | tf_op jit(solution)/shard_map/all_to_all | solution.py:332
  320.5 7.1 all-gather.8.cloned.1.call-done
  330.8 10.5 %fusion.132 = f32[1024,1536]{1,0:T(8,128)S(1)} fusion(bf16[1024,2048]{1,0:T(8,128)(2,1)} %bitcast.43, bf16[2048,1536]{1,0:T(8,128)(2,1)} %all-gather.6.cloned.1.call-done), kind=kOutput, calls=%fused_computation.235 | convolution fusion | flops 6442450944 | bytes 16777216 | tf_op jit(solution)/shard_map/dot_general | solution.py:322
  350.8 8.4 %fusion.134 = f32[1024,1536]{1,0:T(8,128)S(1)} fusion(bf16[1024,2048]{1,0:T(8,128)(2,1)} %collective-permute-done.3, bf16[2048,1536]{1,0:T(8,128)(2,1)S(1)} %bitcast.262), kind=kOutput, calls=%fused_computation.237 | convolution fusion | flops 6442450944 | bytes 16777216 | tf_op jit(solution)/shard_map/dot_general | solution.py:322
  372.6 10.4 %fusion.26 = (bf16[1024,768]{1,0:T(8,128)(2,1)S(1)}, bf16[1024,768]{1,0:T(8,128)(2,1)S(1)}) fusion(f32[1024,1536]{1,0:T(8,128)} %copy-done.21, f32[]{:T(128)} %bitcast.46, bf16[1024,2048]{1,0:T(8,128)(2,1)} %copy-done.65, bf16[2048,768]{1,0:T(8,128)(2,1)} %all-gather.8.cloned.1.call-done), kind=kOutput, calls=%fused_computation.46 | convolution fusion | flops 3241672704 | bytes 16777220 | tf_op jit(solution)/shard_map/dot_general | solution.py:322
  383.0 12.1 %fusion.41 = bf16[1024,2048]{1,0:T(8,128)(2,1)} fusion(bf16[2048,1536]{1,0:T(8,128)(2,1)} %all-gather.6.cloned.1.call-done, bf16[1024,768]{1,0:T(8,128)(2,1)S(1)} %get-tuple-element.98, bf16[1024,768]{1,0:T(8,128)(2,1)S(1)} %get-tuple-element.97), kind=kOutput, calls=%fused_computation.85 | convolution fusion | flops 6448742400 | bytes 13631488 | tf_op jit(solution)/shard_map/dot_general | solution.py:322
  395.2 10.4 %fusion.18 = (bf16[1024,768]{1,0:T(8,128)(2,1)S(1)}, bf16[1024,768]{1,0:T(8,128)(2,1)S(1)}) fusion(f32[1024,1536]{1,0:T(8,128)} %copy-done.22, f32[]{:T(128)} %bitcast.46, bf16[1024,2048]{1,0:T(8,128)(2,1)} %bitcast.40, bf16[2048,768]{1,0:T(8,128)(2,1)} %all-gather.8.cloned.1.call-done), kind=kOutput, calls=%fused_computation.38 | convolution fusion | flops 3241672704 | bytes 16777220 | tf_op jit(solution)/shard_map/dot_general | solution.py:322
  405.6 11.5 %add_convert_fusion.2 = bf16[1024,2048]{1,0:T(8,128)(2,1)S(1)} fusion(bf16[1024,2048]{1,0:T(8,128)(2,1)} %collective-permute-done.4, bf16[2048,1536]{1,0:T(8,128)(2,1)} %all-gather.6.cloned.1.call-done, bf16[1024,768]{1,0:T(8,128)(2,1)S(1)} %get-tuple-element.96, bf16[1024,768]{1,0:T(8,128)(2,1)S(1)} %get-tuple-element.95), kind=kOutput, calls=%fused_computation.9 | convolution fusion | flops 6455033856 | bytes 17825792 | tf_op jit(solution)/shard_map/dot_general | solution.py:322
  433.3 17.6 %fusion.4 = bf16[2048,1536]{1,0:T(8,128)(2,1)} fusion(bf16[1024,2048]{1,0:T(8,128)(2,1)} %collective-permute-done.3, bf16[1024,2048]{1,0:T(8,128)(2,1)} %bitcast.43, bf16[1024,1536]{1,0:T(8,128)(2,1)S(1)} %fusion.40, bf16[1024,1536]{1,0:T(8,128)(2,1)S(1)} %fusion.42), kind=kOutput, calls=%fused_computation.12 | convolution fusion | flops 12917407744 | bytes 20971520 | tf_op jit(solution)/shard_map/dot_general | solution.py:322
  456.4 21.0 %all-to-all-done.9 = bf16[4,256,2048]{2,1,0:T(8,128)(2,1)} async-done(((bf16[4,256,2048]{2,1,0:T(8,128)(2,1)}), bf16[4,256,2048]{2,1,0:T(8,128)(2,1)}, u32[]{:S(2)}, u32[]{:S(2)}) %all-to-all-start.9) | async-done | bytes 4194336 | tf_op jit(solution)/shard_map/all_to_all | solution.py:332
  500.1 46.3 %all-to-all-done.10 = bf16[4,256,2048]{2,1,0:T(8,128)(2,1)} async-done(((bf16[4,256,2048]{2,1,0:T(8,128)(2,1)}), bf16[4,256,2048]{2,1,0:T(8,128)(2,1)}, u32[]{:S(2)}, u32[]{:S(2)}) %all-to-all-start.10) | async-done | bytes 4194336 | tf_op jit(solution)/shard_map/all_to_all | solution.py:332
  578.6 24.7 %recur_backward.1 = (bf16[2048,768]{1,0:T(8,128)(2,1)}, bf16[2048,768]{1,0:T(8,128)(2,1)}, f32[7,8,384]{2,1,0:T(8,128)S(1)}) custom-call(f32[1024,768]{1,0:T(8,128)} %copy-done.1, f32[1024,768]{1,0:T(8,128)} %copy-done.2, f32[1024,384]{1,0:T(8,128)S(1)} %copy-done.4, f32[1024,384]{1,0:T(8,128)S(1)} %copy-done.5, f32[3,2048,128]{2,1,0:T(8,128)} %copy-done, ...), custom_call_target="tpu_custom_call" | custom-call | flops 157286400 | bytes 100663296 | tf_op jit(solution)/shard_map/recur_backward/pallas_call | solution.py:284
  621.2 7.0 add_convert_fusion
  641.6 6.9 fusion.46
  675.0 7.9 %all-to-all-done.11 = bf16[4,256,2048]{2,1,0:T(8,128)(2,1)} async-done(((bf16[4,256,2048]{2,1,0:T(8,128)(2,1)}), bf16[4,256,2048]{2,1,0:T(8,128)(2,1)}, u32[]{:S(2)}, u32[]{:S(2)}) %all-to-all-start.11) | async-done | bytes 4194336 | tf_op jit(solution)/shard_map/all_to_all | solution.py:332
  709.5 12.3 %collective-permute-done.13 = f32[128]{0:T(128)S(1)} collective-permute-done((f32[128]{0:T(128)S(1)}, f32[128]{0:T(128)S(1)}, u32[]{:S(2)}, u32[]{:S(2)}) %collective-permute-start.13) | collective-permute-done | bytes 544 | tf_op jit(solution)/shard_map/ppermute | solution.py:583
  (403 shorter events, 312.8 us)
Async XLA Ops:
  45.0 99.0 %all-gather.4.cloned.1.call-start = ((), (), s32[]{:S(2)}) async-start(), calls=%async_computation.18 | async-start | bytes 4915200 | tf_op jit(solution)/shard_map/all_gather | solution.py:403
  102.9 50.0 %collective-permute-start = (bf16[1024,2048]{1,0:T(8,128)(2,1)}, bf16[1024,2048]{1,0:T(8,128)(2,1)}, u32[]{:S(2)}, u32[]{:S(2)}) collective-permute-start(bf16[1024,2048]{1,0:T(8,128)(2,1)} %bitcast.228), channel_id=1, source_target_pairs={{0,1},{1,0},{2,3},{3,2},{4,5},{5,4},{6,7},{7,6},{8,9},{9,8},{10,11... | collective-permute-start | bytes 12582920 | tf_op jit(solution)/shard_map/ppermute | solution.py:338
  110.1 21.7 %all-to-all-start.3 = ((bf16[4,128,1536]{1,2,0:T(8,128)(2,1)}), bf16[4,128,1536]{1,2,0:T(8,128)(2,1)S(1)}, u32[]{:S(2)}, u32[]{:S(2)}) async-start(bf16[4,128,1536]{1,2,0:T(8,128)(2,1)} %pad_maximum_fusion.8), calls=%async_computation.3 | async-start | bytes 3145728 | tf_op jit(solution)/shard_map/all_to_all | solution.py:332
  134.4 51.8 %all-to-all-start.5 = ((bf16[4,256,2048]{2,1,0:T(8,128)(2,1)}), bf16[4,256,2048]{2,1,0:T(8,128)(2,1)}, u32[]{:S(2)}, u32[]{:S(2)}) async-start(bf16[4,256,2048]{2,1,0:T(8,128)(2,1)} %broadcast_in_dim.64), calls=%async_computation.5 | async-start | bytes 8388608 | tf_op jit(solution)/shard_map/all_to_all | solution.py:332
  139.4 128.3 %all-gather.6.cloned.1.call-start = ((), (), s32[]{:S(2)}) async-start(), calls=%async_computation.19 | async-start | bytes 7864320 | tf_op jit(solution)/shard_map/all_gather | solution.py:403
  202.8 52.0 %all-to-all-start.6 = ((bf16[4,256,2048]{2,1,0:T(8,128)(2,1)}), bf16[4,256,2048]{2,1,0:T(8,128)(2,1)}, u32[]{:S(2)}, u32[]{:S(2)}) async-start(bf16[4,256,2048]{2,1,0:T(8,128)(2,1)} %bitcast.234), calls=%async_computation.6 | async-start | bytes 8388608 | tf_op jit(solution)/shard_map/all_to_all | solution.py:332
  207.7 119.8 %all-gather.8.cloned.1.call-start = ((), (), s32[]{:S(2)}) async-start(), calls=%async_computation.20 | async-start | bytes 3932160 | tf_op jit(solution)/shard_map/all_gather | solution.py:403
  262.7 51.7 %all-to-all-start.7 = ((bf16[4,256,2048]{2,1,0:T(8,128)(2,1)}), bf16[4,256,2048]{2,1,0:T(8,128)(2,1)}, u32[]{:S(2)}, u32[]{:S(2)}) async-start(bf16[4,256,2048]{2,1,0:T(8,128)(2,1)} %broadcast_in_dim.65), calls=%async_computation.7 | async-start | bytes 8388608 | tf_op jit(solution)/shard_map/all_to_all | solution.py:332
  267.6 186.2 %reduce-scatter.5.cloned.1.call-start = ((), (), s32[]{:S(2)}) async-start(), calls=%async_computation.21 | async-start | bytes 3932160 | tf_op jit(solution)/shard_map/reduce_scatter | solution.py:400
  318.9 31.8 %collective-permute-start.3 = (bf16[1024,2048]{1,0:T(8,128)(2,1)}, bf16[1024,2048]{1,0:T(8,128)(2,1)}, u32[]{:S(2)}, u32[]{:S(2)}) collective-permute-start(bf16[1024,2048]{1,0:T(8,128)(2,1)} %broadcast_add_fusion), channel_id=1, source_target_pairs={{0,1},{1,0},{2,3},{3,2},{4,5},{5,4},{6,7},{7,6},{8,9},{9,8},{10,11... | collective-permute-start | bytes 12582920 | tf_op jit(solution)/shard_map/ppermute | solution.py:338
  330.0 31.8 %collective-permute-start.2 = (bf16[1024,2048]{1,0:T(8,128)(2,1)}, bf16[1024,2048]{1,0:T(8,128)(2,1)S(1)}, u32[]{:S(2)}, u32[]{:S(2)}) collective-permute-start(bf16[1024,2048]{1,0:T(8,128)(2,1)} %bitcast.40), channel_id=1, source_target_pairs={{0,1},{1,0},{2,3},{3,2},{4,5},{5,4},{6,7},{7,6},{8,9},{9,8},{10,11... | collective-permute-start | bytes 12582920 | tf_op jit(solution)/shard_map/ppermute | solution.py:338
  424.1 56.6 %collective-permute-start.5 = (bf16[1024,2048]{1,0:T(8,128)(2,1)}, bf16[1024,2048]{1,0:T(8,128)(2,1)}, u32[]{:S(2)}, u32[]{:S(2)}) collective-permute-start(bf16[1024,2048]{1,0:T(8,128)(2,1)} %fusion.48), channel_id=1, source_target_pairs={{0,1},{1,0},{2,3},{3,2},{4,5},{5,4},{6,7},{7,6},{8,9},{9,8},{10,11... | collective-permute-start | bytes 12582920 | tf_op jit(solution)/shard_map/ppermute | solution.py:338
  424.7 52.6 %all-to-all-start.9 = ((bf16[4,256,2048]{2,1,0:T(8,128)(2,1)}), bf16[4,256,2048]{2,1,0:T(8,128)(2,1)}, u32[]{:S(2)}, u32[]{:S(2)}) async-start(bf16[4,256,2048]{2,1,0:T(8,128)(2,1)} %bitcast.233), calls=%async_computation.9 | async-start | bytes 8388608 | tf_op jit(solution)/shard_map/all_to_all | solution.py:332
  494.6 51.7 %all-to-all-start.10 = ((bf16[4,256,2048]{2,1,0:T(8,128)(2,1)}), bf16[4,256,2048]{2,1,0:T(8,128)(2,1)}, u32[]{:S(2)}, u32[]{:S(2)}) async-start(bf16[4,256,2048]{2,1,0:T(8,128)(2,1)} %broadcast_in_dim.67), calls=%async_computation.11 | async-start | bytes 8388608 | tf_op jit(solution)/shard_map/all_to_all | solution.py:332
  499.5 164.9 %reduce-scatter.7.cloned.1.call-start = ((), (), s32[]{:S(2)}) async-start(), calls=%async_computation.22 | async-start | bytes 7864320 | tf_op jit(solution)/shard_map/reduce_scatter | solution.py:400
  546.3 17.4 %collective-permute-start.6 = (bf16[1024,2048]{1,0:T(8,128)(2,1)}, bf16[1024,2048]{1,0:T(8,128)(2,1)}, u32[]{:S(2)}, u32[]{:S(2)}) collective-permute-start(bf16[1024,2048]{1,0:T(8,128)(2,1)} %bitcast.52), channel_id=1, source_target_pairs={{0,1},{1,0},{2,3},{3,2},{4,5},{5,4},{6,7},{7,6},{8,9},{9,8},{10,11... | collective-permute-start | bytes 12582920 | tf_op jit(solution)/shard_map/ppermute | solution.py:338
  547.8 61.9 %all-to-all-start.8 = ((bf16[4,256,2048]{2,1,0:T(8,128)(2,1)}), bf16[4,256,2048]{2,1,0:T(8,128)(2,1)}, u32[]{:S(2)}, u32[]{:S(2)}) async-start(bf16[4,256,2048]{2,1,0:T(8,128)(2,1)} %bitcast.219), calls=%async_computation.8 | async-start | bytes 8388608 | tf_op jit(solution)/shard_map/all_to_all | solution.py:332
  553.3 115.6 %reduce-scatter.9.cloned.1.call-start = ((), (), s32[]{:S(2)}) async-start(), calls=%async_computation.23 | async-start | bytes 1966080 | tf_op jit(solution)/shard_map/reduce_scatter | solution.py:400
  630.3 52.6 %all-to-all-start.11 = ((bf16[4,256,2048]{2,1,0:T(8,128)(2,1)}), bf16[4,256,2048]{2,1,0:T(8,128)(2,1)}, u32[]{:S(2)}, u32[]{:S(2)}) async-start(bf16[4,256,2048]{2,1,0:T(8,128)(2,1)} %bitcast.232), calls=%async_computation.12 | async-start | bytes 8388608 | tf_op jit(solution)/shard_map/all_to_all | solution.py:332
  635.2 101.4 %reduce-scatter.11.cloned.1.call-start = ((), (), s32[]{:S(2)}) async-start(), calls=%async_computation.24 | async-start | bytes 3686400 | tf_op jit(solution)/shard_map/reduce_scatter | solution.py:400
  663.8 43.2 %collective-permute-start.7 = (f32[256,2048]{1,0:T(8,128)}, f32[256,2048]{1,0:T(8,128)}, u32[]{:S(2)}, u32[]{:S(2)}) collective-permute-start(f32[256,2048]{1,0:T(8,128)} %add_add_fusion.2), channel_id=1, source_target_pairs={{0,1},{1,0},{2,3},{3,2},{4,5},{5,4},{6,7},{7,6},{8,9},{9,8},{10,11... | collective-permute-start | bytes 6291464 | tf_op jit(solution)/shard_map/ppermute | solution.py:338
  687.4 39.9 %all-to-all-start.13 = ((bf16[4,128,2624]{1,2,0:T(8,128)(2,1)}), bf16[4,128,2624]{1,2,0:T(8,128)(2,1)S(1)}, u32[]{:S(2)}, u32[]{:S(2)}) async-start(bf16[4,128,2624]{1,2,0:T(8,128)(2,1)} %maximum_add_fusion), calls=%async_computation.17 | async-start | bytes 5373952 | tf_op jit(solution)/shard_map/all_to_all | solution.py:332
  702.1 37.9 %collective-permute-start.9 = (f32[256,2048]{1,0:T(8,128)}, f32[256,2048]{1,0:T(8,128)}, u32[]{:S(2)}, u32[]{:S(2)}) collective-permute-start(f32[256,2048]{1,0:T(8,128)} %fusion.37), channel_id=1, source_target_pairs={{0,1},{1,0},{2,3},{3,2},{4,5},{5,4},{6,7},{7,6},{8,9},{9,8},{10,11... | collective-permute-start | bytes 6291464 | tf_op jit(solution)/shard_map/ppermute | solution.py:338
  703.9 17.9 %collective-permute-start.13 = (f32[128]{0:T(128)S(1)}, f32[128]{0:T(128)S(1)}, u32[]{:S(2)}, u32[]{:S(2)}) collective-permute-start(f32[128]{0:T(128)S(1)} %get-tuple-element.133), channel_id=1, source_target_pairs={{0,2},{2,0},{4,6},{6,4},{8,10},{10,8},{12,14},{14,12},{16,18},{18,... | collective-permute-start | bytes 1544 | tf_op jit(solution)/shard_map/ppermute | solution.py:583
  (87 other events, 697.5 us)
Sparse Core Ops, SparseCore 0:
  48.0 78.1 all-gather.3
  144.1 119.6 all-gather.5
  266.0 61.4 all-gather.7
  395.3 58.5 reduce-scatter.4
  502.3 109.9 reduce-scatter.6
  620.1 33.5 reduce-scatter.8
  662.5 55.8 reduce-scatter.10

commit v5 on v4

--- a/solution.py
+++ b/solution.py
@@ -559,7 +559,9 @@
         input_grad_own = grad_after + grad_x
 
         pieces = [p.reshape(G, depth, -1) for p in (down_piece, in_piece, out_piece)]
-        got = trade(jnp.concatenate(pieces, axis=2) + zero(sums).astype(BF))
+        arrived = sums[:, :depth, :ff]
+        pieces[0] = pieces[0] + (arrived != arrived).astype(BF)
+        got = trade(jnp.concatenate(pieces, axis=2))
         outs = []
         for at, size in ((0, ff), (ff, ff), (2 * ff, ff), (3 * ff, ch)):
             outs.append(jnp.swapaxes(got[:, :, at : at + size], 0, 1).reshape(depth, -1).astype(F32))

time: 774 us -> 779 us (level)
  waiting for transfers between devices: 220 us -> 208 us
  other arithmetic: 58.5 us -> 66.5 us
    unnamed x158 -> x152, local copies, waits for them, and re-layouts: 34.2 us -> 32 us
    slice x17 -> x16, local copies, waits for them, and re-layouts: 17.6 us -> 16.3 us  [index_zero(): e = a[(0,) * a.ndim]]
  transfers between devices with their start and end apart: 37 -> 37, of which waited for: 16 -> 16; matrix products, arithmetic and copies ran while one was open for 32% -> 34% of each run, Pallas kernels for 5% -> 5%
where the time goes in v5:
time: 779 us; the launch traced here: 771 us
  waiting for transfers between devices  208 us (27%)
  matrix products  178 us (23%)
  local copies, waits for them, and re-layouts  98.6 us (13%)
  starting transfers between devices  78.4 us (10%)
  other arithmetic  66.5 us (9%)
  blocking collectives  65.7 us (8%)
  between operations  38.8 us (5%)
  Pallas kernels  36.9 us (5%)
    all_to_all x12, waiting for transfers between devices, trade(): return lax.all_to_all(a, 'dp', 0, 0, axis_index_groups=groups, tiled=True)  187 us
    dot_general x24, matrix products, dot(): lax.dot_general(a, b, (((ca,), (cb,)), ((), ())), preferred_element_type=...  178 us
    all_to_all x2, blocking collectives, trade(): return lax.all_to_all(a, 'dp', 0, 0, axis_index_groups=groups, tiled=True)  65.7 us
    all_to_all x12, starting transfers between devices, trade(): return lax.all_to_all(a, 'dp', 0, 0, axis_index_groups=groups, tiled=True)  54.9 us
    unnamed x152, local copies, waits for them, and re-layouts  32 us
    pallas_call x1, Pallas kernels, backward_call(): pl.pallas_call(functools.partial(backward_kernel, cp, row, unroll, len(ea...  24.7 us
    slice x16, local copies, waits for them, and re-layouts, index_zero(): e = a[(0,) * a.ndim]  16.3 us
    ppermute x12, starting transfers between devices, swap_core(): return lax.ppermute(a, 'mp', cores)  16.1 us
  transfers between devices with their start and end apart: 37, of which 16 were waited for; matrix products, arithmetic and copies ran while one was open for 34% of the time, Pallas kernels for 5%

profile of v5, /device:TPU:1, one launch (start us, length us, event | category | flops | bytes accessed | tf_op | source)
XLA Modules:
  0.0 770.8 jit_solution(12777930874312698539)
XLA Ops:
  19.9 18.3 %all_to_all.70 = bf16[4,137,960]{2,1,0:T(8,128)(2,1)S(1)} all-to-all(bf16[4,137,960]{2,1,0:T(8,128)(2,1)S(1)} %copy.230), channel_id=1, replica_groups={{0,2,4,6},{8,10,12,14},{16,18,20,22},{24,26,28,30},{1,3,5,7},{9,11,13,1..., dimensions={0} | all-to-all | bytes 2104320 | tf_op jit(solution)/shard_map/all_to_all | solution.py:332
  51.9 47.3 %all_to_all.71 = bf16[4,256,2048]{2,1,0:T(8,128)(2,1)} all-to-all(bf16[4,256,2048]{2,1,0:T(8,128)(2,1)S(1)} %broadcast_in_dim.59), channel_id=1, replica_groups={{0,2,4,6},{8,10,12,14},{16,18,20,22},{24,26,28,30},{1,3,5,7},{9,11,13,1..., dimensions={0} | all-to-all | bytes 8388608 | tf_op jit(solution)/shard_map/all_to_all | solution.py:332
  122.9 9.0 %all-to-all-done.3 = bf16[4,128,1536]{1,2,0:T(8,128)(2,1)S(1)} async-done(((bf16[4,128,1536]{1,2,0:T(8,128)(2,1)}), bf16[4,128,1536]{1,2,0:T(8,128)(2,1)S(1)}, u32[]{:S(2)}, u32[]{:S(2)}) %all-to-all-start.3) | async-done | bytes 1572896 | tf_op jit(solution)/shard_map/all_to_all | solution.py:332
  152.9 7.1 fusion.124.far_hbm.mix_far
  161.7 12.2 %recur_forward.1 = (bf16[2048,384]{1,0:T(8,128)(2,1)S(1)}, bf16[2048,384]{1,0:T(8,128)(2,1)S(1)}, f32[6,2112,128]{2,1,0:T(8,128)}, f32[3,2112,128]{2,1,0:T(8,128)S(1)}) custom-call(f32[1024,768]{1,0:T(8,128)S(1)} %fusion.126.near_hbm.mix_near, f32[1024,768]{1,0:T(8,128)S(1)} %fusion.124.far_hbm.mix_far, f32[3,2048,128]{2,1,0:T(8,128)S(1)} %broadcast_in_dim.62.mask_ref, ...), custom_call_target="tpu_custom_call" | custom-call | flops 117964800 | bytes 66060288 | tf_op jit(solution)/shard_map/recur_forward/pallas_call | solution.py:125
  179.1 7.2 all-to-all-done.5
  191.7 6.8 collective-permute-done.1
  208.4 46.4 %all-to-all-done.6 = bf16[4,256,2048]{2,1,0:T(8,128)(2,1)} async-done(((bf16[4,256,2048]{2,1,0:T(8,128)(2,1)}), bf16[4,256,2048]{2,1,0:T(8,128)(2,1)}, u32[]{:S(2)}, u32[]{:S(2)}) %all-to-all-start.6) | async-done | bytes 4194336 | tf_op jit(solution)/shard_map/all_to_all | solution.py:332
  270.2 44.3 %all-to-all-done.7 = bf16[4,256,2048]{2,1,0:T(8,128)(2,1)} async-done(((bf16[4,256,2048]{2,1,0:T(8,128)(2,1)}), bf16[4,256,2048]{2,1,0:T(8,128)(2,1)}, u32[]{:S(2)}, u32[]{:S(2)}) %all-to-all-start.7) | async-done | bytes 4194336 | tf_op jit(solution)/shard_map/all_to_all | solution.py:332
  320.5 7.3 all-gather.8.cloned.1.call-done
  331.0 10.5 %fusion.133 = f32[1024,1536]{1,0:T(8,128)S(1)} fusion(bf16[1024,2048]{1,0:T(8,128)(2,1)} %bitcast.43, bf16[2048,1536]{1,0:T(8,128)(2,1)} %all-gather.6.cloned.1.call-done), kind=kOutput, calls=%fused_computation.237 | convolution fusion | flops 6442450944 | bytes 16777216 | tf_op jit(solution)/shard_map/dot_general | solution.py:322
  351.0 8.4 %fusion.135 = f32[1024,1536]{1,0:T(8,128)S(1)} fusion(bf16[1024,2048]{1,0:T(8,128)(2,1)} %collective-permute-done.3, bf16[2048,1536]{1,0:T(8,128)(2,1)S(1)} %bitcast.265), kind=kOutput, calls=%fused_computation.239 | convolution fusion | flops 6442450944 | bytes 16777216 | tf_op jit(solution)/shard_map/dot_general | solution.py:322
  372.8 10.4 %fusion.26 = (bf16[1024,768]{1,0:T(8,128)(2,1)S(1)}, bf16[1024,768]{1,0:T(8,128)(2,1)S(1)}) fusion(f32[1024,1536]{1,0:T(8,128)} %copy-done.20, f32[]{:T(128)} %bitcast.46, bf16[1024,2048]{1,0:T(8,128)(2,1)} %copy-done.63, bf16[2048,768]{1,0:T(8,128)(2,1)} %all-gather.8.cloned.1.call-done), kind=kOutput, calls=%fused_computation.46 | convolution fusion | flops 3241672704 | bytes 16777220 | tf_op jit(solution)/shard_map/dot_general | solution.py:322
  383.2 12.1 %fusion.41 = bf16[1024,2048]{1,0:T(8,128)(2,1)} fusion(bf16[2048,1536]{1,0:T(8,128)(2,1)} %all-gather.6.cloned.1.call-done, bf16[1024,768]{1,0:T(8,128)(2,1)S(1)} %get-tuple-element.128, bf16[1024,768]{1,0:T(8,128)(2,1)S(1)} %get-tuple-element.127), kind=kOutput, calls=%fused_computation.85 | convolution fusion | flops 6448742400 | bytes 13631488 | tf_op jit(solution)/shard_map/dot_general | solution.py:322
  395.4 10.4 %fusion.18 = (bf16[1024,768]{1,0:T(8,128)(2,1)S(1)}, bf16[1024,768]{1,0:T(8,128)(2,1)S(1)}) fusion(f32[1024,1536]{1,0:T(8,128)} %copy-done.21, f32[]{:T(128)} %bitcast.46, bf16[1024,2048]{1,0:T(8,128)(2,1)} %bitcast.40, bf16[2048,768]{1,0:T(8,128)(2,1)} %all-gather.8.cloned.1.call-done), kind=kOutput, calls=%fused_computation.38 | convolution fusion | flops 3241672704 | bytes 16777220 | tf_op jit(solution)/shard_map/dot_general | solution.py:322
  405.8 11.5 %add_convert_fusion.2 = bf16[1024,2048]{1,0:T(8,128)(2,1)S(1)} fusion(bf16[1024,2048]{1,0:T(8,128)(2,1)} %collective-permute-done.4, bf16[2048,1536]{1,0:T(8,128)(2,1)} %all-gather.6.cloned.1.call-done, bf16[1024,768]{1,0:T(8,128)(2,1)S(1)} %get-tuple-element.126, bf16[1024,768]{1,0:T(8,128)(2,1)S(1)} %get-tuple-element.125), kind=kOutput, calls=%fused_computation.9 | convolution fusion | flops 6455033856 | bytes 17825792 | tf_op jit(solution)/shard_map/dot_general | solution.py:322
  433.5 17.6 %fusion.4 = bf16[2048,1536]{1,0:T(8,128)(2,1)} fusion(bf16[1024,2048]{1,0:T(8,128)(2,1)} %collective-permute-done.3, bf16[1024,2048]{1,0:T(8,128)(2,1)} %bitcast.43, bf16[1024,1536]{1,0:T(8,128)(2,1)S(1)} %fusion.40, bf16[1024,1536]{1,0:T(8,128)(2,1)S(1)} %fusion.42), kind=kOutput, calls=%fused_computation.12 | convolution fusion | flops 12917407744 | bytes 20971520 | tf_op jit(solution)/shard_map/dot_general | solution.py:322
  456.5 21.1 %all-to-all-done.9 = bf16[4,256,2048]{2,1,0:T(8,128)(2,1)} async-done(((bf16[4,256,2048]{2,1,0:T(8,128)(2,1)}), bf16[4,256,2048]{2,1,0:T(8,128)(2,1)}, u32[]{:S(2)}, u32[]{:S(2)}) %all-to-all-start.9) | async-done | bytes 4194336 | tf_op jit(solution)/shard_map/all_to_all | solution.py:332
  500.3 46.3 %all-to-all-done.10 = bf16[4,256,2048]{2,1,0:T(8,128)(2,1)} async-done(((bf16[4,256,2048]{2,1,0:T(8,128)(2,1)}), bf16[4,256,2048]{2,1,0:T(8,128)(2,1)}, u32[]{:S(2)}, u32[]{:S(2)}) %all-to-all-start.10) | async-done | bytes 4194336 | tf_op jit(solution)/shard_map/all_to_all | solution.py:332
  578.8 24.7 %recur_backward.1 = (bf16[2048,768]{1,0:T(8,128)(2,1)}, bf16[2048,768]{1,0:T(8,128)(2,1)}, f32[7,8,384]{2,1,0:T(8,128)S(1)}) custom-call(f32[1024,768]{1,0:T(8,128)} %copy-done.1, f32[1024,768]{1,0:T(8,128)} %copy-done.2, f32[1024,384]{1,0:T(8,128)S(1)} %copy-done.4, f32[1024,384]{1,0:T(8,128)S(1)} %copy-done.5, f32[3,2048,128]{2,1,0:T(8,128)} %copy-done, ...), custom_call_target="tpu_custom_call" | custom-call | flops 157286400 | bytes 100663296 | tf_op jit(solution)/shard_map/recur_backward/pallas_call | solution.py:284
  603.5 6.4 fusion.65
  621.4 7.0 add_convert_fusion
  647.7 9.2 %fusion.46 = f32[2048,768]{0,1:T(8,128)} fusion(bf16[1024,2048]{1,0:T(8,128)(2,1)} %bitcast.233, bf16[2048,768]{1,0:T(8,128)(2,1)} %get-tuple-element.26, bf16[1024,2048]{1,0:T(8,128)(2,1)} %copy-done.26), kind=kOutput, calls=%fused_computation.93 | convolution fusion | flops 3223584768 | bytes 13631488 | tf_op jit(solution)/shard_map/dot_general | solution.py:322
  657.9 8.5 %add_convert_fusion.4 = bf16[2048,768]{0,1:T(8,128)(2,1)S(1)} fusion(f32[2048,768]{0,1:T(8,128)} %fusion.46, bf16[1024,2048]{1,0:T(8,128)(2,1)} %collective-permute-done, bf16[2048,768]{1,0:T(8,128)(2,1)} %get-tuple-element.26, bf16[1024,2048]{1,0:T(8,128)(2,1)} %copy-done.26), kind=kOutput, calls=%fused_computation.17 | convolution fusion | flops 3226730496 | bytes 16777216 | tf_op jit(solution)/shard_map/dot_general | solution.py:322
  (399 shorter events, 321.8 us)
Async XLA Ops:
  45.0 99.0 %all-gather.4.cloned.1.call-start = ((), (), s32[]{:S(2)}) async-start(), calls=%async_computation.18 | async-start | bytes 4915200 | tf_op jit(solution)/shard_map/all_gather | solution.py:403
  102.9 50.0 %collective-permute-start = (bf16[1024,2048]{1,0:T(8,128)(2,1)}, bf16[1024,2048]{1,0:T(8,128)(2,1)}, u32[]{:S(2)}, u32[]{:S(2)}) collective-permute-start(bf16[1024,2048]{1,0:T(8,128)(2,1)} %bitcast.231), channel_id=1, source_target_pairs={{0,1},{1,0},{2,3},{3,2},{4,5},{5,4},{6,7},{7,6},{8,9},{9,8},{10,11... | collective-permute-start | bytes 12582920 | tf_op jit(solution)/shard_map/ppermute | solution.py:338
  110.1 21.7 %all-to-all-start.3 = ((bf16[4,128,1536]{1,2,0:T(8,128)(2,1)}), bf16[4,128,1536]{1,2,0:T(8,128)(2,1)S(1)}, u32[]{:S(2)}, u32[]{:S(2)}) async-start(bf16[4,128,1536]{1,2,0:T(8,128)(2,1)} %pad_maximum_fusion.9), calls=%async_computation.3 | async-start | bytes 3145728 | tf_op jit(solution)/shard_map/all_to_all | solution.py:332
  134.4 51.8 %all-to-all-start.5 = ((bf16[4,256,2048]{2,1,0:T(8,128)(2,1)}), bf16[4,256,2048]{2,1,0:T(8,128)(2,1)}, u32[]{:S(2)}, u32[]{:S(2)}) async-start(bf16[4,256,2048]{2,1,0:T(8,128)(2,1)} %broadcast_in_dim.64), calls=%async_computation.5 | async-start | bytes 8388608 | tf_op jit(solution)/shard_map/all_to_all | solution.py:332
  139.4 128.3 %all-gather.6.cloned.1.call-start = ((), (), s32[]{:S(2)}) async-start(), calls=%async_computation.19 | async-start | bytes 7864320 | tf_op jit(solution)/shard_map/all_gather | solution.py:403
  202.9 52.0 %all-to-all-start.6 = ((bf16[4,256,2048]{2,1,0:T(8,128)(2,1)}), bf16[4,256,2048]{2,1,0:T(8,128)(2,1)}, u32[]{:S(2)}, u32[]{:S(2)}) async-start(bf16[4,256,2048]{2,1,0:T(8,128)(2,1)} %bitcast.237), calls=%async_computation.6 | async-start | bytes 8388608 | tf_op jit(solution)/shard_map/all_to_all | solution.py:332
  207.7 120.0 %all-gather.8.cloned.1.call-start = ((), (), s32[]{:S(2)}) async-start(), calls=%async_computation.20 | async-start | bytes 3932160 | tf_op jit(solution)/shard_map/all_gather | solution.py:403
  262.7 51.7 %all-to-all-start.7 = ((bf16[4,256,2048]{2,1,0:T(8,128)(2,1)}), bf16[4,256,2048]{2,1,0:T(8,128)(2,1)}, u32[]{:S(2)}, u32[]{:S(2)}) async-start(bf16[4,256,2048]{2,1,0:T(8,128)(2,1)} %broadcast_in_dim.65), calls=%async_computation.7 | async-start | bytes 8388608 | tf_op jit(solution)/shard_map/all_to_all | solution.py:332
  267.6 186.4 %reduce-scatter.5.cloned.1.call-start = ((), (), s32[]{:S(2)}) async-start(), calls=%async_computation.21 | async-start | bytes 3932160 | tf_op jit(solution)/shard_map/reduce_scatter | solution.py:400
  318.9 32.0 %collective-permute-start.3 = (bf16[1024,2048]{1,0:T(8,128)(2,1)}, bf16[1024,2048]{1,0:T(8,128)(2,1)}, u32[]{:S(2)}, u32[]{:S(2)}) collective-permute-start(bf16[1024,2048]{1,0:T(8,128)(2,1)} %broadcast_add_fusion), channel_id=1, source_target_pairs={{0,1},{1,0},{2,3},{3,2},{4,5},{5,4},{6,7},{7,6},{8,9},{9,8},{10,11... | collective-permute-start | bytes 12582920 | tf_op jit(solution)/shard_map/ppermute | solution.py:338
  330.2 31.9 %collective-permute-start.2 = (bf16[1024,2048]{1,0:T(8,128)(2,1)}, bf16[1024,2048]{1,0:T(8,128)(2,1)S(1)}, u32[]{:S(2)}, u32[]{:S(2)}) collective-permute-start(bf16[1024,2048]{1,0:T(8,128)(2,1)} %bitcast.40), channel_id=1, source_target_pairs={{0,1},{1,0},{2,3},{3,2},{4,5},{5,4},{6,7},{7,6},{8,9},{9,8},{10,11... | collective-permute-start | bytes 12582920 | tf_op jit(solution)/shard_map/ppermute | solution.py:338
  424.3 56.7 %collective-permute-start.5 = (bf16[1024,2048]{1,0:T(8,128)(2,1)}, bf16[1024,2048]{1,0:T(8,128)(2,1)}, u32[]{:S(2)}, u32[]{:S(2)}) collective-permute-start(bf16[1024,2048]{1,0:T(8,128)(2,1)} %fusion.48), channel_id=1, source_target_pairs={{0,1},{1,0},{2,3},{3,2},{4,5},{5,4},{6,7},{7,6},{8,9},{9,8},{10,11... | collective-permute-start | bytes 12582920 | tf_op jit(solution)/shard_map/ppermute | solution.py:338
  425.0 52.6 %all-to-all-start.9 = ((bf16[4,256,2048]{2,1,0:T(8,128)(2,1)}), bf16[4,256,2048]{2,1,0:T(8,128)(2,1)}, u32[]{:S(2)}, u32[]{:S(2)}) async-start(bf16[4,256,2048]{2,1,0:T(8,128)(2,1)} %bitcast.236), calls=%async_computation.9 | async-start | bytes 8388608 | tf_op jit(solution)/shard_map/all_to_all | solution.py:332
  494.8 51.7 %all-to-all-start.10 = ((bf16[4,256,2048]{2,1,0:T(8,128)(2,1)}), bf16[4,256,2048]{2,1,0:T(8,128)(2,1)}, u32[]{:S(2)}, u32[]{:S(2)}) async-start(bf16[4,256,2048]{2,1,0:T(8,128)(2,1)} %broadcast_in_dim.67), calls=%async_computation.11 | async-start | bytes 8388608 | tf_op jit(solution)/shard_map/all_to_all | solution.py:332
  499.7 176.3 %reduce-scatter.7.cloned.1.call-start = ((), (), s32[]{:S(2)}) async-start(), calls=%async_computation.22 | async-start | bytes 7864320 | tf_op jit(solution)/shard_map/reduce_scatter | solution.py:400
  546.6 17.4 %collective-permute-start.6 = (bf16[1024,2048]{1,0:T(8,128)(2,1)}, bf16[1024,2048]{1,0:T(8,128)(2,1)}, u32[]{:S(2)}, u32[]{:S(2)}) collective-permute-start(bf16[1024,2048]{1,0:T(8,128)(2,1)} %bitcast.52), channel_id=1, source_target_pairs={{0,1},{1,0},{2,3},{3,2},{4,5},{5,4},{6,7},{7,6},{8,9},{9,8},{10,11... | collective-permute-start | bytes 12582920 | tf_op jit(solution)/shard_map/ppermute | solution.py:338
  548.0 61.9 %all-to-all-start.8 = ((bf16[4,256,2048]{2,1,0:T(8,128)(2,1)}), bf16[4,256,2048]{2,1,0:T(8,128)(2,1)}, u32[]{:S(2)}, u32[]{:S(2)}) async-start(bf16[4,256,2048]{2,1,0:T(8,128)(2,1)} %bitcast.222), calls=%async_computation.8 | async-start | bytes 8388608 | tf_op jit(solution)/shard_map/all_to_all | solution.py:332
  553.5 127.0 %reduce-scatter.9.cloned.1.call-start = ((), (), s32[]{:S(2)}) async-start(), calls=%async_computation.23 | async-start | bytes 1966080 | tf_op jit(solution)/shard_map/reduce_scatter | solution.py:400
  637.2 52.7 %all-to-all-start.11 = ((bf16[4,256,2048]{1,2,0:T(8,128)(2,1)}), bf16[4,256,2048]{1,2,0:T(8,128)(2,1)}, u32[]{:S(2)}, u32[]{:S(2)}) async-start(bf16[4,256,2048]{1,2,0:T(8,128)(2,1)} %copy.248), calls=%async_computation.12 | async-start | bytes 8388608 | tf_op jit(solution)/shard_map/all_to_all | solution.py:332
  642.1 99.6 %reduce-scatter.11.cloned.1.call-start = ((), (), s32[]{:S(2)}) async-start(), calls=%async_computation.24 | async-start | bytes 3686400 | tf_op jit(solution)/shard_map/reduce_scatter | solution.py:400
  675.4 45.6 %collective-permute-start.7 = (f32[256,2048]{1,0:T(8,128)}, f32[256,2048]{1,0:T(8,128)}, u32[]{:S(2)}, u32[]{:S(2)}) collective-permute-start(f32[256,2048]{1,0:T(8,128)} %add_add_fusion.2), channel_id=1, source_target_pairs={{0,1},{1,0},{2,3},{3,2},{4,5},{5,4},{6,7},{7,6},{8,9},{9,8},{10,11... | collective-permute-start | bytes 6291464 | tf_op jit(solution)/shard_map/ppermute | solution.py:338
  692.9 40.5 %all-to-all-start.13 = ((bf16[4,128,2624]{1,2,0:T(8,128)(2,1)}), bf16[4,128,2624]{1,2,0:T(8,128)(2,1)}, u32[]{:S(2)}, u32[]{:S(2)}) async-start(bf16[4,128,2624]{1,2,0:T(8,128)(2,1)} %pad_maximum_fusion.3), calls=%async_computation.17 | async-start | bytes 5373952 | tf_op jit(solution)/shard_map/all_to_all | solution.py:332
  716.1 29.0 %collective-permute-start.9 = (f32[256,2048]{1,0:T(8,128)}, f32[256,2048]{1,0:T(8,128)}, u32[]{:S(2)}, u32[]{:S(2)}) collective-permute-start(f32[256,2048]{1,0:T(8,128)} %fusion.37), channel_id=1, source_target_pairs={{0,1},{1,0},{2,3},{3,2},{4,5},{5,4},{6,7},{7,6},{8,9},{9,8},{10,11... | collective-permute-start | bytes 6291464 | tf_op jit(solution)/shard_map/ppermute | solution.py:338
  741.6 13.9 %all-to-all-start.12 = ((bf16[4,140,640]{2,1,0:T(8,128)(2,1)}), bf16[4,140,640]{2,1,0:T(8,128)(2,1)S(1)}, u32[]{:S(2)}, u32[]{:S(2)}) async-start(bf16[4,140,640]{2,1,0:T(8,128)(2,1)} %reduce-scatter.11.cloned.1.call-done), calls=%async_computation.16 | async-start | bytes 1474560 | tf_op jit(solution)/shard_map/all_to_all | solution.py:332
  (84 other events, 665.4 us)
Sparse Core Ops, SparseCore 0:
  48.0 78.1 all-gather.3
  144.1 119.8 all-gather.5
  266.2 61.4 all-gather.7
  395.5 58.5 reduce-scatter.4
  502.5 109.9 reduce-scatter.6
  620.3 33.5 reduce-scatter.8
  674.0 55.8 reduce-scatter.10
